TPU v7x, 32 devices: a whole 2x2x4 slice. The times are simulated.
32 devices in a mesh: seq: 8 (over z, x), head: 4 (over y, core).
Axes of the slice: x: 2, y: 2, z: 4, core: 2. Of those that a mesh axis runs over, the one named last changes fastest.
Arguments:
- queries: bfloat16 [4096, 2048], P('seq', 'head'), may hold values from -6 to 6
- keys: bfloat16 [4096, 2048], P('seq', 'head'), may hold values from -6 to 6
- values: bfloat16 [4096, 2048], P('seq', 'head'), may hold values from -6 to 6
- summary_lists: int32 [8, 8, 16], P('seq', 'head'), may hold values from 0 to 6, as said below
- out_weight: bfloat16 [2048, 2048], P('head'), may hold values from -0.125 to 0.125
Outputs:
- mixed: bfloat16 [4096, 2048], P(('seq', 'head'))
Inputs may be any that keep to these rules, and one draw needn't show every extreme that they name: `summary_lists`: entry [b, f, k] names a block. In every query block b above 0 it is below b, and entry [b, f, 0] is b - 1; in query block 0 every entry is 0 and names nothing. Entries may repeat.
All inputs are finite; a program needn't handle non-finite values.
Results may differ from a plain program's by a relative error of at most 0.014.
Values may be sent and summed in bfloat16 or wider, within the bound.
No kernel may reach another device: no remote copies, remote signals or barrier semaphores. Data moves between devices by JAX's collectives and lax.ppermute only.
A program may use at most 64 MiB of HBM per device.

v0:
```python
import math

import jax
import jax.numpy as jnp
from jax import lax
from jax.sharding import PartitionSpec as P

HEAD_DIM = 128
BLK = 512
SUMMARY = 32
ROWS_DEV = 1


NEG = -1e30


def softmax_rounded(scores, valid):
    scores = jnp.where(valid, scores, NEG)
    peak = jnp.max(scores, axis=-1, keepdims=True)
    weights = jnp.where(valid, jnp.exp(scores - peak), 0.0)
    return (weights / jnp.sum(weights, axis=-1, keepdims=True)).astype(jnp.bfloat16)


def column_attend(pieces):
    col_q, col_k, col_v = pieces
    scale = HEAD_DIM ** (-0.5)
    scores = jnp.einsum("rxcd,sxcd->xcrs", col_q, col_k, preferred_element_type=jnp.float32) * scale
    blocks = col_q.shape[0]
    earlier = jnp.arange(blocks)[:, None] >= jnp.arange(blocks)[None, :]
    weights = softmax_rounded(scores, earlier)
    return jnp.einsum("xcrs,sxcd->rxcd", weights, col_v, preferred_element_type=jnp.float32).astype(
        jnp.bfloat16
    )


def absorb(state, scores, multiplier):
    old_peak, old_denom = (state[0], state[1])
    new_peak = jnp.maximum(old_peak, jnp.max(scores, axis=(3, 4)))
    weights = jnp.exp(scores - new_peak[..., None, None]) * multiplier[:, :, None, :, None]
    shrink = jnp.exp(old_peak - new_peak)
    return (new_peak, old_denom * shrink + jnp.sum(weights, axis=(3, 4)), shrink, weights)


def per_device(queries, keys, values, summary_lists, out_weight):
    scale = HEAD_DIM ** (-0.5)
    seq_count = lax.axis_size("seq")
    query_heads = queries.reshape(ROWS_DEV, BLK, 4, HEAD_DIM)
    key_heads = keys.reshape(ROWS_DEV, BLK, 4, HEAD_DIM)
    value_heads = values.reshape(ROWS_DEV, BLK, 4, HEAD_DIM)
    causal = jnp.arange(BLK)[:, None] >= jnp.arange(BLK)[None, :]
    block_index = lax.axis_index("seq") * ROWS_DEV + jnp.arange(ROWS_DEV, dtype=jnp.int32)

    def column_layout(source):
        return source[:, :, 1].reshape(ROWS_DEV, seq_count, BLK // seq_count, HEAD_DIM)

    column_moved = column_attend(
        (
            lax.all_to_all(
                column_layout(query_heads), "seq", split_axis=1, concat_axis=0, tiled=True
            ),
            lax.all_to_all(
                column_layout(key_heads), "seq", split_axis=1, concat_axis=0, tiled=True
            ),
            lax.all_to_all(
                column_layout(value_heads), "seq", split_axis=1, concat_axis=0, tiled=True
            ),
        )
    )
    row_scores = (
        jnp.einsum(
            "rid,rjd->rij",
            query_heads[:, :, 0],
            key_heads[:, :, 0],
            preferred_element_type=jnp.float32,
        )
        * scale
    )
    row_weights = softmax_rounded(row_scores, causal)
    row_out = jnp.einsum(
        "rij,rjd->rid", row_weights, value_heads[:, :, 0], preferred_element_type=jnp.float32
    ).astype(jnp.bfloat16)
    fixed_q = query_heads[:, :, 2:]
    fixed_k = key_heads[:, :, 2:]
    fixed_v = value_heads[:, :, 2:]
    own_scores = (
        jnp.einsum("rifd,rjfd->rfij", fixed_q, fixed_k, preferred_element_type=jnp.float32) * scale
    )
    own_scores = jnp.where(causal, own_scores, NEG)
    own_peak = jnp.max(own_scores, axis=-1)
    own_weights = jnp.exp(own_scores - own_peak[..., None])
    own_denom = jnp.sum(own_weights, axis=-1)
    own_sum = jnp.einsum(
        "rfij,rjfd->rfid",
        own_weights.astype(jnp.bfloat16),
        fixed_v,
        preferred_element_type=jnp.float32,
    )
    tail_k = jnp.swapaxes(fixed_k[:, BLK - SUMMARY :], 1, 2)
    tail_v = jnp.swapaxes(fixed_v[:, BLK - SUMMARY :], 1, 2)
    piece_k = lax.all_gather(tail_k, "seq", axis=0, tiled=True)
    piece_v = lax.all_gather(tail_v, "seq", axis=0, tiled=True)
    arrived = piece_k.shape[0]
    stride = math.gcd(arrived, 8)

    def inner(turn, running):
        offset = turn * stride
        part_k = lax.dynamic_slice_in_dim(piece_k, offset, stride, 0)
        part_v = lax.dynamic_slice_in_dim(piece_v, offset, stride, 0)
        tile_index = offset + jnp.arange(stride, dtype=jnp.int32)
        matches = (summary_lists[:, :, :, None] == tile_index) & (
            tile_index < block_index[:, None, None, None]
        )
        multiplier = jnp.sum(matches.astype(jnp.float32), axis=2)
        scores = (
            jnp.einsum("rifd,nfcd->rfinc", fixed_q, part_k, preferred_element_type=jnp.float32)
            * scale
        )
        scores = jnp.where(multiplier[:, :, None, :, None] > 0, scores, NEG)
        new_peak, new_denom, shrink, weights = absorb(running, scores, multiplier)
        new_sum = running[2] * shrink[..., None] + jnp.einsum(
            "rfinc,nfcd->rfid",
            weights.astype(jnp.bfloat16),
            part_v,
            preferred_element_type=jnp.float32,
        )
        return (new_peak, new_denom, new_sum)

    final_peak, final_denom, final_sum = lax.fori_loop(
        0, arrived // stride, inner, (own_peak, own_denom, own_sum)
    )
    fixed_out = jnp.swapaxes((final_sum / final_denom[..., None]).astype(jnp.bfloat16), 1, 2)
    column_out = lax.all_to_all(
        column_moved, "seq", split_axis=0, concat_axis=1, tiled=True
    ).reshape(ROWS_DEV, BLK, HEAD_DIM)
    attended = jnp.concatenate(
        [row_out[:, :, None], column_out[:, :, None], fixed_out], axis=2
    ).reshape(ROWS_DEV * BLK, 4 * HEAD_DIM)
    swapped = lax.all_to_all(attended, "head", split_axis=0, concat_axis=1, tiled=True)
    mixed = jnp.dot(
        swapped,
        lax.all_gather(out_weight, "head", axis=0, tiled=True),
        preferred_element_type=jnp.float32,
    )
    return mixed.astype(jnp.bfloat16)


def solution(mesh):
    return jax.shard_map(
        per_device,
        mesh=mesh,
        in_specs=(
            P("seq", "head"),
            P("seq", "head"),
            P("seq", "head"),
            P("seq", "head", None),
            P("head", None),
        ),
        out_specs=P(("seq", "head"), None),
        check_vma=False,
    )
```

profile of v0, /device:TPU:0, one launch (start us, length us, event | category | flops | bytes accessed | tf_op | source)
XLA Modules:
  0.0 146.6 jit_solution(15217500131195344572)
XLA Ops:
  6.5 0.7 all-gather.2.cloned.1.call-update
  7.8 0.8 copy.76
  8.6 7.3 %all-to-all-start = ((bf16[1,8,64,128]{3,2,0,1:T(8,128)(2,1)}), bf16[1,8,64,128]{3,2,0,1:T(8,128)(2,1)S(1)}, u32[]{:S(2)}, u32[]{:S(2)}) async-start(bf16[1,8,64,128]{3,2,0,1:T(8,128)(2,1)} %bitcast.8), calls=%async_computation | async-start | bytes 262144 | tf_op jit(solution)/shard_map/all_to_all | solution.py:58
  16.7 0.8 copy.79
  17.5 0.7 copy.83
  18.2 31.1 %all_gather.9 = bf16[8,2,32,128]{3,2,0,1:T(8,128)(2,1)S(1)} all-gather(bf16[1,2,32,128]{3,2,0,1:T(8,128)(2,1)S(1)} %bitcast.125), channel_id=1, replica_groups=mesh['seq'=8,'head'=4] {'seq'}, dimensions={0}, use_global_device_ids=true | all-gather | bytes 147456 | tf_op jit(solution)/shard_map/all_gather | solution.py:100
  49.9 0.6 fusion.1
  50.6 32.5 %all_gather.10 = bf16[8,2,32,128]{3,2,0,1:T(8,128)(2,1)} all-gather(bf16[1,2,32,128]{3,2,0,1:T(8,128)(2,1)S(1)} %bitcast.124), channel_id=1, replica_groups=mesh['seq'=8,'head'=4] {'seq'}, dimensions={0}, use_global_device_ids=true | all-gather | bytes 147456 | tf_op jit(solution)/shard_map/all_gather | solution.py:101
  83.4 1.3 fusion.54
  84.8 0.5 fusion.2
  85.3 1.7 %fusion.8 = f32[1,2,512,128]{3,2,1,0:T(8,128)} fusion(f32[2,512,512]{1,2,0:T(8,128)S(1)} %get-tuple-element.26, f32[2,512]{1,0:T(2,128)S(1)} %get-tuple-element.25, pred[512,512]{0,1:T(8,128)(4,1)S(1)} %iota_compare_fusion, bf16[1,512,4,128]{1,3,2,0:T(8,128)(2,1)S(1)} %bitcast.117, f32[2,512]{1,0:T(2,128)S(1)} %get-tuple-element.24), kind=kOutput, calls=%fused_computation.14 | convolution fusion | flops 136445952 | bytes 3153920 | tf_op jit(solution)/shard_map/rfij,rjfd->rfid/dot_general | solution.py:92
  87.0 5.4 %all-to-all-start.1 = ((bf16[1,8,64,128]{3,2,0,1:T(8,128)(2,1)}), bf16[1,8,64,128]{3,2,0,1:T(8,128)(2,1)S(1)}, u32[]{:S(2)}, u32[]{:S(2)}) async-start(bf16[1,8,64,128]{3,2,0,1:T(8,128)(2,1)} %bitcast.11), calls=%async_computation.1 | async-start | bytes 262144 | tf_op jit(solution)/shard_map/all_to_all | solution.py:61
  92.4 1.5 %fusion.12 = bf16[1,512,2,128]{3,1,2,0:T(8,128)(2,1)S(1)} fusion(f32[1,2,512,128]{3,2,1,0:T(8,128)} %fusion.8, bf16[8,2,32,128]{3,2,0,1:T(8,128)(2,1)S(1)} %copy-done.4, f32[1,2,512,8,32]{2,4,3,1,0:T(8,128)S(1)} %get-tuple-element.28, f32[2,8]{1,0:T(2,128)S(1)} %convert_reduce_fusion, f32[2,512]{1,0:T(2,128)S(1)} %max.19, f32[2,512]{1,0:T(2,128)S(1)} %get-tuple-element.23), kind=kOutput, calls=%fused_computation.19 | convolution fusion | flops 68288512 | bytes 1974336 | tf_op jit(solution)/shard_map/while/body/eval_jaxpr/rfinc,nfcd->rfid/dot_general | solution.py:120
  93.9 5.8 %all-to-all-done.1 = bf16[1,8,64,128]{3,2,0,1:T(8,128)(2,1)S(1)} async-done(((bf16[1,8,64,128]{3,2,0,1:T(8,128)(2,1)}), bf16[1,8,64,128]{3,2,0,1:T(8,128)(2,1)S(1)}, u32[]{:S(2)}, u32[]{:S(2)}) %all-to-all-start.1) | async-done | bytes 131104 | tf_op jit(solution)/shard_map/all_to_all | solution.py:61
  99.7 3.4 %all-to-all-start.2 = ((bf16[1,8,64,128]{3,2,0,1:T(8,128)(2,1)}), bf16[1,8,64,128]{3,2,0,1:T(8,128)(2,1)S(1)}, u32[]{:S(2)}, u32[]{:S(2)}) async-start(bf16[1,8,64,128]{3,2,0,1:T(8,128)(2,1)} %bitcast.14), calls=%async_computation.2 | async-start | bytes 262144 | tf_op jit(solution)/shard_map/all_to_all | solution.py:64
  103.5 0.8 fusion.53
  104.5 5.9 %all-to-all-done.2 = bf16[1,8,64,128]{3,2,0,1:T(8,128)(2,1)S(1)} async-done(((bf16[1,8,64,128]{3,2,0,1:T(8,128)(2,1)}), bf16[1,8,64,128]{3,2,0,1:T(8,128)(2,1)S(1)}, u32[]{:S(2)}, u32[]{:S(2)}) %all-to-all-start.2) | async-done | bytes 131104 | tf_op jit(solution)/shard_map/all_to_all | solution.py:64
  110.6 0.7 copy.87
  111.3 3.4 %all-to-all-start.3 = ((bf16[8,1,64,128]{3,2,1,0:T(8,128)(2,1)}), bf16[8,1,64,128]{3,2,1,0:T(8,128)(2,1)S(1)}, u32[]{:S(2)}, u32[]{:S(2)}) async-start(bf16[8,1,64,128]{3,2,1,0:T(8,128)(2,1)} %copy.87), calls=%async_computation.3 | async-start | bytes 262144 | tf_op jit(solution)/shard_map/all_to_all | solution.py:132
  114.6 0.4 fusion.13
  115.0 6.9 %all-to-all-done.3 = bf16[8,1,64,128]{3,2,1,0:T(8,128)(2,1)S(1)} async-done(((bf16[8,1,64,128]{3,2,1,0:T(8,128)(2,1)}), bf16[8,1,64,128]{3,2,1,0:T(8,128)(2,1)S(1)}, u32[]{:S(2)}, u32[]{:S(2)}) %all-to-all-start.3) | async-done | bytes 131104 | tf_op jit(solution)/shard_map/all_to_all | solution.py:132
  122.0 0.4 copy.94
  122.6 11.4 %all_to_all.55 = bf16[4,128,512]{2,1,0:T(8,128)(2,1)S(1)} all-to-all(bf16[4,128,512]{2,1,0:T(8,128)(2,1)S(1)} %all_to_all.21), channel_id=1, replica_groups=mesh['seq'=8,'head'=4] {'head'}, dimensions={0} | all-to-all | bytes 1048576 | tf_op jit(solution)/shard_map/all_to_all | solution.py:138
  134.3 5.5 %convolution_convert_fusion = bf16[128,2048]{1,0:T(8,128)(2,1)} fusion(bf16[128,2048]{0,1:T(8,128)(2,1)S(1)} %bitcast.109, bf16[2048,2048]{1,0:T(8,128)(2,1)} %all-gather.2.cloned.1.call-done), kind=kOutput, calls=%fused_computation.1 | convolution fusion | flops 1074003968 | bytes 9437184 | tf_op jit(solution)/shard_map/dot_general | solution.py:139
  (43 shorter events, 3.6 us)
Async XLA Ops:
  6.5 1.0 copy-start.1
  6.5 9.3 %copy-start.2 = (bf16[512,512]{1,0:T(8,128)(2,1)S(1)}, bf16[512,512]{1,0:T(8,128)(2,1)}, u32[]{:S(2)}) copy-start(bf16[512,512]{1,0:T(8,128)(2,1)} %param.6) | copy-start | bytes 1572868
  6.5 127.8 %all-gather.2.cloned.1.call-start = ((), (), s32[]{:S(2)}) async-start(), calls=%async_computation.5 | async-start | bytes 10485760 | tf_op jit(solution)/shard_map/all_gather | solution.py:141
  7.6 8.6 %copy-start.3 = (bf16[512,512]{1,0:T(8,128)(2,1)S(1)}, bf16[512,512]{1,0:T(8,128)(2,1)}, u32[]{:S(2)}) copy-start(bf16[512,512]{1,0:T(8,128)(2,1)} %param.7) | copy-start | bytes 1572868
  7.8 41.5 %copy-start.5 = (s32[1,2,16]{2,1,0:T(2,128)S(1)}, s32[1,2,16]{2,1,0:T(2,128)}, u32[]{:S(2)}) copy-start(s32[1,2,16]{2,1,0:T(2,128)} %param.8) | copy-start | bytes 388
  8.6 78.4 %all-to-all-start = ((bf16[1,8,64,128]{3,2,0,1:T(8,128)(2,1)}), bf16[1,8,64,128]{3,2,0,1:T(8,128)(2,1)S(1)}, u32[]{:S(2)}, u32[]{:S(2)}) async-start(bf16[1,8,64,128]{3,2,0,1:T(8,128)(2,1)} %bitcast.8), calls=%async_computation | async-start | bytes 262144 | tf_op jit(solution)/shard_map/all_to_all | solution.py:58
  16.1 33.9 %copy-start = (bf16[512,512]{0,1:T(8,128)(2,1)}, bf16[512,512]{0,1:T(8,128)(2,1)S(1)}, u32[]{:S(2)}) copy-start(bf16[512,512]{0,1:T(8,128)(2,1)S(1)} %copy.74) | copy-start | bytes 1572868
  85.3 7.1 %copy-start.4 = (bf16[8,2,32,128]{3,2,0,1:T(8,128)(2,1)S(1)}, bf16[8,2,32,128]{3,2,0,1:T(8,128)(2,1)}, u32[]{:S(2)}) copy-start(bf16[8,2,32,128]{3,2,0,1:T(8,128)(2,1)} %all_gather.10) | copy-start | bytes 393220
  87.0 12.7 %all-to-all-start.1 = ((bf16[1,8,64,128]{3,2,0,1:T(8,128)(2,1)}), bf16[1,8,64,128]{3,2,0,1:T(8,128)(2,1)S(1)}, u32[]{:S(2)}, u32[]{:S(2)}) async-start(bf16[1,8,64,128]{3,2,0,1:T(8,128)(2,1)} %bitcast.11), calls=%async_computation.1 | async-start | bytes 262144 | tf_op jit(solution)/shard_map/all_to_all | solution.py:61
  99.7 10.7 %all-to-all-start.2 = ((bf16[1,8,64,128]{3,2,0,1:T(8,128)(2,1)}), bf16[1,8,64,128]{3,2,0,1:T(8,128)(2,1)S(1)}, u32[]{:S(2)}, u32[]{:S(2)}) async-start(bf16[1,8,64,128]{3,2,0,1:T(8,128)(2,1)} %bitcast.14), calls=%async_computation.2 | async-start | bytes 262144 | tf_op jit(solution)/shard_map/all_to_all | solution.py:64
  111.3 10.7 %all-to-all-start.3 = ((bf16[8,1,64,128]{3,2,1,0:T(8,128)(2,1)}), bf16[8,1,64,128]{3,2,1,0:T(8,128)(2,1)S(1)}, u32[]{:S(2)}, u32[]{:S(2)}) async-start(bf16[8,1,64,128]{3,2,1,0:T(8,128)(2,1)} %copy.87), calls=%async_computation.3 | async-start | bytes 262144 | tf_op jit(solution)/shard_map/all_to_all | solution.py:132
Sparse Core Ops, SparseCore 0:
  8.9 60.9 all-gather.1
where the time goes:
time: 147 us
  blocking collectives  75.1 us (51%)
  starting transfers between devices  19.4 us (13%)
  waiting for transfers between devices  19.4 us (13%)
  between operations  13.6 us (9%)
  matrix products  11.7 us (8%)
  local copies, waits for them, and re-layouts  5.47 us (4%)
  other arithmetic  2.06 us (1%)
    all_gather x1, blocking collectives, per_device(): piece_v = lax.all_gather(tail_v, 'seq', axis=0, tiled=True)  32.5 us
    all_gather x1, blocking collectives, per_device(): piece_k = lax.all_gather(tail_k, 'seq', axis=0, tiled=True)  31.1 us
    all_to_all x1, blocking collectives, per_device(): lax.all_to_all(attended, 'head', split_axis=0, concat_axis=1, tiled=True)  11.4 us
    all_to_all x1, starting transfers between devices, per_device(): lax.all_to_all(column_layout(query_heads), 'seq', split_axis=1, concat_ax...  7.25 us
    all_to_all x1, waiting for transfers between devices, per_device(): lax.all_to_all(column_moved, 'seq', split_axis=0, concat_axis=1, tiled=True)  6.91 us
    all_to_all x1, waiting for transfers between devices, per_device(): lax.all_to_all(column_layout(value_heads), 'seq', split_axis=1, concat_ax...  5.91 us
    all_to_all x1, waiting for transfers between devices, per_device(): lax.all_to_all(column_layout(key_heads), 'seq', split_axis=1, concat_axis...  5.81 us
    dot_general x1, matrix products, per_device(): jnp.dot(swapped, lax.all_gather(out_weight, 'head', axis=0, tiled=True),...  5.46 us
  transfers between devices with their start and end apart: 5, of which 3 were waited for; matrix products, arithmetic and copies ran while one was open for 9% of the time, Pallas kernels for 0%

commit v1 on v0

v1 whole, which is shorter than its diff:
```python
import functools
import math

import jax
import jax.numpy as jnp
from jax import lax
from jax.experimental import pallas as pl
from jax.experimental.pallas import tpu as pltpu
from jax.sharding import PartitionSpec as P

HEAD_DIM = 128
SUMMARY = 32
NEG = -1e30
BF16 = jnp.bfloat16
F32 = jnp.float32
VMEM = pl.BlockSpec(memory_space=pltpu.VMEM)
SCALE2 = HEAD_DIM ** (-0.5) * math.log2(math.e)


def call(kernel, out, operands, flops=0):
    out = [jax.ShapeDtypeStruct(shape, BF16) for shape in out]
    moved = sum(x.size * x.dtype.itemsize for x in operands) + sum(2 * math.prod(x.shape) for x in out)
    return pl.pallas_call(
        kernel,
        out_shape=out,
        in_specs=[VMEM] * len(operands),
        out_specs=[VMEM] * len(out),
        compiler_params=pltpu.CompilerParams(vmem_limit_bytes=40 * 1024 * 1024),
        cost_estimate=pl.CostEstimate(flops=flops, bytes_accessed=moved, transcendentals=flops // 512),
    )(*operands)


def dot_t(a, b):
    return lax.dot_general(a, b, (((1,), (1,)), ((), ())), preferred_element_type=F32)


def dot(a, b):
    return jnp.dot(a, b, preferred_element_type=F32)


def masked_attention(q, k, v, valid):
    scores = jnp.where(valid, dot_t(q, k), NEG)
    peak = jnp.max(scores, axis=1, keepdims=True)
    weights = jnp.exp2((scores - peak) * SCALE2)
    denom = jnp.sum(weights, axis=1, keepdims=True)
    return dot(weights.astype(BF16), v) / denom


def column_kernel(columns, moved_ref, out_ref):
    outer, _, inner, depth = moved_ref.shape
    rows = outer * inner
    q, k, v = (moved_ref[:, i].reshape(rows, depth) for i in range(3))
    at_q = lax.broadcasted_iota(jnp.int32, (rows, 1), 0)
    at_k = lax.broadcasted_iota(jnp.int32, (1, rows), 1)
    valid = (lax.rem(at_q, columns) == lax.rem(at_k, columns)) & (at_k <= at_q)
    out = masked_attention(q, k, v, valid)
    out_ref[...] = out.astype(BF16).reshape(outer, inner, depth)


def part_kernel(flips, parts, stages, q_ref, k_ref, v_ref, w_ref, mult_ref, *refs):
    tails, outs = refs[:stages], refs[stages:]
    block = q_ref.shape[0]
    rows = block // parts
    me = lax.axis_index("head")
    far = [[], [], [], []]
    for tail in tails:
        for slot in range(tail.shape[0]):
            for i in range(4):
                far[i].append(tail[slot, i])
    far = [jnp.concatenate(x, axis=0) for x in far]
    for flip, out_ref in zip(flips, outs):
        first = pl.multiple_of((me ^ flip) * rows, rows)
        at_q = first + lax.broadcasted_iota(jnp.int32, (rows, 1), 0)
        at_k = lax.broadcasted_iota(jnp.int32, (1, block), 1)
        causal = at_k <= at_q
        q = q_ref[pl.ds(first, rows), :]
        attended = masked_attention(q[:, :HEAD_DIM], k_ref[:, :HEAD_DIM], v_ref[:, :HEAD_DIM], causal)
        total = dot(attended.astype(BF16), w_ref[:HEAD_DIM])
        for f in range(2):
            cols = slice((2 + f) * HEAD_DIM, (3 + f) * HEAD_DIM)
            mult = mult_ref[f : f + 1, :]
            own = jnp.where(causal, dot_t(q[:, cols], k_ref[:, cols]), NEG)
            away = jnp.where(mult > 0, dot_t(q[:, cols], far[f]), NEG)
            peak = jnp.maximum(jnp.max(own, axis=1, keepdims=True), jnp.max(away, axis=1, keepdims=True))
            own = jnp.exp2((own - peak) * SCALE2)
            away = jnp.exp2((away - peak) * SCALE2) * mult
            denom = jnp.sum(own, axis=1, keepdims=True) + jnp.sum(away, axis=1, keepdims=True)
            attended = (dot(own.astype(BF16), v_ref[:, cols]) + dot(away.astype(BF16), far[2 + f])) / denom
            total += dot(attended.astype(BF16), w_ref[cols, :])
        out_ref[...] = total.astype(BF16)


def last_kernel(own_ref, core_ref, far_ref, moved_ref, w0, w1, w2, w3, out_ref):
    total = own_ref[...].astype(F32) + core_ref[...].astype(F32) + far_ref[...].astype(F32)
    outer, heads, inner, depth = moved_ref.shape
    for flip, w in enumerate((w0, w1, w2, w3)):
        total += dot(moved_ref[:, flip].reshape(outer * inner, depth), w[...])
    out_ref[...] = total.astype(BF16)


def swap(x, axis, flip, count):
    return lax.ppermute(x, axis, [(i, i ^ flip) for i in range(count)])


def gather_tails(mine, count):
    have, arrays = 1, [mine[None]]
    while have < count:
        held = arrays[0] if len(arrays) == 1 else jnp.concatenate(arrays, axis=0)
        radix = 2 if have == 1 or count == 2 * have else 4
        arrays = [held] + [swap(held, "seq", have * i, count) for i in range(1, radix)]
        have *= radix
    return arrays


def per_device(queries, keys, values, summary_lists, out_weight):
    count, parts = lax.axis_size("seq"), lax.axis_size("head")
    block = queries.shape[0]
    me = lax.axis_index("seq")
    per = block // (count * parts)
    columns = per * parts
    col = slice(HEAD_DIM, 2 * HEAD_DIM)

    tail = jnp.stack(
        [x[block - SUMMARY :, h * HEAD_DIM : (h + 1) * HEAD_DIM] for x in (keys, values) for h in (2, 3)]
    )
    tails = gather_tails(tail, count)

    packed = jnp.stack([x[:, col].reshape(parts, count, per, HEAD_DIM) for x in (queries, keys, values)])
    packed = packed.transpose(2, 0, 1, 3, 4).reshape(count, 3 * columns, HEAD_DIM)
    moved = lax.all_to_all(packed, "seq", split_axis=0, concat_axis=0, tiled=True)
    moved = moved.reshape(count, 3, columns, HEAD_DIM)
    if columns % 16:
        moved = moved.transpose(1, 0, 2, 3).reshape(1, 3, block, HEAD_DIM)

    w_col = out_weight[col]
    w_far = swap(w_col, "head", 2, parts)
    w_core = swap(w_col, "head", 1, parts)
    w_both = swap(w_far, "head", 1, parts)

    slot_block = me ^ jnp.arange(count, dtype=jnp.int32)
    names = (summary_lists[0][:, :, None] == slot_block) & (slot_block < me)
    mult = jnp.repeat(jnp.sum(names.astype(F32), axis=1), SUMMARY, axis=1)

    def partial_sums(flips):
        shape = (block // parts, out_weight.shape[1])
        flops = len(flips) * shape[0] * 2 * 3 * HEAD_DIM * (3 * block + shape[1])
        return call(
            functools.partial(part_kernel, flips, parts, len(tails)),
            [shape] * len(flips),
            (queries, keys, values, out_weight, mult, *tails),
            flops,
        )

    (both_sum,) = partial_sums((3,))
    both_in = swap(both_sum, "head", 1, parts)
    (far_sum,) = partial_sums((2,))
    far_in = swap((far_sum.astype(F32) + both_in.astype(F32)).astype(BF16), "head", 2, parts)
    core_sum, own_sum = partial_sums((1, 0))
    core_in = swap(core_sum, "head", 1, parts)

    column_shape = (moved.shape[0], moved.shape[2], HEAD_DIM)
    (column_out,) = call(
        functools.partial(column_kernel, columns), [column_shape], (moved,), 4 * block * block * HEAD_DIM
    )
    column_out = column_out.reshape(count * parts, per, HEAD_DIM)
    back = lax.all_to_all(column_out, ("seq", "head"), split_axis=0, concat_axis=0, tiled=True)
    back = back.reshape(count, parts, per, HEAD_DIM)
    if per % 16:
        back = back.transpose(1, 0, 2, 3).reshape(1, parts, count * per, HEAD_DIM)
    back = back[:, lax.axis_index("head") ^ jnp.arange(parts)]
    (mixed,) = call(
        last_kernel,
        [own_sum.shape],
        (own_sum, core_in, far_in, back, w_col, w_core, w_far, w_both),
        2 * own_sum.size * parts * HEAD_DIM,
    )
    return mixed


def solution(mesh):
    return jax.shard_map(
        per_device,
        mesh=mesh,
        in_specs=(
            P("seq", "head"),
            P("seq", "head"),
            P("seq", "head"),
            P("seq", "head", None),
            P("head", None),
        ),
        out_specs=P(("seq", "head"), None),
        check_vma=False,
    )
```

time: 147 us -> 66.5 us (0.45)
  blocking collectives: 75.1 us -> 0 us
  between operations: 13.6 us -> 0.21 us
  Pallas kernels: 0 us -> 13 us
  matrix products: 11.7 us -> 0 us
  local copies, waits for them, and re-layouts: 5.47 us -> 16.6 us
  waiting for transfers between devices: 19.4 us -> 13.1 us
    all_gather x2 -> x0, blocking collectives: 63.7 us -> none  [the longest x1 32.5 us: per_device(): piece_v = lax.all_gather(tail_v, 'seq', axis=0, tiled=True)]
    pallas_call x0 -> x5, Pallas kernels: none -> 13 us  [call(): pl.pallas_call(kernel, out_shape=out, in_specs=[VMEM] * len(operands), ou...]
    dot_general x9 -> x0, matrix products: 11.7 us -> none  [the longest x1 5.46 us: per_device(): jnp.dot(swapped, lax.all_gather(out_weight, 'head', axis=0, tiled=True),...]
    all_to_all x1 -> x0, blocking collectives: 11.4 us -> none  [per_device(): lax.all_to_all(attended, 'head', split_axis=0, concat_axis=1, tiled=True)]
    unnamed x17 -> x36, local copies, waits for them, and re-layouts: 1.15 us -> 12.4 us
    ppermute x0 -> x10, starting transfers between devices: none -> 10.6 us  [swap(): return lax.ppermute(x, axis, [(i, i ^ flip) for i in range(count)])]
    all_to_all x4 -> x2, waiting for transfers between devices: 18.6 us -> 8.2 us  [the longest x1 8.2 us: per_device(): lax.all_to_all(column_out, ('seq', 'head'), split_axis=0, concat_axis=0,...]
    all_to_all x4 -> x2, starting transfers between devices: 19.4 us -> 10 us  [the longest x1 5.92 us: per_device(): lax.all_to_all(column_out, ('seq', 'head'), split_axis=0, concat_axis=0,...]
  transfers between devices with their start and end apart: 5 -> 12, of which waited for: 3 -> 3; matrix products, arithmetic and copies ran while one was open for 9% -> 8% of each run, Pallas kernels for 0% -> 15%
where the time goes in v1:
time: 66.5 us; the launch traced here: 65.6 us
  starting transfers between devices  20.7 us (31%)
  local copies, waits for them, and re-layouts  16.6 us (25%)
  waiting for transfers between devices  13.1 us (20%)
  Pallas kernels  13 us (20%)
  other arithmetic  2.09 us (3%)
    pallas_call x5, Pallas kernels, call(): pl.pallas_call(kernel, out_shape=out, in_specs=[VMEM] * len(operands), ou...  13 us
    unnamed x36, local copies, waits for them, and re-layouts  12.4 us
    ppermute x10, starting transfers between devices, swap(): return lax.ppermute(x, axis, [(i, i ^ flip) for i in range(count)])  10.6 us
    all_to_all x1, waiting for transfers between devices, per_device(): lax.all_to_all(column_out, ('seq', 'head'), split_axis=0, concat_axis=0,...  8.2 us
    all_to_all x1, starting transfers between devices, per_device(): lax.all_to_all(column_out, ('seq', 'head'), split_axis=0, concat_axis=0,...  5.92 us
    ppermute x10, waiting for transfers between devices, swap(): return lax.ppermute(x, axis, [(i, i ^ flip) for i in range(count)])  4.87 us
    all_to_all x1, starting transfers between devices, per_device(): lax.all_to_all(packed, 'seq', split_axis=0, concat_axis=0, tiled=True)  4.1 us
    slice x1, local copies, waits for them, and re-layouts, per_device(): w_col = out_weight[col]  1.88 us
  transfers between devices with their start and end apart: 12, of which 3 were waited for; matrix products, arithmetic and copies ran while one was open for 8% of the time, Pallas kernels for 15%

profile of v1, /device:TPU:0, one launch (start us, length us, event | category | flops | bytes accessed | tf_op | source)
XLA Modules:
  0.0 65.6 jit_solution(170857043812001516)
XLA Ops:
  0.8 3.0 %collective-permute-start = (bf16[1,4,32,128]{3,2,1,0:T(8,128)(2,1)S(1)}, bf16[1,4,32,128]{3,2,1,0:T(8,128)(2,1)S(1)}, u32[]{:S(2)}, u32[]{:S(2)}) collective-permute-start(bf16[1,4,32,128]{3,2,1,0:T(8,128)(2,1)S(1)} %maximum_bitcast_fusion.1), channel_id=1, source_target_pairs={{0,4},{4,0},{8,12},{12,8},{16,20},{20,16},{24,28},{28,24},{1,5},{5... | collective-permute-start | bytes 98312 | tf_op jit(solution)/shard_map/ppermute | solution.py:102
  3.8 1.9 %slice.31.w0 = bf16[128,2048]{1,0:T(8,128)(2,1)} slice(bf16[512,2048]{1,0:T(8,128)(2,1)} %w_ref.5), slice={[128:256], [0:2048]} | slice | bytes 1048576 | tf_op jit(solution)/shard_map/slice | solution.py:135
  5.6 1.5 %collective-permute-start.8 = (bf16[128,2048]{1,0:T(8,128)(2,1)}, bf16[128,2048]{1,0:T(8,128)(2,1)}, u32[]{:S(2)}, u32[]{:S(2)}) collective-permute-start(bf16[128,2048]{1,0:T(8,128)(2,1)} %slice.31.w0), channel_id=1, source_target_pairs={{0,2},{1,3},{2,0},{3,1},{4,6},{5,7},{6,4},{7,5},{8,10},{9,11},{10,... | collective-permute-start | bytes 1572872 | tf_op jit(solution)/shard_map/ppermute | solution.py:102
  7.2 1.6 %collective-permute-start.1 = (bf16[2,4,32,128]{3,2,1,0:T(8,128)(2,1)S(1)}, bf16[2,4,32,128]{3,2,1,0:T(8,128)(2,1)S(1)}, u32[]{:S(2)}, u32[]{:S(2)}) collective-permute-start(bf16[2,4,32,128]{3,2,1,0:T(8,128)(2,1)S(1)} %pad_maximum_fusion.refs_0_), channel_id=1, source_target_pairs={{0,8},{4,12},{8,0},{12,4},{16,24},{20,28},{24,16},{28,20},{1,9},{5... | collective-permute-start | bytes 196616 | tf_op jit(solution)/shard_map/ppermute | solution.py:102
  8.8 2.6 %collective-permute-start.2 = (bf16[2,4,32,128]{3,2,1,0:T(8,128)(2,1)S(1)}, bf16[2,4,32,128]{3,2,1,0:T(8,128)(2,1)S(1)}, u32[]{:S(2)}, u32[]{:S(2)}) collective-permute-start(bf16[2,4,32,128]{3,2,1,0:T(8,128)(2,1)S(1)} %pad_maximum_fusion.refs_0_), channel_id=1, source_target_pairs={{0,16},{4,20},{8,24},{12,28},{16,0},{20,4},{24,8},{28,12},{1,17},{... | collective-permute-start | bytes 196616 | tf_op jit(solution)/shard_map/ppermute | solution.py:102
  12.6 2.9 %collective-permute-done.2.refs_2_ = bf16[2,4,32,128]{3,2,1,0:T(8,128)(2,1)S(1)} collective-permute-done((bf16[2,4,32,128]{3,2,1,0:T(8,128)(2,1)S(1)}, bf16[2,4,32,128]{3,2,1,0:T(8,128)(2,1)S(1)}, u32[]{:S(2)}, u32[]{:S(2)}) %collective-permute-start.2) | collective-permute-done | bytes 65568 | tf_op jit(solution)/shard_map/ppermute | solution.py:102
  15.5 2.0 %collective-permute-done.3.refs_3_ = bf16[2,4,32,128]{3,2,1,0:T(8,128)(2,1)S(1)} collective-permute-done((bf16[2,4,32,128]{3,2,1,0:T(8,128)(2,1)S(1)}, bf16[2,4,32,128]{3,2,1,0:T(8,128)(2,1)S(1)}, u32[]{:S(2)}, u32[]{:S(2)}) %collective-permute-start.3) | collective-permute-done | bytes 65568 | tf_op jit(solution)/shard_map/ppermute | solution.py:102
  17.5 1.6 %copy-done = bf16[512,2048]{1,0:T(8,128)(2,1)S(1)} copy-done((bf16[512,2048]{1,0:T(8,128)(2,1)S(1)}, bf16[512,2048]{1,0:T(8,128)(2,1)}, u32[]{:S(2)}) %copy-start) | copy-done | bytes 2097176
  19.1 1.0 %copy-done.2 = bf16[512,512]{1,0:T(8,128)(2,1)S(1)} copy-done((bf16[512,512]{1,0:T(8,128)(2,1)S(1)}, bf16[512,512]{1,0:T(8,128)(2,1)}, u32[]{:S(2)}) %copy-start.2) | copy-done | bytes 524312
  20.1 1.0 %copy-done.4 = bf16[512,512]{1,0:T(8,128)(2,1)S(1)} copy-done((bf16[512,512]{1,0:T(8,128)(2,1)S(1)}, bf16[512,512]{1,0:T(8,128)(2,1)}, u32[]{:S(2)}) %copy-start.4) | copy-done | bytes 524312
  21.2 1.0 %copy-done.6 = bf16[512,512]{1,0:T(8,128)(2,1)S(1)} copy-done((bf16[512,512]{1,0:T(8,128)(2,1)S(1)}, bf16[512,512]{1,0:T(8,128)(2,1)}, u32[]{:S(2)}) %copy-start.6) | copy-done | bytes 524312
  22.2 2.5 %shard_map.57 = bf16[128,2048]{1,0:T(8,128)(2,1)} custom-call(bf16[512,512]{1,0:T(8,128)(2,1)S(1)} %copy-done.6, bf16[512,512]{1,0:T(8,128)(2,1)S(1)} %copy-done.2, bf16[512,512]{1,0:T(8,128)(2,1)S(1)} %copy-done.4, bf16[512,2048]{1,0:T(8,128)(2,1)S(1)} %copy-done, f32[2,256]{1,0:T(2,128)S(1)} %reshape.39.mult_ref, ...), custom_call_target="tpu_custom_call" | custom-call | flops 352321536 | bytes 4458496 | tf_op jit(solution)/shard_map/pallas_call | solution.py:23
  28.6 4.1 %all-to-all-start = ((bf16[8,192,128]{2,1,0:T(8,128)(2,1)}), bf16[8,192,128]{2,1,0:T(8,128)(2,1)}, u32[]{:S(2)}, u32[]{:S(2)}) async-start(bf16[8,192,128]{2,1,0:T(8,128)(2,1)} %bitcast.29), calls=%async_computation | async-start | bytes 786432 | tf_op jit(solution)/shard_map/all_to_all | solution.py:130
  32.7 1.0 %copy-done.7 = bf16[512,512]{1,0:T(8,128)(2,1)S(1)} copy-done((bf16[512,512]{1,0:T(8,128)(2,1)S(1)}, bf16[512,512]{1,0:T(8,128)(2,1)}, u32[]{:S(2)}) %copy-start.7) | copy-done | bytes 524312
  33.8 0.8 %copy-done.9 = bf16[2,4,32,128]{3,2,1,0:T(8,128)(2,1)S(1)} copy-done((bf16[2,4,32,128]{3,2,1,0:T(8,128)(2,1)S(1)}, bf16[2,4,32,128]{3,2,1,0:T(8,128)(2,1)}, u32[]{:S(2)}) %copy-start.9) | copy-done | bytes 65560
  34.6 0.8 %copy-done.11 = bf16[2,4,32,128]{3,2,1,0:T(8,128)(2,1)S(1)} copy-done((bf16[2,4,32,128]{3,2,1,0:T(8,128)(2,1)S(1)}, bf16[2,4,32,128]{3,2,1,0:T(8,128)(2,1)}, u32[]{:S(2)}) %copy-start.11) | copy-done | bytes 65560
  35.4 0.8 %copy-done.13 = bf16[2,4,32,128]{3,2,1,0:T(8,128)(2,1)S(1)} copy-done((bf16[2,4,32,128]{3,2,1,0:T(8,128)(2,1)S(1)}, bf16[2,4,32,128]{3,2,1,0:T(8,128)(2,1)}, u32[]{:S(2)}) %copy-start.13) | copy-done | bytes 65560
  37.1 3.4 %shard_map.55 = (bf16[128,2048]{1,0:T(8,128)(2,1)}, bf16[128,2048]{1,0:T(8,128)(2,1)S(1)}) custom-call(bf16[512,512]{1,0:T(8,128)(2,1)S(1)} %copy-done.7, bf16[512,512]{1,0:T(8,128)(2,1)S(1)} %copy-done.3, bf16[512,512]{1,0:T(8,128)(2,1)S(1)} %copy-done.5, bf16[512,2048]{1,0:T(8,128)(2,1)S(1)} %copy-done.1, f32[2,256]{1,0:T(2,128)S(1)} %reshape.39.mult_ref, ...), custom_call_target="tpu_custom_call" | custom-call | flops 704643072 | bytes 4982784 | tf_op jit(solution)/shard_map/pallas_call | solution.py:23
  41.4 1.7 %shard_map.56 = bf16[128,2048]{1,0:T(8,128)(2,1)S(1)} custom-call(bf16[512,512]{1,0:T(8,128)(2,1)S(1)} %copy-done.7, bf16[512,512]{1,0:T(8,128)(2,1)S(1)} %copy-done.3, bf16[512,512]{1,0:T(8,128)(2,1)S(1)} %copy-done.5, bf16[512,2048]{1,0:T(8,128)(2,1)S(1)} %copy-done.1, f32[2,256]{1,0:T(2,128)S(1)} %reshape.39.mult_ref, ...), custom_call_target="tpu_custom_call" | custom-call | flops 352321536 | bytes 4458496 | tf_op jit(solution)/shard_map/pallas_call | solution.py:23
  43.6 1.2 %add_convert_fusion = bf16[128,2048]{1,0:T(8,128)(2,1)S(1)} fusion(bf16[128,2048]{1,0:T(8,128)(2,1)} %collective-permute-done.5, bf16[128,2048]{1,0:T(8,128)(2,1)S(1)} %shard_map.56), kind=kLoop, calls=%fused_computation.1 | loop fusion | flops 1048576 | bytes 1572864 | tf_op jit(solution)/shard_map/convert_element_type | solution.py:157
  45.3 2.4 %shard_map.58 = bf16[8,64,128]{2,1,0:T(8,128)(2,1)} custom-call(bf16[8,3,64,128]{3,2,1,0:T(8,128)(2,1)} %bitcast.11.moved_ref), custom_call_target="tpu_custom_call" | custom-call | flops 134217728 | bytes 524288 | tf_op jit(solution)/shard_map/pallas_call | solution.py:23
  47.8 5.9 %all-to-all-start.1 = ((bf16[32,16,128]{2,1,0:T(8,128)(2,1)}), bf16[32,16,128]{2,1,0:T(8,128)(2,1)S(1)}, u32[]{:S(2)}, u32[]{:S(2)}) async-start(bf16[32,16,128]{2,1,0:T(8,128)(2,1)} %bitcast.12), calls=%async_computation.1 | async-start | bytes 262144 | tf_op jit(solution)/shard_map/all_to_all | solution.py:166
  53.7 8.2 %all-to-all-done.1 = bf16[32,16,128]{2,1,0:T(8,128)(2,1)S(1)} async-done(((bf16[32,16,128]{2,1,0:T(8,128)(2,1)}), bf16[32,16,128]{2,1,0:T(8,128)(2,1)S(1)}, u32[]{:S(2)}, u32[]{:S(2)}) %all-to-all-start.1) | async-done | bytes 131104 | tf_op jit(solution)/shard_map/all_to_all | solution.py:166
  62.6 3.0 %shard_map.59 = bf16[128,2048]{1,0:T(8,128)(2,1)} custom-call(bf16[128,2048]{1,0:T(8,128)(2,1)S(1)} %copy-done.17, bf16[128,2048]{1,0:T(8,128)(2,1)} %collective-permute-done.4.core_ref, bf16[128,2048]{1,0:T(8,128)(2,1)S(1)} %collective-permute-done.6.far_ref, bf16[8,4,16,128]{3,2,1,0:T(8,128)(2,1)S(1)} %bitcast.28, bf16[128,2048]{1,0:T(8,128)(2,1)} %slice.31.w0, ...), custom_call_target="tpu_custom_call" | custom-call | flops 268435456 | bytes 4325376 | tf_op jit(solution)/shard_map/pallas_call | solution.py:23
  (63 shorter events, 9.3 us)
Async XLA Ops:
  0.8 6.4 %collective-permute-start = (bf16[1,4,32,128]{3,2,1,0:T(8,128)(2,1)S(1)}, bf16[1,4,32,128]{3,2,1,0:T(8,128)(2,1)S(1)}, u32[]{:S(2)}, u32[]{:S(2)}) collective-permute-start(bf16[1,4,32,128]{3,2,1,0:T(8,128)(2,1)S(1)} %maximum_bitcast_fusion.1), channel_id=1, source_target_pairs={{0,4},{4,0},{8,12},{12,8},{16,20},{20,16},{24,28},{28,24},{1,5},{5... | collective-permute-start | bytes 98312 | tf_op jit(solution)/shard_map/ppermute | solution.py:102
  5.6 37.4 %collective-permute-start.8 = (bf16[128,2048]{1,0:T(8,128)(2,1)}, bf16[128,2048]{1,0:T(8,128)(2,1)}, u32[]{:S(2)}, u32[]{:S(2)}) collective-permute-start(bf16[128,2048]{1,0:T(8,128)(2,1)} %slice.31.w0), channel_id=1, source_target_pairs={{0,2},{1,3},{2,0},{3,1},{4,6},{5,7},{6,4},{7,5},{8,10},{9,11},{10,... | collective-permute-start | bytes 1572872 | tf_op jit(solution)/shard_map/ppermute | solution.py:102
  7.2 5.4 %collective-permute-start.1 = (bf16[2,4,32,128]{3,2,1,0:T(8,128)(2,1)S(1)}, bf16[2,4,32,128]{3,2,1,0:T(8,128)(2,1)S(1)}, u32[]{:S(2)}, u32[]{:S(2)}) collective-permute-start(bf16[2,4,32,128]{3,2,1,0:T(8,128)(2,1)S(1)} %pad_maximum_fusion.refs_0_), channel_id=1, source_target_pairs={{0,8},{4,12},{8,0},{12,4},{16,24},{20,28},{24,16},{28,20},{1,9},{5... | collective-permute-start | bytes 196616 | tf_op jit(solution)/shard_map/ppermute | solution.py:102
  8.8 6.7 %collective-permute-start.2 = (bf16[2,4,32,128]{3,2,1,0:T(8,128)(2,1)S(1)}, bf16[2,4,32,128]{3,2,1,0:T(8,128)(2,1)S(1)}, u32[]{:S(2)}, u32[]{:S(2)}) collective-permute-start(bf16[2,4,32,128]{3,2,1,0:T(8,128)(2,1)S(1)} %pad_maximum_fusion.refs_0_), channel_id=1, source_target_pairs={{0,16},{4,20},{8,24},{12,28},{16,0},{20,4},{24,8},{28,12},{1,17},{... | collective-permute-start | bytes 196616 | tf_op jit(solution)/shard_map/ppermute | solution.py:102
  11.4 6.1 %collective-permute-start.3 = (bf16[2,4,32,128]{3,2,1,0:T(8,128)(2,1)S(1)}, bf16[2,4,32,128]{3,2,1,0:T(8,128)(2,1)S(1)}, u32[]{:S(2)}, u32[]{:S(2)}) collective-permute-start(bf16[2,4,32,128]{3,2,1,0:T(8,128)(2,1)S(1)} %pad_maximum_fusion.refs_0_), channel_id=1, source_target_pairs={{0,24},{4,28},{8,16},{12,20},{16,8},{20,12},{24,0},{28,4},{1,25},{... | collective-permute-start | bytes 196616 | tf_op jit(solution)/shard_map/ppermute | solution.py:102
  17.5 1.6 %copy-start = (bf16[512,2048]{1,0:T(8,128)(2,1)S(1)}, bf16[512,2048]{1,0:T(8,128)(2,1)}, u32[]{:S(2)}) copy-start(bf16[512,2048]{1,0:T(8,128)(2,1)} %w_ref.5) | copy-start | bytes 6291460
  19.1 1.0 %copy-start.2 = (bf16[512,512]{1,0:T(8,128)(2,1)S(1)}, bf16[512,512]{1,0:T(8,128)(2,1)}, u32[]{:S(2)}) copy-start(bf16[512,512]{1,0:T(8,128)(2,1)} %k_ref.5) | copy-start | bytes 1572868
  20.1 1.0 %copy-start.4 = (bf16[512,512]{1,0:T(8,128)(2,1)S(1)}, bf16[512,512]{1,0:T(8,128)(2,1)}, u32[]{:S(2)}) copy-start(bf16[512,512]{1,0:T(8,128)(2,1)} %v_ref.5) | copy-start | bytes 1572868
  21.2 1.0 %copy-start.6 = (bf16[512,512]{1,0:T(8,128)(2,1)S(1)}, bf16[512,512]{1,0:T(8,128)(2,1)}, u32[]{:S(2)}) copy-start(bf16[512,512]{1,0:T(8,128)(2,1)} %q_ref.5) | copy-start | bytes 1572868
  22.2 5.5 %slice-start = ((bf16[512,512]{1,0:T(8,128)(2,1)}), bf16[512,128]{1,0:T(8,128)(2,1)S(1)}, s32[]{:S(2)}) async-start(bf16[512,512]{1,0:T(8,128)(2,1)} %k_ref.5), calls=%async_computation.2 | async-start | bytes 262144 | tf_op jit(solution)/shard_map/slice | solution.py:128
  22.2 5.5 %slice-start.1 = ((bf16[512,512]{1,0:T(8,128)(2,1)}), bf16[512,128]{1,0:T(8,128)(2,1)S(1)}, s32[]{:S(2)}) async-start(bf16[512,512]{1,0:T(8,128)(2,1)} %v_ref.5), calls=%async_computation.3 | async-start | bytes 262144 | tf_op jit(solution)/shard_map/slice | solution.py:128
  22.2 5.5 %slice-start.2 = ((bf16[512,512]{1,0:T(8,128)(2,1)}), bf16[512,128]{1,0:T(8,128)(2,1)S(1)}, s32[]{:S(2)}) async-start(bf16[512,512]{1,0:T(8,128)(2,1)} %q_ref.5), calls=%async_computation.4 | async-start | bytes 262144 | tf_op jit(solution)/shard_map/slice | solution.py:128
  27.2 5.5 %copy-start.1 = (bf16[512,2048]{1,0:T(8,128)(2,1)S(1)}, bf16[512,2048]{1,0:T(8,128)(2,1)}, u32[]{:S(2)}) copy-start(bf16[512,2048]{1,0:T(8,128)(2,1)} %w_ref.5) | copy-start | bytes 6291460
  27.2 5.5 %copy-start.3 = (bf16[512,512]{1,0:T(8,128)(2,1)S(1)}, bf16[512,512]{1,0:T(8,128)(2,1)}, u32[]{:S(2)}) copy-start(bf16[512,512]{1,0:T(8,128)(2,1)} %k_ref.5) | copy-start | bytes 1572868
  27.2 5.5 %copy-start.5 = (bf16[512,512]{1,0:T(8,128)(2,1)S(1)}, bf16[512,512]{1,0:T(8,128)(2,1)}, u32[]{:S(2)}) copy-start(bf16[512,512]{1,0:T(8,128)(2,1)} %v_ref.5) | copy-start | bytes 1572868
  27.2 16.4 %collective-permute-start.5 = (bf16[128,2048]{1,0:T(8,128)(2,1)}, bf16[128,2048]{1,0:T(8,128)(2,1)}, u32[]{:S(2)}, u32[]{:S(2)}) collective-permute-start(bf16[128,2048]{1,0:T(8,128)(2,1)} %shard_map.57), channel_id=1, source_target_pairs={{0,1},{1,0},{2,3},{3,2},{4,5},{5,4},{6,7},{7,6},{8,9},{9,8},{10,11... | collective-permute-start | bytes 1572872 | tf_op jit(solution)/shard_map/ppermute | solution.py:102
  27.2 35.3 %collective-permute-start.7 = (bf16[128,2048]{1,0:T(8,128)(2,1)}, bf16[128,2048]{1,0:T(8,128)(2,1)}, u32[]{:S(2)}, u32[]{:S(2)}) collective-permute-start(bf16[128,2048]{1,0:T(8,128)(2,1)} %slice.31.w0), channel_id=1, source_target_pairs={{0,1},{1,0},{2,3},{3,2},{4,5},{5,4},{6,7},{7,6},{8,9},{9,8},{10,11... | collective-permute-start | bytes 1572872 | tf_op jit(solution)/shard_map/ppermute | solution.py:102
  28.6 16.8 %all-to-all-start = ((bf16[8,192,128]{2,1,0:T(8,128)(2,1)}), bf16[8,192,128]{2,1,0:T(8,128)(2,1)}, u32[]{:S(2)}, u32[]{:S(2)}) async-start(bf16[8,192,128]{2,1,0:T(8,128)(2,1)} %bitcast.29), calls=%async_computation | async-start | bytes 786432 | tf_op jit(solution)/shard_map/all_to_all | solution.py:130
  32.7 1.0 %copy-start.7 = (bf16[512,512]{1,0:T(8,128)(2,1)S(1)}, bf16[512,512]{1,0:T(8,128)(2,1)}, u32[]{:S(2)}) copy-start(bf16[512,512]{1,0:T(8,128)(2,1)} %q_ref.5) | copy-start | bytes 1572868
  41.3 21.3 %collective-permute-start.4 = (bf16[128,2048]{1,0:T(8,128)(2,1)}, bf16[128,2048]{1,0:T(8,128)(2,1)}, u32[]{:S(2)}, u32[]{:S(2)}) collective-permute-start(bf16[128,2048]{1,0:T(8,128)(2,1)} %get-tuple-element.8), channel_id=1, source_target_pairs={{0,1},{1,0},{2,3},{3,2},{4,5},{5,4},{6,7},{7,6},{8,9},{9,8},{10,11... | collective-permute-start | bytes 1572872 | tf_op jit(solution)/shard_map/ppermute | solution.py:102
  43.1 19.5 %copy-start.17 = (bf16[128,2048]{1,0:T(8,128)(2,1)S(1)}, bf16[128,2048]{1,0:T(8,128)(2,1)}, u32[]{:S(2)}) copy-start(bf16[128,2048]{1,0:T(8,128)(2,1)} %copy-done.16) | copy-start | bytes 1572868
  43.1 19.5 %collective-permute-start.9 = (bf16[128,2048]{1,0:T(8,128)(2,1)}, bf16[128,2048]{1,0:T(8,128)(2,1)S(1)}, u32[]{:S(2)}, u32[]{:S(2)}) collective-permute-start(bf16[128,2048]{1,0:T(8,128)(2,1)} %collective-permute-done.8.w2), channel_id=1, source_target_pairs={{0,1},{1,0},{2,3},{3,2},{4,5},{5,4},{6,7},{7,6},{8,9},{9,8},{10,11... | collective-permute-start | bytes 1572872 | tf_op jit(solution)/shard_map/ppermute | solution.py:102
  44.7 17.8 %collective-permute-start.6 = (bf16[128,2048]{1,0:T(8,128)(2,1)S(1)}, bf16[128,2048]{1,0:T(8,128)(2,1)S(1)}, u32[]{:S(2)}, u32[]{:S(2)}) collective-permute-start(bf16[128,2048]{1,0:T(8,128)(2,1)S(1)} %add_convert_fusion), channel_id=1, source_target_pairs={{0,2},{1,3},{2,0},{3,1},{4,6},{5,7},{6,4},{7,5},{8,10},{9,11},{10,... | collective-permute-start | bytes 1572872 | tf_op jit(solution)/shard_map/ppermute | solution.py:102
  47.8 14.2 %all-to-all-start.1 = ((bf16[32,16,128]{2,1,0:T(8,128)(2,1)}), bf16[32,16,128]{2,1,0:T(8,128)(2,1)S(1)}, u32[]{:S(2)}, u32[]{:S(2)}) async-start(bf16[32,16,128]{2,1,0:T(8,128)(2,1)} %bitcast.12), calls=%async_computation.1 | async-start | bytes 262144 | tf_op jit(solution)/shard_map/all_to_all | solution.py:166
  (9 other events, 6.6 us)

commit v2 on v1

v2 whole, which is shorter than its diff:
```python
import functools
import math

import jax
import jax.numpy as jnp
from jax import lax
from jax.experimental import pallas as pl
from jax.experimental.pallas import tpu as pltpu
from jax.sharding import PartitionSpec as P

HEAD_DIM = 128
SUMMARY = 32
NEG = -1e30
JOIN_COST = 10**10
LAST_COST = 10**10
OWN_ROOM = 48
BF16 = jnp.bfloat16
F32 = jnp.float32
HBM = pl.BlockSpec(memory_space=pltpu.HBM)
VMEM = pl.BlockSpec(memory_space=pltpu.VMEM)
SCALE2 = HEAD_DIM ** (-0.5) * math.log2(math.e)


def call(kernel, out, operands, scratch=(), copies=1, cost=1, room=24):
    return pl.pallas_call(
        kernel,
        out_shape=[jax.ShapeDtypeStruct(x[1], x[2] if len(x) > 2 else BF16) for x in out],
        in_specs=[memory for memory, _ in operands],
        out_specs=[x[0] for x in out],
        scratch_shapes=[*scratch, pltpu.SemaphoreType.DMA((copies,))],
        compiler_params=pltpu.CompilerParams(vmem_limit_bytes=room * 2**20),
        cost_estimate=pl.CostEstimate(flops=cost, bytes_accessed=1, transcendentals=0),
    )(*(x for _, x in operands))


def start(sems, pairs, first=0):
    copies = [pltpu.make_async_copy(src, dst, sems.at[first + i]) for i, (src, dst) in enumerate(pairs)]
    for copy in copies:
        copy.start()
    return copies


def wait(copies):
    for copy in copies:
        copy.wait()


def dot_t(a, b):
    return lax.dot_general(a, b, (((1,), (1,)), ((), ())), preferred_element_type=F32)


def dot(a, b):
    return jnp.dot(a, b, preferred_element_type=F32)


def weigh(scores, valid):
    scores = jnp.where(valid, scores, NEG)
    peak = jnp.max(scores, axis=1, keepdims=True)
    weights = jnp.exp2((scores - peak) * SCALE2)
    return weights.astype(BF16), jnp.sum(weights, axis=1, keepdims=True), peak


def head(h):
    return slice(h * HEAD_DIM, (h + 1) * HEAD_DIM)


def tail_kernel(k_ref, v_ref, tail, sems):
    block = k_ref.shape[0]
    pairs = []
    for i, ref in enumerate((k_ref, v_ref)):
        for f in range(2):
            pairs.append((ref.at[pl.ds(block - SUMMARY, SUMMARY), pl.ds((2 + f) * HEAD_DIM, HEAD_DIM)], tail.at[2 * i + f]))
    wait(start(sems, pairs))


def pack_kernel(q_ref, k_ref, v_ref, w_ref, packed_ref, w_col_ref, cols, w_col, sems):
    parts = q_ref.shape[0]
    come, leave = [], []
    for i, ref in enumerate((q_ref, k_ref, v_ref)):
        come.append((ref.at[:, :, :, pl.ds(HEAD_DIM, HEAD_DIM)], cols.at[i]))
        for part in range(parts):
            leave.append((cols.at[i, part], packed_ref.at[:, i, part]))
    come.append((w_ref.at[pl.ds(HEAD_DIM, HEAD_DIM)], w_col))
    leave.append((w_col, w_col_ref))
    come = start(sems, come)
    gone = []
    first = len(come)
    for copy, makes in zip(come, (parts, parts, parts, 1)):
        wait([copy])
        gone += start(sems, leave[:makes], first)
        leave, first = leave[makes:], first + makes
    wait(gone)


def pack(queries, keys, values, out_weight, count, parts, per):
    width = queries.shape[1]
    (tail,) = call(tail_kernel, [(VMEM, (4, SUMMARY, HEAD_DIM))], [(HBM, keys), (HBM, values)], (), 4, room=63)
    if per % 16:
        cut = [x[:, HEAD_DIM : 2 * HEAD_DIM].reshape(parts, count, per, HEAD_DIM) for x in (queries, keys, values)]
        packed = jnp.stack(cut).transpose(2, 0, 1, 3, 4)
        return packed, tail, out_weight[HEAD_DIM : 2 * HEAD_DIM]
    w_shape = (HEAD_DIM, out_weight.shape[1])
    cut = [x.reshape(parts, count, per, width) for x in (queries, keys, values)]
    packed, w_col = call(
        pack_kernel,
        [(HBM, (count, 3, parts, per, HEAD_DIM)), (HBM, w_shape)],
        [(HBM, x) for x in (*cut, out_weight)],
        [pltpu.VMEM((3, parts, count, per, HEAD_DIM), BF16), pltpu.VMEM(w_shape, BF16)],
        5 + 3 * parts,
        room=63,
    )
    return packed, tail, w_col


def column_kernel(columns, moved_ref, out_ref, held, done, sems):
    outer, _, inner, depth = moved_ref.shape
    rows = outer * inner
    copies = start(sems, [(moved_ref.at[:, i], held.at[i]) for i in range(3)])
    wait(copies[:2])
    q, k, v = (held.at[i] for i in range(3))
    step = HEAD_DIM
    results = []
    for first in range(0, rows, step):
        upto = first + step
        at_q = first + lax.broadcasted_iota(jnp.int32, (step, 1), 0)
        at_k = lax.broadcasted_iota(jnp.int32, (1, upto), 1)
        valid = (lax.rem(at_q, columns) == lax.rem(at_k, columns)) & (at_k <= at_q)
        q_rows = q[...].reshape(rows, depth)[first:upto]
        results.append((upto, *weigh(dot_t(q_rows, k[...].reshape(rows, depth)[:upto]), valid)))
    wait(copies[2:])
    out = [dot(weights, v[...].reshape(rows, depth)[:upto]) / denom for upto, weights, denom, _ in results]
    done[...] = jnp.concatenate(out, axis=0).astype(BF16).reshape(outer, inner, depth)
    wait(start(sems, [(done, out_ref)]))


def own_kernel(q_ref, k_ref, v_ref, w_ref, row_ref, sum_ref, stat_ref, q_fixed, w_all, q_all, k_all, v_all, sems):
    pairs = [(q_ref, q_all), (k_ref, k_all), (v_ref, v_all)]
    pairs += [(q_ref.at[:, pl.ds(2 * HEAD_DIM, 2 * HEAD_DIM)], q_fixed)]
    pairs += [(w_ref.at[pl.ds(0, HEAD_DIM)], w_all.at[pl.ds(0, HEAD_DIM)])]
    pairs += [(w_ref.at[pl.ds(2 * HEAD_DIM, 2 * HEAD_DIM)], w_all.at[pl.ds(HEAD_DIM, 2 * HEAD_DIM)])]
    copies = start(sems, pairs)
    wait(copies[:3])
    block, step = q_ref.shape[0], HEAD_DIM
    for first in range(0, block, step):
        upto = first + step
        rows = slice(first, upto)
        at_q = first + lax.broadcasted_iota(jnp.int32, (step, 1), 0)
        at_k = lax.broadcasted_iota(jnp.int32, (1, upto), 1)
        for h in (0, 2, 3):
            weights, denom, peak = weigh(dot_t(q_all[rows, head(h)], k_all[:upto, head(h)]), at_k <= at_q)
            total = dot(weights, v_all[:upto, head(h)])
            if h == 0:
                row_ref[rows] = (total / denom).astype(BF16)
            else:
                sum_ref[h - 2, rows] = total
                low = lax.broadcasted_iota(jnp.int32, (step, HEAD_DIM), 1) < HEAD_DIM // 2
                stat_ref[h - 2, rows] = jnp.where(low, denom, peak)
    wait(copies[3:])


def own_part(queries, keys, values, out_weight):
    block = queries.shape[0]
    state = (VMEM, (2, block, HEAD_DIM), F32)
    weight_shape = (3 * HEAD_DIM, out_weight.shape[1])
    return call(
        own_kernel,
        [(VMEM, (block, HEAD_DIM)), state, state, (VMEM, (block, 2 * HEAD_DIM)), (VMEM, weight_shape)],
        [(HBM, x) for x in (queries, keys, values, out_weight)],
        [pltpu.VMEM(queries.shape, BF16)] * 3,
        6,
        room=OWN_ROOM,
    )


def part_kernel(flips, parts, slots, row_ref, sum_ref, stat_ref, q_ref, w_ref, mult_ref, *refs):
    tails, refs = refs[: len(slots)], refs[len(slots) :]
    outs, (far, sems) = refs[: len(flips)], refs[len(flips) :]
    pairs, at = [], 0
    for tail, many in zip(tails, slots):
        pairs.append((tail, far.at[pl.ds(at, many)]))
        at += many
    wait(start(sems, pairs))
    rows = q_ref.shape[0] // parts
    me = lax.axis_index("head")
    away_kv = [far[:, i].reshape(at * SUMMARY, HEAD_DIM) for i in range(4)]
    for flip, out_ref in zip(flips, outs):
        here = pl.ds(pl.multiple_of((me ^ flip) * rows, rows), rows)
        found = [row_ref[here, :]]
        for f in range(2):
            mult = mult_ref[f : f + 1, :]
            away = jnp.where(mult > 0, dot_t(q_ref[here, head(f)], away_kv[f]), NEG)
            own_denom, own_peak = stat_ref[f, here, :1], stat_ref[f, here, HEAD_DIM // 2 : HEAD_DIM // 2 + 1]
            peak = jnp.maximum(own_peak, jnp.max(away, axis=1, keepdims=True))
            shrink = jnp.exp2((own_peak - peak) * SCALE2)
            away = jnp.exp2((away - peak) * SCALE2) * mult
            denom = own_denom * shrink + jnp.sum(away, axis=1, keepdims=True)
            total = sum_ref[f, here, :] * shrink + dot(away.astype(BF16), away_kv[2 + f])
            found.append((total / denom).astype(BF16))
        out_ref[...] = dot(jnp.concatenate(found, axis=1), w_ref[...]).astype(BF16)


def add_kernel(a_ref, b_ref, out_ref, _):
    out_ref[...] = (a_ref[...].astype(F32) + b_ref[...].astype(F32)).astype(BF16)


def join_kernel(*refs):
    at = 0
    for ref in refs[:-2]:
        refs[-2][at : at + ref.shape[0]] = ref[...]
        at += ref.shape[0]


def near_kernel(own_ref, core_ref, moved_ref, *refs):
    ws, (out_ref, sums, moved, w_all, sems) = refs[:-5], refs[-5:]
    pairs = [(moved_ref, moved)] + [(w, w_all.at[i]) for i, w in enumerate(ws)]
    pairs += [(ref, sums.at[i]) for i, ref in enumerate((own_ref, core_ref))]
    wait(start(sems, pairs))
    outer, heads, inner, depth = moved.shape
    me = lax.axis_index("head")
    found = jnp.concatenate([moved[:, me ^ i].reshape(outer * inner, depth) for i in range(heads)], axis=1)
    total = dot(found, w_all[...].reshape(heads * depth, w_all.shape[2]))
    out_ref[...] = total + sums[0].astype(F32) + sums[1].astype(F32)


def last_kernel(near_ref, far_ref, out_ref, near, far, done, sems):
    pieces = sems.shape[0] // 3
    cut = done.shape[1] // pieces
    cols = [pl.ds(i * cut, cut) for i in range(pieces)]
    copies = start(sems, [(a.at[:, c], b.at[:, c]) for c in cols for a, b in ((near_ref, near), (far_ref, far))])
    sent = []
    for i, c in enumerate(cols):
        wait(copies[2 * i : 2 * i + 2])
        done[:, c] = (near[:, c] + far[:, c].astype(F32)).astype(BF16)
        sent += start(sems, [(done.at[:, c], out_ref.at[:, c])], 2 * pieces + i)
    wait(sent)


def swap(x, axis, flip, count):
    return lax.ppermute(x, axis, [(i, i ^ flip) for i in range(count)])


def gather_tails(mine, count):
    order, arrays = [0], [mine[None]]
    bits = [(count // 4**i, 4) for i in range(1, 8) if count % 4**i == 0 and count // 4**i >= 2] + [(1, 2)]
    if count & (count - 1) or bits[-2:][0][0] != 2:
        return [lax.all_gather(mine, "seq")], None
    for step, radix in bits:
        held = arrays[0]
        if len(arrays) > 1:
            shape = (sum(x.shape[0] for x in arrays), *mine.shape)
            (held,) = call(join_kernel, [(VMEM, shape)], [(VMEM, x) for x in arrays], cost=JOIN_COST)
        arrays = [held] + [swap(held, "seq", step * i, count) for i in range(1, radix)]
        order = [j ^ (step * i) for i in range(radix) for j in order]
    return arrays, order


def per_device(queries, keys, values, summary_lists, out_weight):
    count, parts = lax.axis_size("seq"), lax.axis_size("head")
    block = queries.shape[0]
    me = lax.axis_index("seq")
    per = block // (count * parts)
    columns = per * parts

    packed, tail, w_col = pack(queries, keys, values, out_weight, count, parts, per)
    tails, order = gather_tails(tail, count)

    moved = lax.all_to_all(
        packed.reshape(count, 3 * columns, HEAD_DIM), "seq", split_axis=0, concat_axis=0, tiled=True
    )
    moved = moved.reshape(count, 3, columns, HEAD_DIM)
    if columns % 16:
        moved = moved.transpose(1, 0, 2, 3).reshape(1, 3, block, HEAD_DIM)

    w_far = swap(w_col, "head", 2, parts)
    w_core = swap(w_col, "head", 1, parts)
    w_both = swap(w_far, "head", 1, parts)

    slot_block = jnp.arange(count, dtype=jnp.int32) if order is None else me ^ jnp.array(order, jnp.int32)
    names = (summary_lists[0][:, :, None] == slot_block) & (slot_block < me)
    mult = jnp.repeat(jnp.sum(names.astype(F32), axis=1), SUMMARY, axis=1)

    shape = (block // parts, out_weight.shape[1])
    held = [queries, keys, values, out_weight]
    if len(tails) > 1:
        *held, tails[0] = lax.optimization_barrier((*held, tails[0]))
    own = own_part(*held)

    column_shape = (moved.shape[0], moved.shape[2], HEAD_DIM)
    (column_out,) = call(
        functools.partial(column_kernel, columns),
        [(HBM, column_shape)],
        [(HBM, moved)],
        [pltpu.VMEM((3, *column_shape), BF16), pltpu.VMEM(column_shape, BF16)],
        3,
    )

    def partial_sums(flips):
        return call(
            functools.partial(part_kernel, flips, parts, [x.shape[0] for x in tails]),
            [(VMEM, shape)] * len(flips),
            [(VMEM, x) for x in (*own, mult)] + [(HBM, x) for x in tails],
            [pltpu.VMEM((count, 4, SUMMARY, HEAD_DIM), BF16)],
            len(tails),
        )

    both_sum, far_sum = partial_sums((3, 2))
    both_in = swap(both_sum, "head", 1, parts)
    (far_sum,) = call(add_kernel, [(VMEM, shape)], [(VMEM, far_sum), (VMEM, both_in)])
    far_in = swap(far_sum, "head", 2, parts)
    core_sum, own_sum = partial_sums((1, 0))
    core_in = swap(core_sum, "head", 1, parts)

    column_out = column_out.reshape(count * parts, per, HEAD_DIM)
    back = lax.all_to_all(column_out, ("seq", "head"), split_axis=0, concat_axis=0, tiled=True)
    back = back.reshape(count, parts, per, HEAD_DIM)
    if per % 16:
        back = back.transpose(1, 0, 2, 3).reshape(1, parts, count * per, HEAD_DIM)
    (near_sum,) = call(
        near_kernel,
        [(VMEM, shape, F32)],
        [(HBM, x) for x in (own_sum, core_in, back, w_col, w_core, w_far, w_both)],
        [
            pltpu.VMEM((2, *shape), BF16),
            pltpu.VMEM(back.shape, BF16),
            pltpu.VMEM((parts, HEAD_DIM, shape[1]), BF16),
        ],
        3 + parts,
        cost=LAST_COST,
    )
    (mixed,) = call(
        last_kernel,
        [(HBM, shape)],
        [(HBM, near_sum), (HBM, far_in)],
        [pltpu.VMEM(shape, F32), pltpu.VMEM(shape, BF16), pltpu.VMEM(shape, BF16)],
        3 * 4,
    )
    return mixed


def solution(mesh):
    return jax.shard_map(
        per_device,
        mesh=mesh,
        in_specs=(
            P("seq", "head"),
            P("seq", "head"),
            P("seq", "head"),
            P("seq", "head", None),
            P("head", None),
        ),
        out_specs=P(("seq", "head"), None),
        check_vma=False,
    )
```

time: 66.5 us -> 53.3 us (0.80)
  local copies, waits for them, and re-layouts: 16.6 us -> 1.24 us
  Pallas kernels: 13 us -> 16.3 us
  starting transfers between devices: 20.7 us -> 22.8 us
  other arithmetic: 2.09 us -> 0.17 us
  waiting for transfers between devices: 13.1 us -> 12.3 us
    unnamed x36 -> x18, local copies, waits for them, and re-layouts: 12.4 us -> 1.08 us
    pallas_call x5 -> x10, Pallas kernels: 13 us -> 16.3 us  [call(): pl.pallas_call(kernel, out_shape=[jax.ShapeDtypeStruct(x[1], x[2] if len(...]
    ppermute x10, starting transfers between devices: 10.6 us -> 12.5 us  [swap(): return lax.ppermute(x, axis, [(i, i ^ flip) for i in range(count)])]
    slice x7 -> x0, local copies, waits for them, and re-layouts: 1.89 us -> none  [the longest x1 1.88 us: per_device(): w_col = out_weight[col]]
    all_to_all x1, waiting for transfers between devices: 8.2 us -> 6.33 us  [per_device(): lax.all_to_all(column_out, ('seq', 'head'), split_axis=0, concat_axis=0,...]
    all_to_all x1, starting transfers between devices: 4.1 us -> 5.81 us  [per_device(): lax.all_to_all(packed.reshape(count, 3 * columns, HEAD_DIM), 'seq', split...]
    all_to_all x1, starting transfers between devices: 5.92 us -> 4.44 us  [per_device(): lax.all_to_all(column_out, ('seq', 'head'), split_axis=0, concat_axis=0,...]
    convert_element_type x1 -> x0, other arithmetic: 1.17 us -> none  [per_device(): (far_sum.astype(F32) + both_in.astype(F32)).astype(BF16)]
  transfers between devices with their start and end apart: 12 -> 12, of which waited for: 3 -> 3; matrix products, arithmetic and copies ran while one was open for 8% -> 1% of each run, Pallas kernels for 15% -> 26%
where the time goes in v2:
time: 53.3 us; the launch traced here: 52.9 us
  starting transfers between devices  22.8 us (43%)
  Pallas kernels  16.3 us (31%)
  waiting for transfers between devices  12.3 us (23%)
  local copies, waits for them, and re-layouts  1.24 us (2%)
    pallas_call x10, Pallas kernels, call(): pl.pallas_call(kernel, out_shape=[jax.ShapeDtypeStruct(x[1], x[2] if len(...  16.3 us
    ppermute x10, starting transfers between devices, swap(): return lax.ppermute(x, axis, [(i, i ^ flip) for i in range(count)])  12.5 us
    all_to_all x1, waiting for transfers between devices, per_device(): lax.all_to_all(column_out, ('seq', 'head'), split_axis=0, concat_axis=0,...  6.33 us
    ppermute x10, waiting for transfers between devices, swap(): return lax.ppermute(x, axis, [(i, i ^ flip) for i in range(count)])  5.95 us
    all_to_all x1, starting transfers between devices, per_device(): lax.all_to_all(packed.reshape(count, 3 * columns, HEAD_DIM), 'seq', split...  5.81 us
    all_to_all x1, starting transfers between devices, per_device(): lax.all_to_all(column_out, ('seq', 'head'), split_axis=0, concat_axis=0,...  4.44 us
    unnamed x18, local copies, waits for them, and re-layouts  1.08 us
  transfers between devices with their start and end apart: 12, of which 3 were waited for; matrix products, arithmetic and copies ran while one was open for 1% of the time, Pallas kernels for 26%

profile of v2, /device:TPU:0, one launch (start us, length us, event | category | flops | bytes accessed | tf_op | source)
XLA Modules:
  0.0 52.9 jit_solution(5329382280157582180)
XLA Ops:
  0.0 1.4 %shard_map.64 = bf16[4,32,128]{2,1,0:T(8,128)(2,1)} custom-call(bf16[512,512]{1,0:T(8,128)(2,1)} %k_ref.2, bf16[512,512]{1,0:T(8,128)(2,1)} %v_ref.2), custom_call_target="tpu_custom_call" | custom-call | flops 1 | bytes 1 | tf_op jit(solution)/shard_map/pallas_call | solution.py:25
  1.4 3.1 %collective-permute-start = (bf16[1,4,32,128]{3,2,1,0:T(8,128)(2,1)}, bf16[1,4,32,128]{3,2,1,0:T(8,128)(2,1)S(1)}, u32[]{:S(2)}, u32[]{:S(2)}) collective-permute-start(bf16[1,4,32,128]{3,2,1,0:T(8,128)(2,1)} %bitcast.14), channel_id=1, source_target_pairs={{0,8},{4,12},{8,0},{12,4},{16,24},{20,28},{24,16},{28,20},{1,9},{5... | collective-permute-start | bytes 98312 | tf_op jit(solution)/shard_map/ppermute | solution.py:239
  4.5 2.6 %collective-permute-start.1 = (bf16[1,4,32,128]{3,2,1,0:T(8,128)(2,1)}, bf16[1,4,32,128]{3,2,1,0:T(8,128)(2,1)S(1)}, u32[]{:S(2)}, u32[]{:S(2)}) collective-permute-start(bf16[1,4,32,128]{3,2,1,0:T(8,128)(2,1)} %bitcast.15), channel_id=1, source_target_pairs={{0,16},{4,20},{8,24},{12,28},{16,0},{20,4},{24,8},{28,12},{1,17},{... | collective-permute-start | bytes 98312 | tf_op jit(solution)/shard_map/ppermute | solution.py:239
  7.1 2.2 %shard_map.68 = (bf16[8,3,4,16,128]{4,3,2,1,0:T(8,128)(2,1)}, bf16[128,2048]{1,0:T(8,128)(2,1)}) custom-call(bf16[4,8,16,512]{3,2,1,0:T(8,128)(2,1)} %bitcast.11, bf16[4,8,16,512]{3,2,1,0:T(8,128)(2,1)} %bitcast.9, bf16[4,8,16,512]{3,2,1,0:T(8,128)(2,1)} %bitcast.10, bf16[512,2048]{1,0:T(8,128)(2,1)} %w_ref.2), custom_call_target="tpu_custom_call" | custom-call | flops 1 | bytes 1 | tf_op jit(solution)/shard_map/pallas_call | solution.py:25
  9.3 1.8 %collective-permute-start.6 = (bf16[128,2048]{1,0:T(8,128)(2,1)}, bf16[128,2048]{1,0:T(8,128)(2,1)S(1)}, u32[]{:S(2)}, u32[]{:S(2)}) collective-permute-start(bf16[128,2048]{1,0:T(8,128)(2,1)} %get-tuple-element.34.refs_0_), channel_id=1, source_target_pairs={{0,2},{1,3},{2,0},{3,1},{4,6},{5,7},{6,4},{7,5},{8,10},{9,11},{10,... | collective-permute-start | bytes 1572872 | tf_op jit(solution)/shard_map/ppermute | solution.py:239
  11.1 5.8 %all-to-all-start = ((bf16[8,192,128]{2,1,0:T(8,128)(2,1)}), bf16[8,192,128]{2,1,0:T(8,128)(2,1)S(1)}, u32[]{:S(2)}, u32[]{:S(2)}) async-start(bf16[8,192,128]{2,1,0:T(8,128)(2,1)} %bitcast.18), calls=%async_computation | async-start | bytes 786432 | tf_op jit(solution)/shard_map/all_to_all | solution.py:267
  17.1 2.1 %collective-permute-start.3 = (bf16[4,4,32,128]{3,2,1,0:T(8,128)(2,1)S(1)}, bf16[4,4,32,128]{3,2,1,0:T(8,128)(2,1)S(1)}, u32[]{:S(2)}, u32[]{:S(2)}) collective-permute-start(bf16[4,4,32,128]{3,2,1,0:T(8,128)(2,1)S(1)} %shard_map.65.refs_0_), channel_id=1, source_target_pairs={{0,4},{4,0},{8,12},{12,8},{16,20},{20,16},{24,28},{28,24},{1,5},{5... | collective-permute-start | bytes 393224 | tf_op jit(solution)/shard_map/ppermute | solution.py:239
  19.1 0.2 convert_reduce_fusion
  19.5 3.1 %shard_map.66 = (bf16[512,128]{1,0:T(8,128)(2,1)S(1)}, f32[2,512,128]{2,1,0:T(8,128)S(1)}, f32[2,512,128]{2,1,0:T(8,128)S(1)}, bf16[512,256]{1,0:T(8,128)(2,1)S(1)}, bf16[384,2048]{1,0:T(8,128)(2,1)S(1)}) custom-call(bf16[512,512]{1,0:T(8,128)(2,1)S(1)} %copy-done.2, bf16[512,512]{1,0:T(8,128)(2,1)S(1)} %copy-done, bf16[512,512]{1,0:T(8,128)(2,1)S(1)} %copy-done.1, ...), custom_call_target="tpu_custom_call" | custom-call | flops 1 | bytes 1 | tf_op jit(solution)/shard_map/pallas_call | solution.py:25
  22.6 1.8 %collective-permute-done.3.refs_1_ = bf16[4,4,32,128]{3,2,1,0:T(8,128)(2,1)S(1)} collective-permute-done((bf16[4,4,32,128]{3,2,1,0:T(8,128)(2,1)S(1)}, bf16[4,4,32,128]{3,2,1,0:T(8,128)(2,1)S(1)}, u32[]{:S(2)}, u32[]{:S(2)}) %collective-permute-start.3) | collective-permute-done | bytes 131104 | tf_op jit(solution)/shard_map/ppermute | solution.py:239
  24.4 2.4 %shard_map.71 = (bf16[128,2048]{1,0:T(8,128)(2,1)}, bf16[128,2048]{1,0:T(8,128)(2,1)S(1)}) custom-call(bf16[512,128]{1,0:T(8,128)(2,1)S(1)} %get-tuple-element.25.row_ref, f32[2,512,128]{2,1,0:T(8,128)S(1)} %get-tuple-element.26.sum_ref, f32[2,512,128]{2,1,0:T(8,128)S(1)} %get-tuple-element.27.stat_ref, bf16[512,256]{1,0:T(8,128)(2,1)S(1)} %get-tuple-element.28.q_ref, ...), custom_call_target="tpu_custom_call" | custom-call | flops 1 | bytes 1 | tf_op jit(solution)/shard_map/pallas_call | solution.py:25
  26.9 0.5 collective-permute-start.5
  27.4 2.4 %shard_map.67 = (bf16[128,2048]{1,0:T(8,128)(2,1)}, bf16[128,2048]{1,0:T(8,128)(2,1)S(1)}) custom-call(bf16[512,128]{1,0:T(8,128)(2,1)S(1)} %get-tuple-element.25.row_ref, f32[2,512,128]{2,1,0:T(8,128)S(1)} %get-tuple-element.26.sum_ref, f32[2,512,128]{2,1,0:T(8,128)S(1)} %get-tuple-element.27.stat_ref, bf16[512,256]{1,0:T(8,128)(2,1)S(1)} %get-tuple-element.28.q_ref, ...), custom_call_target="tpu_custom_call" | custom-call | flops 1 | bytes 1 | tf_op jit(solution)/shard_map/pallas_call | solution.py:25
  29.8 0.1 collective-permute-start.4
  29.9 0.4 collective-permute-start.7
  30.3 1.4 %shard_map.69 = bf16[8,64,128]{2,1,0:T(8,128)(2,1)} custom-call(bf16[8,3,64,128]{3,2,1,0:T(8,128)(2,1)S(1)} %bitcast.12), custom_call_target="tpu_custom_call" | custom-call | flops 1 | bytes 1 | tf_op jit(solution)/shard_map/pallas_call | solution.py:25
  31.8 4.4 %all-to-all-start.1 = ((bf16[32,16,128]{2,1,0:T(8,128)(2,1)}), bf16[32,16,128]{2,1,0:T(8,128)(2,1)S(1)}, u32[]{:S(2)}, u32[]{:S(2)}) async-start(bf16[32,16,128]{2,1,0:T(8,128)(2,1)} %bitcast.7), calls=%async_computation.1 | async-start | bytes 262144 | tf_op jit(solution)/shard_map/all_to_all | solution.py:314
  36.3 0.1 shard_map.72
  36.4 1.8 %collective-permute-start.9 = (bf16[128,2048]{1,0:T(8,128)(2,1)S(1)}, bf16[128,2048]{1,0:T(8,128)(2,1)S(1)}, u32[]{:S(2)}, u32[]{:S(2)}) collective-permute-start(bf16[128,2048]{1,0:T(8,128)(2,1)S(1)} %shard_map.72), channel_id=1, source_target_pairs={{0,2},{1,3},{2,0},{3,1},{4,6},{5,7},{6,4},{7,5},{8,10},{9,11},{10,... | collective-permute-start | bytes 1572872 | tf_op jit(solution)/shard_map/ppermute | solution.py:239
  38.2 6.3 %all-to-all-done.1 = bf16[32,16,128]{2,1,0:T(8,128)(2,1)S(1)} async-done(((bf16[32,16,128]{2,1,0:T(8,128)(2,1)}), bf16[32,16,128]{2,1,0:T(8,128)(2,1)S(1)}, u32[]{:S(2)}, u32[]{:S(2)}) %all-to-all-start.1) | async-done | bytes 131104 | tf_op jit(solution)/shard_map/all_to_all | solution.py:314
  44.6 1.0 %copy-done.6 = bf16[128,2048]{1,0:T(8,128)(2,1)S(1)} copy-done((bf16[128,2048]{1,0:T(8,128)(2,1)S(1)}, bf16[128,2048]{1,0:T(8,128)(2,1)}, u32[]{:S(2)}) %copy-start.6) | copy-done | bytes 524312
  45.6 2.1 %shard_map.70.near_ref = f32[128,2048]{1,0:T(8,128)S(1)} custom-call(bf16[128,2048]{1,0:T(8,128)(2,1)S(1)} %copy-done.6, bf16[128,2048]{1,0:T(8,128)(2,1)} %collective-permute-done.4.core_ref, bf16[8,4,16,128]{3,2,1,0:T(8,128)(2,1)S(1)} %bitcast.13, bf16[128,2048]{1,0:T(8,128)(2,1)S(1)} %copy-done.4, bf16[128,2048]{1,0:T(8,128)(2,1)} %collective-permute-done.5.refs_1_, ...), custom_call_target="tpu_custom_call" | custom-call | flops 10000000000 | bytes 1 | tf_op jit(solution)/shard_map/pallas_call | solution.py:25
  47.7 4.2 %collective-permute-done.9.far_ref = bf16[128,2048]{1,0:T(8,128)(2,1)S(1)} collective-permute-done((bf16[128,2048]{1,0:T(8,128)(2,1)S(1)}, bf16[128,2048]{1,0:T(8,128)(2,1)S(1)}, u32[]{:S(2)}, u32[]{:S(2)}) %collective-permute-start.9) | collective-permute-done | bytes 524320 | tf_op jit(solution)/shard_map/ppermute | solution.py:239
  51.9 1.1 %shard_map.73 = bf16[128,2048]{1,0:T(8,128)(2,1)} custom-call(f32[128,2048]{1,0:T(8,128)S(1)} %shard_map.70.near_ref, bf16[128,2048]{1,0:T(8,128)(2,1)S(1)} %collective-permute-done.9.far_ref), custom_call_target="tpu_custom_call" | custom-call | flops 1 | bytes 1 | tf_op jit(solution)/shard_map/pallas_call | solution.py:25
  (33 shorter events, 0.3 us)
Async XLA Ops:
  1.4 15.6 %collective-permute-start = (bf16[1,4,32,128]{3,2,1,0:T(8,128)(2,1)}, bf16[1,4,32,128]{3,2,1,0:T(8,128)(2,1)S(1)}, u32[]{:S(2)}, u32[]{:S(2)}) collective-permute-start(bf16[1,4,32,128]{3,2,1,0:T(8,128)(2,1)} %bitcast.14), channel_id=1, source_target_pairs={{0,8},{4,12},{8,0},{12,4},{16,24},{20,28},{24,16},{28,20},{1,9},{5... | collective-permute-start | bytes 98312 | tf_op jit(solution)/shard_map/ppermute | solution.py:239
  4.5 12.5 %collective-permute-start.1 = (bf16[1,4,32,128]{3,2,1,0:T(8,128)(2,1)}, bf16[1,4,32,128]{3,2,1,0:T(8,128)(2,1)S(1)}, u32[]{:S(2)}, u32[]{:S(2)}) collective-permute-start(bf16[1,4,32,128]{3,2,1,0:T(8,128)(2,1)} %bitcast.15), channel_id=1, source_target_pairs={{0,16},{4,20},{8,24},{12,28},{16,0},{20,4},{24,8},{28,12},{1,17},{... | collective-permute-start | bytes 98312 | tf_op jit(solution)/shard_map/ppermute | solution.py:239
  7.1 9.9 %collective-permute-start.2 = (bf16[1,4,32,128]{3,2,1,0:T(8,128)(2,1)}, bf16[1,4,32,128]{3,2,1,0:T(8,128)(2,1)S(1)}, u32[]{:S(2)}, u32[]{:S(2)}) collective-permute-start(bf16[1,4,32,128]{3,2,1,0:T(8,128)(2,1)} %bitcast.16), channel_id=1, source_target_pairs={{0,24},{4,28},{8,16},{12,20},{16,8},{20,12},{24,0},{28,4},{1,25},{... | collective-permute-start | bytes 98312 | tf_op jit(solution)/shard_map/ppermute | solution.py:239
  7.1 9.8 %copy-start.8 = (s32[8]{0:T(128)S(1)}, s32[8]{0:T(128)}, u32[]{:S(2)}) copy-start(s32[8]{0:T(128)} %constant.10.clone) | copy-start | bytes 100
  7.1 9.9 %copy-start.3 = (bf16[4,32,128]{2,1,0:T(8,128)(2,1)S(1)}, bf16[4,32,128]{2,1,0:T(8,128)(2,1)}, u32[]{:S(2)}) copy-start(bf16[4,32,128]{2,1,0:T(8,128)(2,1)} %shard_map.64) | copy-start | bytes 98308
  9.3 20.6 %collective-permute-start.6 = (bf16[128,2048]{1,0:T(8,128)(2,1)}, bf16[128,2048]{1,0:T(8,128)(2,1)S(1)}, u32[]{:S(2)}, u32[]{:S(2)}) collective-permute-start(bf16[128,2048]{1,0:T(8,128)(2,1)} %get-tuple-element.34.refs_0_), channel_id=1, source_target_pairs={{0,2},{1,3},{2,0},{3,1},{4,6},{5,7},{6,4},{7,5},{8,10},{9,11},{10,... | collective-permute-start | bytes 1572872 | tf_op jit(solution)/shard_map/ppermute | solution.py:239
  11.1 19.2 %all-to-all-start = ((bf16[8,192,128]{2,1,0:T(8,128)(2,1)}), bf16[8,192,128]{2,1,0:T(8,128)(2,1)S(1)}, u32[]{:S(2)}, u32[]{:S(2)}) async-start(bf16[8,192,128]{2,1,0:T(8,128)(2,1)} %bitcast.18), calls=%async_computation | async-start | bytes 786432 | tf_op jit(solution)/shard_map/all_to_all | solution.py:267
  16.9 2.2 %copy-start.7 = (s32[1,2,16]{2,1,0:T(2,128)S(1)}, s32[1,2,16]{2,1,0:T(2,128)}, u32[]{:S(2)}) copy-start(s32[1,2,16]{2,1,0:T(2,128)} %param.9) | copy-start | bytes 388
  17.0 2.5 %copy-start = (bf16[512,512]{1,0:T(8,128)(2,1)S(1)}, bf16[512,512]{1,0:T(8,128)(2,1)}, u32[]{:S(2)}) copy-start(bf16[512,512]{1,0:T(8,128)(2,1)} %k_ref.2) | copy-start | bytes 1572868
  17.0 2.5 %copy-start.1 = (bf16[512,512]{1,0:T(8,128)(2,1)S(1)}, bf16[512,512]{1,0:T(8,128)(2,1)}, u32[]{:S(2)}) copy-start(bf16[512,512]{1,0:T(8,128)(2,1)} %v_ref.2) | copy-start | bytes 1572868
  17.0 2.5 %copy-start.2 = (bf16[512,512]{1,0:T(8,128)(2,1)S(1)}, bf16[512,512]{1,0:T(8,128)(2,1)}, u32[]{:S(2)}) copy-start(bf16[512,512]{1,0:T(8,128)(2,1)} %q_ref) | copy-start | bytes 1572868
  17.1 7.3 %collective-permute-start.3 = (bf16[4,4,32,128]{3,2,1,0:T(8,128)(2,1)S(1)}, bf16[4,4,32,128]{3,2,1,0:T(8,128)(2,1)S(1)}, u32[]{:S(2)}, u32[]{:S(2)}) collective-permute-start(bf16[4,4,32,128]{3,2,1,0:T(8,128)(2,1)S(1)} %shard_map.65.refs_0_), channel_id=1, source_target_pairs={{0,4},{4,0},{8,12},{12,8},{16,20},{20,16},{24,28},{28,24},{1,5},{5... | collective-permute-start | bytes 393224 | tf_op jit(solution)/shard_map/ppermute | solution.py:239
  22.6 4.3 %copy-start.4 = (bf16[128,2048]{1,0:T(8,128)(2,1)S(1)}, bf16[128,2048]{1,0:T(8,128)(2,1)}, u32[]{:S(2)}) copy-start(bf16[128,2048]{1,0:T(8,128)(2,1)} %get-tuple-element.34.refs_0_) | copy-start | bytes 1572868
  26.8 9.5 %collective-permute-start.8 = (bf16[128,2048]{1,0:T(8,128)(2,1)}, bf16[128,2048]{1,0:T(8,128)(2,1)S(1)}, u32[]{:S(2)}, u32[]{:S(2)}) collective-permute-start(bf16[128,2048]{1,0:T(8,128)(2,1)} %get-tuple-element.36), channel_id=1, source_target_pairs={{0,1},{1,0},{2,3},{3,2},{4,5},{5,4},{6,7},{7,6},{8,9},{9,8},{10,11... | collective-permute-start | bytes 1572872 | tf_op jit(solution)/shard_map/ppermute | solution.py:239
  26.9 11.4 %collective-permute-start.5 = (bf16[128,2048]{1,0:T(8,128)(2,1)S(1)}, bf16[128,2048]{1,0:T(8,128)(2,1)}, u32[]{:S(2)}, u32[]{:S(2)}) collective-permute-start(bf16[128,2048]{1,0:T(8,128)(2,1)S(1)} %copy-done.4), channel_id=1, source_target_pairs={{0,1},{1,0},{2,3},{3,2},{4,5},{5,4},{6,7},{7,6},{8,9},{9,8},{10,11... | collective-permute-start | bytes 1572872 | tf_op jit(solution)/shard_map/ppermute | solution.py:239
  29.8 6.5 %copy-start.5 = (bf16[128,2048]{1,0:T(8,128)(2,1)}, bf16[128,2048]{1,0:T(8,128)(2,1)S(1)}, u32[]{:S(2)}) copy-start(bf16[128,2048]{1,0:T(8,128)(2,1)S(1)} %get-tuple-element.31.own_ref) | copy-start | bytes 1572868
  29.8 8.5 %collective-permute-start.4 = (bf16[128,2048]{1,0:T(8,128)(2,1)}, bf16[128,2048]{1,0:T(8,128)(2,1)}, u32[]{:S(2)}, u32[]{:S(2)}) collective-permute-start(bf16[128,2048]{1,0:T(8,128)(2,1)} %get-tuple-element.32), channel_id=1, source_target_pairs={{0,1},{1,0},{2,3},{3,2},{4,5},{5,4},{6,7},{7,6},{8,9},{9,8},{10,11... | collective-permute-start | bytes 1572872 | tf_op jit(solution)/shard_map/ppermute | solution.py:239
  29.9 14.7 %collective-permute-start.7 = (bf16[128,2048]{1,0:T(8,128)(2,1)S(1)}, bf16[128,2048]{1,0:T(8,128)(2,1)}, u32[]{:S(2)}, u32[]{:S(2)}) collective-permute-start(bf16[128,2048]{1,0:T(8,128)(2,1)S(1)} %collective-permute-done.6.refs_2_), channel_id=1, source_target_pairs={{0,1},{1,0},{2,3},{3,2},{4,5},{5,4},{6,7},{7,6},{8,9},{9,8},{10,11... | collective-permute-start | bytes 1572872 | tf_op jit(solution)/shard_map/ppermute | solution.py:239
  31.8 12.8 %all-to-all-start.1 = ((bf16[32,16,128]{2,1,0:T(8,128)(2,1)}), bf16[32,16,128]{2,1,0:T(8,128)(2,1)S(1)}, u32[]{:S(2)}, u32[]{:S(2)}) async-start(bf16[32,16,128]{2,1,0:T(8,128)(2,1)} %bitcast.7), calls=%async_computation.1 | async-start | bytes 262144 | tf_op jit(solution)/shard_map/all_to_all | solution.py:314
  36.4 15.5 %collective-permute-start.9 = (bf16[128,2048]{1,0:T(8,128)(2,1)S(1)}, bf16[128,2048]{1,0:T(8,128)(2,1)S(1)}, u32[]{:S(2)}, u32[]{:S(2)}) collective-permute-start(bf16[128,2048]{1,0:T(8,128)(2,1)S(1)} %shard_map.72), channel_id=1, source_target_pairs={{0,2},{1,3},{2,0},{3,1},{4,6},{5,7},{6,4},{7,5},{8,10},{9,11},{10,... | collective-permute-start | bytes 1572872 | tf_op jit(solution)/shard_map/ppermute | solution.py:239
  44.6 1.0 %copy-start.6 = (bf16[128,2048]{1,0:T(8,128)(2,1)S(1)}, bf16[128,2048]{1,0:T(8,128)(2,1)}, u32[]{:S(2)}) copy-start(bf16[128,2048]{1,0:T(8,128)(2,1)} %copy-done.5) | copy-start | bytes 1572868

commit v3 on v2

--- a/solution.py
+++ b/solution.py
@@ -11,8 +11,9 @@
 HEAD_DIM = 128
 SUMMARY = 32
 NEG = -1e30
-JOIN_COST = 10**10
-LAST_COST = 10**10
+JOIN_COST = 10**9
+COLUMN_COST = 10**9*3
+LAST_COST = 1
 OWN_ROOM = 48
 BF16 = jnp.bfloat16
 F32 = jnp.float32
@@ -211,15 +212,14 @@
 
 
 def near_kernel(own_ref, core_ref, moved_ref, *refs):
-    ws, (out_ref, sums, moved, w_all, sems) = refs[:-5], refs[-5:]
-    pairs = [(moved_ref, moved)] + [(w, w_all.at[i]) for i, w in enumerate(ws)]
-    pairs += [(ref, sums.at[i]) for i, ref in enumerate((own_ref, core_ref))]
-    wait(start(sems, pairs))
+    ws, (out_ref, moved, sems) = refs[:-3], refs[-3:]
+    wait(start(sems, [(moved_ref, moved)]))
     outer, heads, inner, depth = moved.shape
     me = lax.axis_index("head")
-    found = jnp.concatenate([moved[:, me ^ i].reshape(outer * inner, depth) for i in range(heads)], axis=1)
-    total = dot(found, w_all[...].reshape(heads * depth, w_all.shape[2]))
-    out_ref[...] = total + sums[0].astype(F32) + sums[1].astype(F32)
+    total = own_ref[...].astype(F32) + core_ref[...].astype(F32)
+    for i, w in enumerate(ws):
+        total += dot(moved[:, me ^ i].reshape(outer * inner, depth), w[...])
+    out_ref[...] = total
 
 
 def last_kernel(near_ref, far_ref, out_ref, near, far, done, sems):
@@ -271,6 +271,10 @@
     if columns % 16:
         moved = moved.transpose(1, 0, 2, 3).reshape(1, 3, block, HEAD_DIM)
 
+    held = [queries, keys, values, out_weight, w_col]
+    if len(tails) > 1:
+        *held, tails[0] = lax.optimization_barrier((*held, tails[0]))
+    w_col = held[4]
     w_far = swap(w_col, "head", 2, parts)
     w_core = swap(w_col, "head", 1, parts)
     w_both = swap(w_far, "head", 1, parts)
@@ -280,10 +284,7 @@
     mult = jnp.repeat(jnp.sum(names.astype(F32), axis=1), SUMMARY, axis=1)
 
     shape = (block // parts, out_weight.shape[1])
-    held = [queries, keys, values, out_weight]
-    if len(tails) > 1:
-        *held, tails[0] = lax.optimization_barrier((*held, tails[0]))
-    own = own_part(*held)
+    own = own_part(*held[:4])
 
     column_shape = (moved.shape[0], moved.shape[2], HEAD_DIM)
     (column_out,) = call(
@@ -292,6 +293,7 @@
         [(HBM, moved)],
         [pltpu.VMEM((3, *column_shape), BF16), pltpu.VMEM(column_shape, BF16)],
         3,
+        COLUMN_COST,
     )
 
     def partial_sums(flips):
@@ -318,13 +320,8 @@
     (near_sum,) = call(
         near_kernel,
         [(VMEM, shape, F32)],
-        [(HBM, x) for x in (own_sum, core_in, back, w_col, w_core, w_far, w_both)],
-        [
-            pltpu.VMEM((2, *shape), BF16),
-            pltpu.VMEM(back.shape, BF16),
-            pltpu.VMEM((parts, HEAD_DIM, shape[1]), BF16),
-        ],
-        3 + parts,
+        [(VMEM, own_sum), (VMEM, core_in), (HBM, back)] + [(VMEM, x) for x in (w_col, w_core, w_far, w_both)],
+        [pltpu.VMEM(back.shape, BF16)],
         cost=LAST_COST,
     )
     (mixed,) = call(

time: 53.3 us -> 50.1 us (0.940)
  starting transfers between devices: 22.8 us -> 21.4 us
  waiting for transfers between devices: 12.3 us -> 11 us
    ppermute x10, waiting for transfers between devices: 5.95 us -> 1.87 us  [swap(): return lax.ppermute(x, axis, [(i, i ^ flip) for i in range(count)])]
    all_to_all x1, waiting for transfers between devices: 6.33 us -> 9.18 us  [per_device(): lax.all_to_all(column_out, ('seq', 'head'), split_axis=0, concat_axis=0,...]
    ppermute x10, starting transfers between devices: 12.5 us -> 11.6 us  [swap(): return lax.ppermute(x, axis, [(i, i ^ flip) for i in range(count)])]
    all_to_all x1, starting transfers between devices: 4.44 us -> 3.63 us  [per_device(): lax.all_to_all(column_out, ('seq', 'head'), split_axis=0, concat_axis=0,...]
    unnamed x18 -> x16, local copies, waits for them, and re-layouts: 1.08 us -> 0.68 us
where the time goes in v3:
time: 50.1 us; the launch traced here: 49.8 us
  starting transfers between devices  21.4 us (43%)
  Pallas kernels  16.1 us (32%)
  waiting for transfers between devices  11 us (22%)
  local copies, waits for them, and re-layouts  0.84 us (2%)
    pallas_call x10, Pallas kernels, call(): pl.pallas_call(kernel, out_shape=[jax.ShapeDtypeStruct(x[1], x[2] if len(...  16.1 us
    ppermute x10, starting transfers between devices, swap(): return lax.ppermute(x, axis, [(i, i ^ flip) for i in range(count)])  11.6 us
    all_to_all x1, waiting for transfers between devices, per_device(): lax.all_to_all(column_out, ('seq', 'head'), split_axis=0, concat_axis=0,...  9.18 us
    all_to_all x1, starting transfers between devices, per_device(): lax.all_to_all(packed.reshape(count, 3 * columns, HEAD_DIM), 'seq', split...  6.17 us
    all_to_all x1, starting transfers between devices, per_device(): lax.all_to_all(column_out, ('seq', 'head'), split_axis=0, concat_axis=0,...  3.63 us
    ppermute x10, waiting for transfers between devices, swap(): return lax.ppermute(x, axis, [(i, i ^ flip) for i in range(count)])  1.87 us
  transfers between devices with their start and end apart: 12, of which 3 were waited for; matrix products, arithmetic and copies ran while one was open for 1% of the time, Pallas kernels for 26%

profile of v3, /device:TPU:0, one launch (start us, length us, event | category | flops | bytes accessed | tf_op | source)
XLA Modules:
  0.0 49.8 jit_solution(9670302581597844099)
XLA Ops:
  0.0 1.4 %shard_map.65 = bf16[4,32,128]{2,1,0:T(8,128)(2,1)} custom-call(bf16[512,512]{1,0:T(8,128)(2,1)} %k_ref.2, bf16[512,512]{1,0:T(8,128)(2,1)} %v_ref.2), custom_call_target="tpu_custom_call" | custom-call | flops 1 | bytes 1 | tf_op jit(solution)/shard_map/pallas_call | solution.py:26
  1.4 3.1 %collective-permute-start = (bf16[1,4,32,128]{3,2,1,0:T(8,128)(2,1)}, bf16[1,4,32,128]{3,2,1,0:T(8,128)(2,1)S(1)}, u32[]{:S(2)}, u32[]{:S(2)}) collective-permute-start(bf16[1,4,32,128]{3,2,1,0:T(8,128)(2,1)} %bitcast.15), channel_id=1, source_target_pairs={{0,8},{4,12},{8,0},{12,4},{16,24},{20,28},{24,16},{28,20},{1,9},{5... | collective-permute-start | bytes 98312 | tf_op jit(solution)/shard_map/ppermute | solution.py:239
  4.5 2.6 %collective-permute-start.1 = (bf16[1,4,32,128]{3,2,1,0:T(8,128)(2,1)}, bf16[1,4,32,128]{3,2,1,0:T(8,128)(2,1)S(1)}, u32[]{:S(2)}, u32[]{:S(2)}) collective-permute-start(bf16[1,4,32,128]{3,2,1,0:T(8,128)(2,1)} %bitcast.16), channel_id=1, source_target_pairs={{0,16},{4,20},{8,24},{12,28},{16,0},{20,4},{24,8},{28,12},{1,17},{... | collective-permute-start | bytes 98312 | tf_op jit(solution)/shard_map/ppermute | solution.py:239
  7.1 2.2 %shard_map.64 = (bf16[8,3,4,16,128]{4,3,2,1,0:T(8,128)(2,1)}, bf16[128,2048]{1,0:T(8,128)(2,1)}) custom-call(bf16[4,8,16,512]{3,2,1,0:T(8,128)(2,1)} %bitcast.11, bf16[4,8,16,512]{3,2,1,0:T(8,128)(2,1)} %bitcast.9, bf16[4,8,16,512]{3,2,1,0:T(8,128)(2,1)} %bitcast.10, bf16[512,2048]{1,0:T(8,128)(2,1)} %w_ref.2), custom_call_target="tpu_custom_call" | custom-call | flops 1 | bytes 1 | tf_op jit(solution)/shard_map/pallas_call | solution.py:26
  9.3 6.2 %all-to-all-start = ((bf16[8,192,128]{2,1,0:T(8,128)(2,1)}), bf16[8,192,128]{2,1,0:T(8,128)(2,1)S(1)}, u32[]{:S(2)}, u32[]{:S(2)}) async-start(bf16[8,192,128]{2,1,0:T(8,128)(2,1)} %bitcast.19), calls=%async_computation | async-start | bytes 786432 | tf_op jit(solution)/shard_map/all_to_all | solution.py:267
  15.6 2.1 %collective-permute-start.3 = (bf16[4,4,32,128]{3,2,1,0:T(8,128)(2,1)S(1)}, bf16[4,4,32,128]{3,2,1,0:T(8,128)(2,1)S(1)}, u32[]{:S(2)}, u32[]{:S(2)}) collective-permute-start(bf16[4,4,32,128]{3,2,1,0:T(8,128)(2,1)S(1)} %shard_map.66.refs_0_), channel_id=1, source_target_pairs={{0,4},{4,0},{8,12},{12,8},{16,20},{20,16},{24,28},{28,24},{1,5},{5... | collective-permute-start | bytes 393224 | tf_op jit(solution)/shard_map/ppermute | solution.py:239
  17.7 0.2 convert_reduce_fusion
  17.9 0.1 reshape.30.mult_ref
  18.0 1.5 %collective-permute-start.6 = (bf16[128,2048]{1,0:T(8,128)(2,1)S(1)}, bf16[128,2048]{1,0:T(8,128)(2,1)S(1)}, u32[]{:S(2)}, u32[]{:S(2)}) collective-permute-start(bf16[128,2048]{1,0:T(8,128)(2,1)S(1)} %copy-done.3), channel_id=1, source_target_pairs={{0,2},{1,3},{2,0},{3,1},{4,6},{5,7},{6,4},{7,5},{8,10},{9,11},{10,... | collective-permute-start | bytes 1572872 | tf_op jit(solution)/shard_map/ppermute | solution.py:239
  19.5 3.1 %shard_map.67 = (bf16[512,128]{1,0:T(8,128)(2,1)S(1)}, f32[2,512,128]{2,1,0:T(8,128)S(1)}, f32[2,512,128]{2,1,0:T(8,128)S(1)}, bf16[512,256]{1,0:T(8,128)(2,1)S(1)}, bf16[384,2048]{1,0:T(8,128)(2,1)S(1)}) custom-call(bf16[512,512]{1,0:T(8,128)(2,1)S(1)} %copy-done.2, bf16[512,512]{1,0:T(8,128)(2,1)S(1)} %copy-done, bf16[512,512]{1,0:T(8,128)(2,1)S(1)} %copy-done.1, ...), custom_call_target="tpu_custom_call" | custom-call | flops 1 | bytes 1 | tf_op jit(solution)/shard_map/pallas_call | solution.py:26
  22.7 0.6 %collective-permute-done.3.refs_1_ = bf16[4,4,32,128]{3,2,1,0:T(8,128)(2,1)S(1)} collective-permute-done((bf16[4,4,32,128]{3,2,1,0:T(8,128)(2,1)S(1)}, bf16[4,4,32,128]{3,2,1,0:T(8,128)(2,1)S(1)}, u32[]{:S(2)}, u32[]{:S(2)}) %collective-permute-start.3) | collective-permute-done | bytes 131104 | tf_op jit(solution)/shard_map/ppermute | solution.py:239
  23.3 2.4 %shard_map.71 = (bf16[128,2048]{1,0:T(8,128)(2,1)S(1)}, bf16[128,2048]{1,0:T(8,128)(2,1)S(1)}) custom-call(bf16[512,128]{1,0:T(8,128)(2,1)S(1)} %get-tuple-element.27.row_ref, f32[2,512,128]{2,1,0:T(8,128)S(1)} %get-tuple-element.28.sum_ref, f32[2,512,128]{2,1,0:T(8,128)S(1)} %get-tuple-element.29.stat_ref, bf16[512,256]{1,0:T(8,128)(2,1)S(1)} %get-tuple-element.30.q_ref, ...), custom_call_target="tpu_custom_call" | custom-call | flops 1 | bytes 1 | tf_op jit(solution)/shard_map/pallas_call | solution.py:26
  25.7 0.5 collective-permute-start.5
  26.2 2.4 %shard_map.68 = (bf16[128,2048]{1,0:T(8,128)(2,1)}, bf16[128,2048]{1,0:T(8,128)(2,1)S(1)}) custom-call(bf16[512,128]{1,0:T(8,128)(2,1)S(1)} %get-tuple-element.27.row_ref, f32[2,512,128]{2,1,0:T(8,128)S(1)} %get-tuple-element.28.sum_ref, f32[2,512,128]{2,1,0:T(8,128)S(1)} %get-tuple-element.29.stat_ref, bf16[512,256]{1,0:T(8,128)(2,1)S(1)} %get-tuple-element.30.q_ref, ...), custom_call_target="tpu_custom_call" | custom-call | flops 1 | bytes 1 | tf_op jit(solution)/shard_map/pallas_call | solution.py:26
  28.6 0.1 collective-permute-start.4
  28.8 1.2 %collective-permute-done.6.refs_2_ = bf16[128,2048]{1,0:T(8,128)(2,1)S(1)} collective-permute-done((bf16[128,2048]{1,0:T(8,128)(2,1)S(1)}, bf16[128,2048]{1,0:T(8,128)(2,1)S(1)}, u32[]{:S(2)}, u32[]{:S(2)}) %collective-permute-start.6) | collective-permute-done | bytes 524320 | tf_op jit(solution)/shard_map/ppermute | solution.py:239
  30.0 0.9 %shard_map.72 = bf16[128,2048]{1,0:T(8,128)(2,1)} custom-call(bf16[128,2048]{1,0:T(8,128)(2,1)S(1)} %get-tuple-element.37.a_ref, bf16[128,2048]{1,0:T(8,128)(2,1)S(1)} %collective-permute-done.8.b_ref), custom_call_target="tpu_custom_call" | custom-call | flops 1 | bytes 1 | tf_op jit(solution)/shard_map/pallas_call | solution.py:26
  30.9 1.6 %collective-permute-start.9 = (bf16[128,2048]{1,0:T(8,128)(2,1)}, bf16[128,2048]{1,0:T(8,128)(2,1)}, u32[]{:S(2)}, u32[]{:S(2)}) collective-permute-start(bf16[128,2048]{1,0:T(8,128)(2,1)} %shard_map.72), channel_id=1, source_target_pairs={{0,2},{1,3},{2,0},{3,1},{4,6},{5,7},{6,4},{7,5},{8,10},{9,11},{10,... | collective-permute-start | bytes 1572872 | tf_op jit(solution)/shard_map/ppermute | solution.py:239
  32.5 0.9 %shard_map.69 = bf16[8,64,128]{2,1,0:T(8,128)(2,1)S(1)} custom-call(bf16[8,3,64,128]{3,2,1,0:T(8,128)(2,1)S(1)} %bitcast.13), custom_call_target="tpu_custom_call" | custom-call | flops 3000000000 | bytes 1 | tf_op jit(solution)/shard_map/pallas_call | solution.py:26
  33.5 0.6 %copy-done.4 = bf16[8,64,128]{2,1,0:T(8,128)(2,1)} copy-done((bf16[8,64,128]{2,1,0:T(8,128)(2,1)}, bf16[8,64,128]{2,1,0:T(8,128)(2,1)S(1)}, u32[]{:S(2)}) %copy-start.4) | copy-done | bytes 131096
  34.1 3.6 %all-to-all-start.1 = ((bf16[32,16,128]{2,1,0:T(8,128)(2,1)}), bf16[32,16,128]{2,1,0:T(8,128)(2,1)S(1)}, u32[]{:S(2)}, u32[]{:S(2)}) async-start(bf16[32,16,128]{2,1,0:T(8,128)(2,1)} %bitcast.14), calls=%async_computation.1 | async-start | bytes 262144 | tf_op jit(solution)/shard_map/all_to_all | solution.py:316
  37.8 9.2 %all-to-all-done.1 = bf16[32,16,128]{2,1,0:T(8,128)(2,1)S(1)} async-done(((bf16[32,16,128]{2,1,0:T(8,128)(2,1)}), bf16[32,16,128]{2,1,0:T(8,128)(2,1)S(1)}, u32[]{:S(2)}, u32[]{:S(2)}) %all-to-all-start.1) | async-done | bytes 131104 | tf_op jit(solution)/shard_map/all_to_all | solution.py:316
  47.0 0.9 %shard_map.70.near_ref = f32[128,2048]{1,0:T(8,128)S(1)} custom-call(bf16[128,2048]{1,0:T(8,128)(2,1)S(1)} %get-tuple-element.33.own_ref, bf16[128,2048]{1,0:T(8,128)(2,1)S(1)} %collective-permute-done.4.core_ref, bf16[8,4,16,128]{3,2,1,0:T(8,128)(2,1)S(1)} %bitcast.12, bf16[128,2048]{1,0:T(8,128)(2,1)S(1)} %copy-done.3, ...), custom_call_target="tpu_custom_call" | custom-call | flops 1 | bytes 1 | tf_op jit(solution)/shard_map/pallas_call | solution.py:26
  47.9 1.9 %shard_map.73 = bf16[128,2048]{1,0:T(8,128)(2,1)} custom-call(f32[128,2048]{1,0:T(8,128)S(1)} %shard_map.70.near_ref, bf16[128,2048]{1,0:T(8,128)(2,1)} %collective-permute-done.9.far_ref), custom_call_target="tpu_custom_call" | custom-call | flops 1 | bytes 1 | tf_op jit(solution)/shard_map/pallas_call | solution.py:26
  (31 shorter events, 0.2 us)
Async XLA Ops:
  1.4 14.2 %collective-permute-start = (bf16[1,4,32,128]{3,2,1,0:T(8,128)(2,1)}, bf16[1,4,32,128]{3,2,1,0:T(8,128)(2,1)S(1)}, u32[]{:S(2)}, u32[]{:S(2)}) collective-permute-start(bf16[1,4,32,128]{3,2,1,0:T(8,128)(2,1)} %bitcast.15), channel_id=1, source_target_pairs={{0,8},{4,12},{8,0},{12,4},{16,24},{20,28},{24,16},{28,20},{1,9},{5... | collective-permute-start | bytes 98312 | tf_op jit(solution)/shard_map/ppermute | solution.py:239
  4.5 11.1 %collective-permute-start.1 = (bf16[1,4,32,128]{3,2,1,0:T(8,128)(2,1)}, bf16[1,4,32,128]{3,2,1,0:T(8,128)(2,1)S(1)}, u32[]{:S(2)}, u32[]{:S(2)}) collective-permute-start(bf16[1,4,32,128]{3,2,1,0:T(8,128)(2,1)} %bitcast.16), channel_id=1, source_target_pairs={{0,16},{4,20},{8,24},{12,28},{16,0},{20,4},{24,8},{28,12},{1,17},{... | collective-permute-start | bytes 98312 | tf_op jit(solution)/shard_map/ppermute | solution.py:239
  7.1 8.5 %collective-permute-start.2 = (bf16[1,4,32,128]{3,2,1,0:T(8,128)(2,1)}, bf16[1,4,32,128]{3,2,1,0:T(8,128)(2,1)S(1)}, u32[]{:S(2)}, u32[]{:S(2)}) collective-permute-start(bf16[1,4,32,128]{3,2,1,0:T(8,128)(2,1)} %bitcast.17), channel_id=1, source_target_pairs={{0,24},{4,28},{8,16},{12,20},{16,8},{20,12},{24,0},{28,4},{1,25},{... | collective-permute-start | bytes 98312 | tf_op jit(solution)/shard_map/ppermute | solution.py:239
  7.1 8.5 %copy-start.7 = (s32[8]{0:T(128)S(1)}, s32[8]{0:T(128)}, u32[]{:S(2)}) copy-start(s32[8]{0:T(128)} %constant.10.clone) | copy-start | bytes 100
  7.1 8.5 %copy-start.5 = (bf16[4,32,128]{2,1,0:T(8,128)(2,1)S(1)}, bf16[4,32,128]{2,1,0:T(8,128)(2,1)}, u32[]{:S(2)}) copy-start(bf16[4,32,128]{2,1,0:T(8,128)(2,1)} %shard_map.65) | copy-start | bytes 98308
  9.3 8.4 %copy-start.6 = (s32[1,2,16]{2,1,0:T(2,128)S(1)}, s32[1,2,16]{2,1,0:T(2,128)}, u32[]{:S(2)}) copy-start(s32[1,2,16]{2,1,0:T(2,128)} %param.9) | copy-start | bytes 388
  9.3 8.7 %copy-start.3 = (bf16[128,2048]{1,0:T(8,128)(2,1)S(1)}, bf16[128,2048]{1,0:T(8,128)(2,1)}, u32[]{:S(2)}) copy-start(bf16[128,2048]{1,0:T(8,128)(2,1)} %get-tuple-element.36.refs_0_) | copy-start | bytes 1572868
  9.3 10.2 %copy-start = (bf16[512,512]{1,0:T(8,128)(2,1)S(1)}, bf16[512,512]{1,0:T(8,128)(2,1)}, u32[]{:S(2)}) copy-start(bf16[512,512]{1,0:T(8,128)(2,1)} %k_ref.2) | copy-start | bytes 1572868
  9.3 10.2 %copy-start.1 = (bf16[512,512]{1,0:T(8,128)(2,1)S(1)}, bf16[512,512]{1,0:T(8,128)(2,1)}, u32[]{:S(2)}) copy-start(bf16[512,512]{1,0:T(8,128)(2,1)} %v_ref.2) | copy-start | bytes 1572868
  9.3 10.2 %copy-start.2 = (bf16[512,512]{1,0:T(8,128)(2,1)S(1)}, bf16[512,512]{1,0:T(8,128)(2,1)}, u32[]{:S(2)}) copy-start(bf16[512,512]{1,0:T(8,128)(2,1)} %q_ref) | copy-start | bytes 1572868
  9.3 23.2 %all-to-all-start = ((bf16[8,192,128]{2,1,0:T(8,128)(2,1)}), bf16[8,192,128]{2,1,0:T(8,128)(2,1)S(1)}, u32[]{:S(2)}, u32[]{:S(2)}) async-start(bf16[8,192,128]{2,1,0:T(8,128)(2,1)} %bitcast.19), calls=%async_computation | async-start | bytes 786432 | tf_op jit(solution)/shard_map/all_to_all | solution.py:267
  15.6 7.7 %collective-permute-start.3 = (bf16[4,4,32,128]{3,2,1,0:T(8,128)(2,1)S(1)}, bf16[4,4,32,128]{3,2,1,0:T(8,128)(2,1)S(1)}, u32[]{:S(2)}, u32[]{:S(2)}) collective-permute-start(bf16[4,4,32,128]{3,2,1,0:T(8,128)(2,1)S(1)} %shard_map.66.refs_0_), channel_id=1, source_target_pairs={{0,4},{4,0},{8,12},{12,8},{16,20},{20,16},{24,28},{28,24},{1,5},{5... | collective-permute-start | bytes 393224 | tf_op jit(solution)/shard_map/ppermute | solution.py:239
  18.0 12.0 %collective-permute-start.6 = (bf16[128,2048]{1,0:T(8,128)(2,1)S(1)}, bf16[128,2048]{1,0:T(8,128)(2,1)S(1)}, u32[]{:S(2)}, u32[]{:S(2)}) collective-permute-start(bf16[128,2048]{1,0:T(8,128)(2,1)S(1)} %copy-done.3), channel_id=1, source_target_pairs={{0,2},{1,3},{2,0},{3,1},{4,6},{5,7},{6,4},{7,5},{8,10},{9,11},{10,... | collective-permute-start | bytes 1572872 | tf_op jit(solution)/shard_map/ppermute | solution.py:239
  25.7 4.3 %collective-permute-start.8 = (bf16[128,2048]{1,0:T(8,128)(2,1)S(1)}, bf16[128,2048]{1,0:T(8,128)(2,1)S(1)}, u32[]{:S(2)}, u32[]{:S(2)}) collective-permute-start(bf16[128,2048]{1,0:T(8,128)(2,1)S(1)} %get-tuple-element.38), channel_id=1, source_target_pairs={{0,1},{1,0},{2,3},{3,2},{4,5},{5,4},{6,7},{7,6},{8,9},{9,8},{10,11... | collective-permute-start | bytes 1572872 | tf_op jit(solution)/shard_map/ppermute | solution.py:239
  25.7 12.0 %collective-permute-start.5 = (bf16[128,2048]{1,0:T(8,128)(2,1)S(1)}, bf16[128,2048]{1,0:T(8,128)(2,1)S(1)}, u32[]{:S(2)}, u32[]{:S(2)}) collective-permute-start(bf16[128,2048]{1,0:T(8,128)(2,1)S(1)} %copy-done.3), channel_id=1, source_target_pairs={{0,1},{1,0},{2,3},{3,2},{4,5},{5,4},{6,7},{7,6},{8,9},{9,8},{10,11... | collective-permute-start | bytes 1572872 | tf_op jit(solution)/shard_map/ppermute | solution.py:239
  28.6 9.1 %collective-permute-start.4 = (bf16[128,2048]{1,0:T(8,128)(2,1)}, bf16[128,2048]{1,0:T(8,128)(2,1)S(1)}, u32[]{:S(2)}, u32[]{:S(2)}) collective-permute-start(bf16[128,2048]{1,0:T(8,128)(2,1)} %get-tuple-element.34), channel_id=1, source_target_pairs={{0,1},{1,0},{2,3},{3,2},{4,5},{5,4},{6,7},{7,6},{8,9},{9,8},{10,11... | collective-permute-start | bytes 1572872 | tf_op jit(solution)/shard_map/ppermute | solution.py:239
  30.0 17.0 %collective-permute-start.7 = (bf16[128,2048]{1,0:T(8,128)(2,1)S(1)}, bf16[128,2048]{1,0:T(8,128)(2,1)S(1)}, u32[]{:S(2)}, u32[]{:S(2)}) collective-permute-start(bf16[128,2048]{1,0:T(8,128)(2,1)S(1)} %collective-permute-done.6.refs_2_), channel_id=1, source_target_pairs={{0,1},{1,0},{2,3},{3,2},{4,5},{5,4},{6,7},{7,6},{8,9},{9,8},{10,11... | collective-permute-start | bytes 1572872 | tf_op jit(solution)/shard_map/ppermute | solution.py:239
  30.9 16.9 %collective-permute-start.9 = (bf16[128,2048]{1,0:T(8,128)(2,1)}, bf16[128,2048]{1,0:T(8,128)(2,1)}, u32[]{:S(2)}, u32[]{:S(2)}) collective-permute-start(bf16[128,2048]{1,0:T(8,128)(2,1)} %shard_map.72), channel_id=1, source_target_pairs={{0,2},{1,3},{2,0},{3,1},{4,6},{5,7},{6,4},{7,5},{8,10},{9,11},{10,... | collective-permute-start | bytes 1572872 | tf_op jit(solution)/shard_map/ppermute | solution.py:239
  33.5 0.7 %copy-start.4 = (bf16[8,64,128]{2,1,0:T(8,128)(2,1)}, bf16[8,64,128]{2,1,0:T(8,128)(2,1)S(1)}, u32[]{:S(2)}) copy-start(bf16[8,64,128]{2,1,0:T(8,128)(2,1)S(1)} %shard_map.69) | copy-start | bytes 393220
  34.1 12.8 %all-to-all-start.1 = ((bf16[32,16,128]{2,1,0:T(8,128)(2,1)}), bf16[32,16,128]{2,1,0:T(8,128)(2,1)S(1)}, u32[]{:S(2)}, u32[]{:S(2)}) async-start(bf16[32,16,128]{2,1,0:T(8,128)(2,1)} %bitcast.14), calls=%async_computation.1 | async-start | bytes 262144 | tf_op jit(solution)/shard_map/all_to_all | solution.py:316

commit v4 on v3

--- a/solution.py
+++ b/solution.py
@@ -3,6 +3,7 @@
 
 import jax
 import jax.numpy as jnp
+import numpy as np
 from jax import lax
 from jax.experimental import pallas as pl
 from jax.experimental.pallas import tpu as pltpu
@@ -13,12 +14,12 @@
 NEG = -1e30
 JOIN_COST = 10**9
 COLUMN_COST = 10**9*3
-LAST_COST = 1
 OWN_ROOM = 48
 BF16 = jnp.bfloat16
 F32 = jnp.float32
 HBM = pl.BlockSpec(memory_space=pltpu.HBM)
 VMEM = pl.BlockSpec(memory_space=pltpu.VMEM)
+SMEM = pl.BlockSpec(memory_space=pltpu.SMEM)
 SCALE2 = HEAD_DIM ** (-0.5) * math.log2(math.e)
 
 
@@ -65,6 +66,28 @@
     return slice(h * HEAD_DIM, (h + 1) * HEAD_DIM)
 
 
+def pack_kernel(q_ref, k_ref, v_ref, w_ref, tail_ref, packed_ref, w_col_ref, tail, cols, w_col, sems):
+    parts, count, per, _ = q_ref.shape
+    near = pl.ds(count - SUMMARY // per, SUMMARY // per)
+    come = []
+    for i, ref in enumerate((k_ref, v_ref)):
+        for f in range(2):
+            come.append((ref.at[parts - 1, near, :, pl.ds((2 + f) * HEAD_DIM, HEAD_DIM)], tail.at[2 * i + f]))
+    for i, ref in enumerate((q_ref, k_ref, v_ref)):
+        come.append((ref.at[:, :, :, pl.ds(HEAD_DIM, HEAD_DIM)], cols.at[i]))
+    come = start(sems, come + [(w_ref.at[pl.ds(HEAD_DIM, HEAD_DIM)], w_col)])
+    first = len(come)
+    wait(come[:4])
+    gone = start(sems, [(tail, tail_ref)], first)
+    for i, copy in enumerate(come[4:7]):
+        wait([copy])
+        pairs = [(cols.at[i, j], packed_ref.at[:, i, j]) for j in range(parts)]
+        gone += start(sems, pairs, first + 1 + i * parts)
+    wait(come[7:])
+    gone += start(sems, [(w_col, w_col_ref)], first + 1 + 3 * parts)
+    wait(gone)
+
+
 def tail_kernel(k_ref, v_ref, tail, sems):
     block = k_ref.shape[0]
     pairs = []
@@ -74,43 +97,24 @@
     wait(start(sems, pairs))
 
 
-def pack_kernel(q_ref, k_ref, v_ref, w_ref, packed_ref, w_col_ref, cols, w_col, sems):
-    parts = q_ref.shape[0]
-    come, leave = [], []
-    for i, ref in enumerate((q_ref, k_ref, v_ref)):
-        come.append((ref.at[:, :, :, pl.ds(HEAD_DIM, HEAD_DIM)], cols.at[i]))
-        for part in range(parts):
-            leave.append((cols.at[i, part], packed_ref.at[:, i, part]))
-    come.append((w_ref.at[pl.ds(HEAD_DIM, HEAD_DIM)], w_col))
-    leave.append((w_col, w_col_ref))
-    come = start(sems, come)
-    gone = []
-    first = len(come)
-    for copy, makes in zip(come, (parts, parts, parts, 1)):
-        wait([copy])
-        gone += start(sems, leave[:makes], first)
-        leave, first = leave[makes:], first + makes
-    wait(gone)
-
-
 def pack(queries, keys, values, out_weight, count, parts, per):
     width = queries.shape[1]
-    (tail,) = call(tail_kernel, [(VMEM, (4, SUMMARY, HEAD_DIM))], [(HBM, keys), (HBM, values)], (), 4, room=63)
+    tail_shape = (4, SUMMARY, HEAD_DIM)
     if per % 16:
+        (tail,) = call(tail_kernel, [(VMEM, tail_shape)], [(HBM, keys), (HBM, values)], (), 4, room=63)
         cut = [x[:, HEAD_DIM : 2 * HEAD_DIM].reshape(parts, count, per, HEAD_DIM) for x in (queries, keys, values)]
         packed = jnp.stack(cut).transpose(2, 0, 1, 3, 4)
         return packed, tail, out_weight[HEAD_DIM : 2 * HEAD_DIM]
-    w_shape = (HEAD_DIM, out_weight.shape[1])
-    cut = [x.reshape(parts, count, per, width) for x in (queries, keys, values)]
-    packed, w_col = call(
+    tail_cut, w_shape = (4, SUMMARY // per, per, HEAD_DIM), (HEAD_DIM, out_weight.shape[1])
+    tail, packed, w_col = call(
         pack_kernel,
-        [(HBM, (count, 3, parts, per, HEAD_DIM)), (HBM, w_shape)],
-        [(HBM, x) for x in (*cut, out_weight)],
-        [pltpu.VMEM((3, parts, count, per, HEAD_DIM), BF16), pltpu.VMEM(w_shape, BF16)],
-        5 + 3 * parts,
+        [(HBM, tail_cut), (HBM, (count, 3, parts, per, HEAD_DIM)), (HBM, w_shape)],
+        [(HBM, x.reshape(parts, count, per, width)) for x in (queries, keys, values)] + [(HBM, out_weight)],
+        [pltpu.VMEM(tail_cut, BF16), pltpu.VMEM((3, parts, count, per, HEAD_DIM), BF16), pltpu.VMEM(w_shape, BF16)],
+        10 + 3 * parts,
         room=63,
     )
-    return packed, tail, w_col
+    return packed, tail.reshape(tail_shape), w_col
 
 
 def column_kernel(columns, moved_ref, out_ref, held, done, sems):
@@ -134,12 +138,17 @@
     wait(start(sems, [(done, out_ref)]))
 
 
-def own_kernel(q_ref, k_ref, v_ref, w_ref, row_ref, sum_ref, stat_ref, q_fixed, w_all, q_all, k_all, v_all, sems):
+def own_kernel(relative, q_ref, k_ref, v_ref, w_ref, lists_ref, slots_ref, row_ref, sum_ref, stat_ref, q_fixed, w_all, mult_ref, q_all, k_all, v_all, sems):
     pairs = [(q_ref, q_all), (k_ref, k_all), (v_ref, v_all)]
     pairs += [(q_ref.at[:, pl.ds(2 * HEAD_DIM, 2 * HEAD_DIM)], q_fixed)]
     pairs += [(w_ref.at[pl.ds(0, HEAD_DIM)], w_all.at[pl.ds(0, HEAD_DIM)])]
     pairs += [(w_ref.at[pl.ds(2 * HEAD_DIM, 2 * HEAD_DIM)], w_all.at[pl.ds(HEAD_DIM, 2 * HEAD_DIM)])]
     copies = start(sems, pairs)
+    me = lax.axis_index("seq")
+    tile = slots_ref[...] ^ me if relative else slots_ref[...]
+    for f in range(2):
+        times = sum((tile == lists_ref[f, i]).astype(F32) for i in range(lists_ref.shape[1]))
+        mult_ref[f : f + 1, :] = jnp.where(tile < me, times, 0.0)
     wait(copies[:3])
     block, step = q_ref.shape[0], HEAD_DIM
     for first in range(0, block, step):
@@ -159,14 +168,14 @@
     wait(copies[3:])
 
 
-def own_part(queries, keys, values, out_weight):
+def own_part(queries, keys, values, out_weight, lists, slots, relative):
     block = queries.shape[0]
     state = (VMEM, (2, block, HEAD_DIM), F32)
     weight_shape = (3 * HEAD_DIM, out_weight.shape[1])
     return call(
-        own_kernel,
-        [(VMEM, (block, HEAD_DIM)), state, state, (VMEM, (block, 2 * HEAD_DIM)), (VMEM, weight_shape)],
-        [(HBM, x) for x in (queries, keys, values, out_weight)],
+        functools.partial(own_kernel, relative),
+        [(VMEM, (block, HEAD_DIM)), state, state, (VMEM, (block, 2 * HEAD_DIM)), (VMEM, weight_shape), (VMEM, (2, slots.shape[1]), F32)],
+        [(HBM, x) for x in (queries, keys, values, out_weight)] + [(SMEM, lists), (VMEM, jnp.array(slots))],
         [pltpu.VMEM(queries.shape, BF16)] * 3,
         6,
         room=OWN_ROOM,
@@ -200,8 +209,15 @@
         out_ref[...] = dot(jnp.concatenate(found, axis=1), w_ref[...]).astype(BF16)
 
 
-def add_kernel(a_ref, b_ref, out_ref, _):
-    out_ref[...] = (a_ref[...].astype(F32) + b_ref[...].astype(F32)).astype(BF16)
+def add_kernel(a_ref, b_ref, out_ref, done, sems):
+    pieces = sems.shape[0]
+    cut = done.shape[0] // pieces
+    sent = []
+    for i in range(pieces):
+        rows = pl.ds(i * cut, cut)
+        done[rows] = (a_ref[rows, :].astype(F32) + b_ref[rows, :].astype(F32)).astype(BF16)
+        sent += start(sems, [(done.at[rows], out_ref.at[rows])], i)
+    wait(sent)
 
 
 def join_kernel(*refs):
@@ -211,27 +227,23 @@
         at += ref.shape[0]
 
 
-def near_kernel(own_ref, core_ref, moved_ref, *refs):
-    ws, (out_ref, moved, sems) = refs[:-3], refs[-3:]
-    wait(start(sems, [(moved_ref, moved)]))
+def last_kernel(own_ref, core_ref, far_ref, moved_ref, *refs):
+    ws, (out_ref, moved, far, done, sems) = refs[:-5], refs[-5:]
+    pieces = (sems.shape[0] - 1) // 2
+    cut = done.shape[1] // pieces
+    cols = [pl.ds(i * cut, cut) for i in range(pieces)]
+    first, *copies = start(sems, [(moved_ref, moved)] + [(far_ref.at[:, c], far.at[:, c]) for c in cols])
     outer, heads, inner, depth = moved.shape
     me = lax.axis_index("head")
-    total = own_ref[...].astype(F32) + core_ref[...].astype(F32)
-    for i, w in enumerate(ws):
-        total += dot(moved[:, me ^ i].reshape(outer * inner, depth), w[...])
-    out_ref[...] = total
-
-
-def last_kernel(near_ref, far_ref, out_ref, near, far, done, sems):
-    pieces = sems.shape[0] // 3
-    cut = done.shape[1] // pieces
-    cols = [pl.ds(i * cut, cut) for i in range(pieces)]
-    copies = start(sems, [(a.at[:, c], b.at[:, c]) for c in cols for a, b in ((near_ref, near), (far_ref, far))])
+    wait([first])
+    found = jnp.concatenate([moved[:, me ^ i].reshape(outer * inner, depth) for i in range(heads)], axis=1)
     sent = []
     for i, c in enumerate(cols):
-        wait(copies[2 * i : 2 * i + 2])
-        done[:, c] = (near[:, c] + far[:, c].astype(F32)).astype(BF16)
-        sent += start(sems, [(done.at[:, c], out_ref.at[:, c])], 2 * pieces + i)
+        total = dot(found, jnp.concatenate([w[:, c] for w in ws], axis=0))
+        total += own_ref[:, c].astype(F32) + core_ref[:, c].astype(F32)
+        wait(copies[i : i + 1])
+        done[:, c] = (total + far[:, c].astype(F32)).astype(BF16)
+        sent += start(sems, [(done.at[:, c], out_ref.at[:, c])], 1 + pieces + i)
     wait(sent)
 
 
@@ -240,16 +252,20 @@
 
 
 def gather_tails(mine, count):
-    order, arrays = [0], [mine[None]]
     bits = [(count // 4**i, 4) for i in range(1, 8) if count % 4**i == 0 and count // 4**i >= 2] + [(1, 2)]
     if count & (count - 1) or bits[-2:][0][0] != 2:
         return [lax.all_gather(mine, "seq")], None
+    order, arrays = [0], [mine[None]]
     for step, radix in bits:
-        held = arrays[0]
         if len(arrays) > 1:
-            shape = (sum(x.shape[0] for x in arrays), *mine.shape)
-            (held,) = call(join_kernel, [(VMEM, shape)], [(VMEM, x) for x in arrays], cost=JOIN_COST)
-        arrays = [held] + [swap(held, "seq", step * i, count) for i in range(1, radix)]
+            shape = (sum(x.shape[0] for x in arrays[1:]), *mine.shape)
+            (came,) = call(join_kernel, [(VMEM, shape)], [(VMEM, x) for x in arrays[1:]], cost=JOIN_COST)
+            arrays = list(lax.optimization_barrier((arrays[0], came)))
+        if step == 1 or len(arrays) == 1:
+            arrays += [swap(x, "seq", step * i, count) for i in range(1, radix) for x in arrays]
+        else:
+            held = jnp.concatenate(arrays, axis=0)
+            arrays = [held] + [swap(held, "seq", step * i, count) for i in range(1, radix)]
         order = [j ^ (step * i) for i in range(radix) for j in order]
     return arrays, order
 
@@ -279,13 +295,23 @@
     w_core = swap(w_col, "head", 1, parts)
     w_both = swap(w_far, "head", 1, parts)
 
-    slot_block = jnp.arange(count, dtype=jnp.int32) if order is None else me ^ jnp.array(order, jnp.int32)
-    names = (summary_lists[0][:, :, None] == slot_block) & (slot_block < me)
-    mult = jnp.repeat(jnp.sum(names.astype(F32), axis=1), SUMMARY, axis=1)
-
+    slots = np.repeat(np.arange(count) if order is None else np.array(order), SUMMARY)[None].astype(np.int32)
     shape = (block // parts, out_weight.shape[1])
-    own = own_part(*held[:4])
-
+    *own, mult = own_part(*held[:4], summary_lists[0], slots, order is not None)
+
+    def partial_sums(flips):
+        return call(
+            functools.partial(part_kernel, flips, parts, [x.shape[0] for x in tails]),
+            [(VMEM, shape)] * len(flips),
+            [(VMEM, x) for x in (*own, mult)] + [(HBM, x) for x in tails],
+            [pltpu.VMEM((count, 4, SUMMARY, HEAD_DIM), BF16)],
+            len(tails),
+        )
+
+    both_sum, far_sum = partial_sums((3, 2))
+    both_in = swap(both_sum, "head", 1, parts)
+    (far_sum,) = call(add_kernel, [(HBM, shape)], [(VMEM, far_sum), (VMEM, both_in)], [pltpu.VMEM(shape, BF16)], 4)
+    moved, _ = lax.optimization_barrier((moved, far_sum))
     column_shape = (moved.shape[0], moved.shape[2], HEAD_DIM)
     (column_out,) = call(
         functools.partial(column_kernel, columns),
@@ -296,18 +322,6 @@
         COLUMN_COST,
     )
 
-    def partial_sums(flips):
-        return call(
-            functools.partial(part_kernel, flips, parts, [x.shape[0] for x in tails]),
-            [(VMEM, shape)] * len(flips),
-            [(VMEM, x) for x in (*own, mult)] + [(HBM, x) for x in tails],
-            [pltpu.VMEM((count, 4, SUMMARY, HEAD_DIM), BF16)],
-            len(tails),
-        )
-
-    both_sum, far_sum = partial_sums((3, 2))
-    both_in = swap(both_sum, "head", 1, parts)
-    (far_sum,) = call(add_kernel, [(VMEM, shape)], [(VMEM, far_sum), (VMEM, both_in)])
     far_in = swap(far_sum, "head", 2, parts)
     core_sum, own_sum = partial_sums((1, 0))
     core_in = swap(core_sum, "head", 1, parts)
@@ -317,19 +331,12 @@
     back = back.reshape(count, parts, per, HEAD_DIM)
     if per % 16:
         back = back.transpose(1, 0, 2, 3).reshape(1, parts, count * per, HEAD_DIM)
-    (near_sum,) = call(
-        near_kernel,
-        [(VMEM, shape, F32)],
-        [(VMEM, own_sum), (VMEM, core_in), (HBM, back)] + [(VMEM, x) for x in (w_col, w_core, w_far, w_both)],
-        [pltpu.VMEM(back.shape, BF16)],
-        cost=LAST_COST,
-    )
     (mixed,) = call(
         last_kernel,
         [(HBM, shape)],
-        [(HBM, near_sum), (HBM, far_in)],
-        [pltpu.VMEM(shape, F32), pltpu.VMEM(shape, BF16), pltpu.VMEM(shape, BF16)],
-        3 * 4,
+        [(VMEM, own_sum), (VMEM, core_in), (HBM, far_in), (HBM, back)] + [(VMEM, x) for x in (w_col, w_core, w_far, w_both)],
+        [pltpu.VMEM(back.shape, BF16), pltpu.VMEM(shape, BF16), pltpu.VMEM(shape, BF16)],
+        1 + 2 * 1,
     )
     return mixed
 

time: 50.1 us -> 47.9 us (0.956)
  waiting for transfers between devices: 11 us -> 9.41 us
  Pallas kernels: 16.1 us -> 14.8 us
  starting transfers between devices: 21.4 us -> 22.5 us
    pallas_call x10 -> x8, Pallas kernels: 16.1 us -> 14.8 us  [call(): pl.pallas_call(kernel, out_shape=[jax.ShapeDtypeStruct(x[1], x[2] if len(...]
    all_to_all x1, starting transfers between devices: 3.63 us -> 4.73 us  [per_device(): lax.all_to_all(column_out, ('seq', 'head'), split_axis=0, concat_axis=0,...]
    all_to_all x1, waiting for transfers between devices: 9.18 us -> 8.21 us  [per_device(): lax.all_to_all(column_out, ('seq', 'head'), split_axis=0, concat_axis=0,...]
    ppermute x10 -> x11, waiting for transfers between devices: 1.87 us -> 1.2 us  [swap(): return lax.ppermute(x, axis, [(i, i ^ flip) for i in range(count)])]
    ppermute x10 -> x11, starting transfers between devices: 11.6 us -> 11.7 us  [swap(): return lax.ppermute(x, axis, [(i, i ^ flip) for i in range(count)])]
  transfers between devices with their start and end apart: 12 -> 13, of which waited for: 3 -> 3; matrix products, arithmetic and copies ran while one was open for 1% -> 0% of each run, Pallas kernels for 26% -> 22%
where the time goes in v4:
time: 47.9 us; the launch traced here: 47.5 us
  starting transfers between devices  22.5 us (47%)
  Pallas kernels  14.8 us (31%)
  waiting for transfers between devices  9.41 us (20%)
  local copies, waits for them, and re-layouts  0.67 us (1%)
    pallas_call x8, Pallas kernels, call(): pl.pallas_call(kernel, out_shape=[jax.ShapeDtypeStruct(x[1], x[2] if len(...  14.8 us
    ppermute x11, starting transfers between devices, swap(): return lax.ppermute(x, axis, [(i, i ^ flip) for i in range(count)])  11.7 us
    all_to_all x1, waiting for transfers between devices, per_device(): lax.all_to_all(column_out, ('seq', 'head'), split_axis=0, concat_axis=0,...  8.21 us
    all_to_all x1, starting transfers between devices, per_device(): lax.all_to_all(packed.reshape(count, 3 * columns, HEAD_DIM), 'seq', split...  6.16 us
    all_to_all x1, starting transfers between devices, per_device(): lax.all_to_all(column_out, ('seq', 'head'), split_axis=0, concat_axis=0,...  4.73 us
    ppermute x11, waiting for transfers between devices, swap(): return lax.ppermute(x, axis, [(i, i ^ flip) for i in range(count)])  1.2 us
  transfers between devices with their start and end apart: 13, of which 3 were waited for; matrix products, arithmetic and copies ran while one was open for 0% of the time, Pallas kernels for 22%

profile of v4, /device:TPU:0, one launch (start us, length us, event | category | flops | bytes accessed | tf_op | source)
XLA Modules:
  0.0 47.5 jit_solution(5621803172240556903)
XLA Ops:
  0.0 2.3 %shard_map.64 = (bf16[4,2,16,128]{3,2,1,0:T(8,128)(2,1)}, bf16[8,3,4,16,128]{4,3,2,1,0:T(8,128)(2,1)}, bf16[128,2048]{1,0:T(8,128)(2,1)}) custom-call(bf16[4,8,16,512]{3,2,1,0:T(8,128)(2,1)} %bitcast.9, bf16[4,8,16,512]{3,2,1,0:T(8,128)(2,1)} %bitcast.10, bf16[4,8,16,512]{3,2,1,0:T(8,128)(2,1)} %bitcast.11, bf16[512,2048]{1,0:T(8,128)(2,1)} %w_ref.2), custom_call_target="tpu_custom_call" | custom-call | flops 1 | bytes 1 | tf_op jit(solution)/shard_map/pallas_call | solution.py:27
  2.3 3.1 %collective-permute-start = (bf16[1,4,32,128]{3,2,1,0:T(8,128)(2,1)}, bf16[1,4,32,128]{3,2,1,0:T(8,128)(2,1)S(1)}, u32[]{:S(2)}, u32[]{:S(2)}) collective-permute-start(bf16[1,4,32,128]{3,2,1,0:T(8,128)(2,1)} %bitcast.14), channel_id=1, source_target_pairs={{0,8},{4,12},{8,0},{12,4},{16,24},{20,28},{24,16},{28,20},{1,9},{5... | collective-permute-start | bytes 98312 | tf_op jit(solution)/shard_map/ppermute | solution.py:251
  5.4 2.6 %collective-permute-start.1 = (bf16[1,4,32,128]{3,2,1,0:T(8,128)(2,1)}, bf16[1,4,32,128]{3,2,1,0:T(8,128)(2,1)S(1)}, u32[]{:S(2)}, u32[]{:S(2)}) collective-permute-start(bf16[1,4,32,128]{3,2,1,0:T(8,128)(2,1)} %bitcast.15), channel_id=1, source_target_pairs={{0,16},{4,20},{8,24},{12,28},{16,0},{20,4},{24,8},{28,12},{1,17},{... | collective-permute-start | bytes 98312 | tf_op jit(solution)/shard_map/ppermute | solution.py:251
  8.0 0.0 copy-start.1
  8.0 0.0 copy-start.7
  8.0 6.2 %all-to-all-start = ((bf16[8,192,128]{2,1,0:T(8,128)(2,1)}), bf16[8,192,128]{2,1,0:T(8,128)(2,1)S(1)}, u32[]{:S(2)}, u32[]{:S(2)}) async-start(bf16[8,192,128]{2,1,0:T(8,128)(2,1)} %bitcast.22), calls=%async_computation | async-start | bytes 786432 | tf_op jit(solution)/shard_map/all_to_all | solution.py:283
  14.3 2.1 %collective-permute-start.4 = (bf16[3,4,32,128]{3,2,1,0:T(8,128)(2,1)S(1)}, bf16[3,4,32,128]{3,2,1,0:T(8,128)(2,1)S(1)}, u32[]{:S(2)}, u32[]{:S(2)}) collective-permute-start(bf16[3,4,32,128]{3,2,1,0:T(8,128)(2,1)S(1)} %shard_map.65.refs_1_), channel_id=1, source_target_pairs={{0,4},{4,0},{8,12},{12,8},{16,20},{20,16},{24,28},{28,24},{1,5},{5... | collective-permute-start | bytes 294920 | tf_op jit(solution)/shard_map/ppermute | solution.py:251
  16.3 0.1 collective-permute-start.3
  16.4 1.5 %collective-permute-start.9 = (bf16[128,2048]{1,0:T(8,128)(2,1)S(1)}, bf16[128,2048]{1,0:T(8,128)(2,1)S(1)}, u32[]{:S(2)}, u32[]{:S(2)}) collective-permute-start(bf16[128,2048]{1,0:T(8,128)(2,1)S(1)} %copy-done.3), channel_id=1, source_target_pairs={{0,2},{1,3},{2,0},{3,1},{4,6},{5,7},{6,4},{7,5},{8,10},{9,11},{10,... | collective-permute-start | bytes 1572872 | tf_op jit(solution)/shard_map/ppermute | solution.py:251
  18.0 3.7 %shard_map.66 = (bf16[512,128]{1,0:T(8,128)(2,1)S(1)}, f32[2,512,128]{2,1,0:T(8,128)S(1)}, f32[2,512,128]{2,1,0:T(8,128)S(1)}, bf16[512,256]{1,0:T(8,128)(2,1)S(...) custom-call(bf16[512,512]{1,0:T(8,128)(2,1)S(1)} %copy-done, bf16[512,512]{1,0:T(8,128)(2,1)S(1)} %copy-done.1, ...), custom_call_target="tpu_custom_call" | custom-call | flops 1 | bytes 1 | tf_op jit(solution)/shard_map/pallas_call | solution.py:27
  21.7 0.3 collective-permute-done.3.refs_2_
  22.0 2.4 %shard_map.68 = (bf16[128,2048]{1,0:T(8,128)(2,1)S(1)}, bf16[128,2048]{1,0:T(8,128)(2,1)S(1)}) custom-call(bf16[512,128]{1,0:T(8,128)(2,1)S(1)} %get-tuple-element.34.row_ref, f32[2,512,128]{2,1,0:T(8,128)S(1)} %get-tuple-element.35.sum_ref, f32[2,512,128]{2,1,0:T(8,128)S(1)} %get-tuple-element.36.stat_ref, bf16[512,256]{1,0:T(8,128)(2,1)S(1)} %get-tuple-element.37.q_ref, ...), custom_call_target="tpu_custom_call" | custom-call | flops 1 | bytes 1 | tf_op jit(solution)/shard_map/pallas_call | solution.py:27
  24.4 0.1 collective-permute-start.6
  24.5 0.5 %collective-permute-start.8 = (bf16[128,2048]{1,0:T(8,128)(2,1)S(1)}, bf16[128,2048]{1,0:T(8,128)(2,1)S(1)}, u32[]{:S(2)}, u32[]{:S(2)}) collective-permute-start(bf16[128,2048]{1,0:T(8,128)(2,1)S(1)} %copy-done.3), channel_id=1, source_target_pairs={{0,1},{1,0},{2,3},{3,2},{4,5},{5,4},{6,7},{7,6},{8,9},{9,8},{10,11... | collective-permute-start | bytes 1572872 | tf_op jit(solution)/shard_map/ppermute | solution.py:251
  25.0 2.4 %shard_map.67 = (bf16[128,2048]{1,0:T(8,128)(2,1)}, bf16[128,2048]{1,0:T(8,128)(2,1)S(1)}) custom-call(bf16[512,128]{1,0:T(8,128)(2,1)S(1)} %get-tuple-element.34.row_ref, f32[2,512,128]{2,1,0:T(8,128)S(1)} %get-tuple-element.35.sum_ref, f32[2,512,128]{2,1,0:T(8,128)S(1)} %get-tuple-element.36.stat_ref, bf16[512,256]{1,0:T(8,128)(2,1)S(1)} %get-tuple-element.37.q_ref, ...), custom_call_target="tpu_custom_call" | custom-call | flops 1 | bytes 1 | tf_op jit(solution)/shard_map/pallas_call | solution.py:27
  27.4 0.1 collective-permute-start.5
  27.5 0.9 %collective-permute-done.9.refs_2_ = bf16[128,2048]{1,0:T(8,128)(2,1)S(1)} collective-permute-done((bf16[128,2048]{1,0:T(8,128)(2,1)S(1)}, bf16[128,2048]{1,0:T(8,128)(2,1)S(1)}, u32[]{:S(2)}, u32[]{:S(2)}) %collective-permute-start.9) | collective-permute-done | bytes 524320 | tf_op jit(solution)/shard_map/ppermute | solution.py:251
  28.4 0.9 %shard_map.69 = bf16[128,2048]{1,0:T(8,128)(2,1)} custom-call(bf16[128,2048]{1,0:T(8,128)(2,1)S(1)} %get-tuple-element.44.a_ref, bf16[128,2048]{1,0:T(8,128)(2,1)S(1)} %collective-permute-done.6.b_ref), custom_call_target="tpu_custom_call" | custom-call | flops 1 | bytes 1 | tf_op jit(solution)/shard_map/pallas_call | solution.py:27
  29.3 1.6 %collective-permute-start.7 = (bf16[128,2048]{1,0:T(8,128)(2,1)}, bf16[128,2048]{1,0:T(8,128)(2,1)}, u32[]{:S(2)}, u32[]{:S(2)}) collective-permute-start(bf16[128,2048]{1,0:T(8,128)(2,1)} %shard_map.69), channel_id=1, source_target_pairs={{0,2},{1,3},{2,0},{3,1},{4,6},{5,7},{6,4},{7,5},{8,10},{9,11},{10,... | collective-permute-start | bytes 1572872 | tf_op jit(solution)/shard_map/ppermute | solution.py:251
  30.9 0.9 %shard_map.70 = bf16[8,64,128]{2,1,0:T(8,128)(2,1)S(1)} custom-call(bf16[8,3,64,128]{3,2,1,0:T(8,128)(2,1)S(1)} %bitcast.13), custom_call_target="tpu_custom_call" | custom-call | flops 3000000000 | bytes 1 | tf_op jit(solution)/shard_map/pallas_call | solution.py:27
  31.8 0.6 %copy-done.5 = bf16[8,64,128]{2,1,0:T(8,128)(2,1)} copy-done((bf16[8,64,128]{2,1,0:T(8,128)(2,1)}, bf16[8,64,128]{2,1,0:T(8,128)(2,1)S(1)}, u32[]{:S(2)}) %copy-start.5) | copy-done | bytes 131096
  32.5 4.7 %all-to-all-start.1 = ((bf16[32,16,128]{2,1,0:T(8,128)(2,1)}), bf16[32,16,128]{2,1,0:T(8,128)(2,1)S(1)}, u32[]{:S(2)}, u32[]{:S(2)}) async-start(bf16[32,16,128]{2,1,0:T(8,128)(2,1)} %bitcast.20), calls=%async_computation.1 | async-start | bytes 262144 | tf_op jit(solution)/shard_map/all_to_all | solution.py:330
  37.2 8.2 %all-to-all-done.1 = bf16[32,16,128]{2,1,0:T(8,128)(2,1)S(1)} async-done(((bf16[32,16,128]{2,1,0:T(8,128)(2,1)}), bf16[32,16,128]{2,1,0:T(8,128)(2,1)S(1)}, u32[]{:S(2)}, u32[]{:S(2)}) %all-to-all-start.1) | async-done | bytes 131104 | tf_op jit(solution)/shard_map/all_to_all | solution.py:330
  45.4 2.1 %shard_map.71 = bf16[128,2048]{1,0:T(8,128)(2,1)} custom-call(bf16[128,2048]{1,0:T(8,128)(2,1)S(1)} %get-tuple-element.42.own_ref, bf16[128,2048]{1,0:T(8,128)(2,1)S(1)} %collective-permute-done.5.core_ref, bf16[128,2048]{1,0:T(8,128)(2,1)} %collective-permute-done.7.far_ref, bf16[8,4,16,128]{3,2,1,0:T(8,128)(2,1)S(1)} %bitcast.12, ...), custom_call_target="tpu_custom_call" | custom-call | flops 1 | bytes 1 | tf_op jit(solution)/shard_map/pallas_call | solution.py:27
  (26 shorter events, 0.1 us)
Async XLA Ops:
  2.3 11.9 %collective-permute-start = (bf16[1,4,32,128]{3,2,1,0:T(8,128)(2,1)}, bf16[1,4,32,128]{3,2,1,0:T(8,128)(2,1)S(1)}, u32[]{:S(2)}, u32[]{:S(2)}) collective-permute-start(bf16[1,4,32,128]{3,2,1,0:T(8,128)(2,1)} %bitcast.14), channel_id=1, source_target_pairs={{0,8},{4,12},{8,0},{12,4},{16,24},{20,28},{24,16},{28,20},{1,9},{5... | collective-permute-start | bytes 98312 | tf_op jit(solution)/shard_map/ppermute | solution.py:251
  5.4 8.8 %collective-permute-start.1 = (bf16[1,4,32,128]{3,2,1,0:T(8,128)(2,1)}, bf16[1,4,32,128]{3,2,1,0:T(8,128)(2,1)S(1)}, u32[]{:S(2)}, u32[]{:S(2)}) collective-permute-start(bf16[1,4,32,128]{3,2,1,0:T(8,128)(2,1)} %bitcast.15), channel_id=1, source_target_pairs={{0,16},{4,20},{8,24},{12,28},{16,0},{20,4},{24,8},{28,12},{1,17},{... | collective-permute-start | bytes 98312 | tf_op jit(solution)/shard_map/ppermute | solution.py:251
  8.0 6.2 %collective-permute-start.2 = (bf16[1,4,32,128]{3,2,1,0:T(8,128)(2,1)}, bf16[1,4,32,128]{3,2,1,0:T(8,128)(2,1)S(1)}, u32[]{:S(2)}, u32[]{:S(2)}) collective-permute-start(bf16[1,4,32,128]{3,2,1,0:T(8,128)(2,1)} %bitcast.16), channel_id=1, source_target_pairs={{0,24},{4,28},{8,16},{12,20},{16,8},{20,12},{24,0},{28,4},{1,25},{... | collective-permute-start | bytes 98312 | tf_op jit(solution)/shard_map/ppermute | solution.py:251
  8.0 8.4 %copy-start.4 = (bf16[4,2,16,128]{3,2,1,0:T(8,128)(2,1)S(1)}, bf16[4,2,16,128]{3,2,1,0:T(8,128)(2,1)}, u32[]{:S(2)}) copy-start(bf16[4,2,16,128]{3,2,1,0:T(8,128)(2,1)} %get-tuple-element.28) | copy-start | bytes 98308
  8.0 8.4 %copy-start.3 = (bf16[128,2048]{1,0:T(8,128)(2,1)S(1)}, bf16[128,2048]{1,0:T(8,128)(2,1)}, u32[]{:S(2)}) copy-start(bf16[128,2048]{1,0:T(8,128)(2,1)} %get-tuple-element.48.refs_0_) | copy-start | bytes 1572868
  8.0 10.0 %copy-start = (bf16[512,512]{1,0:T(8,128)(2,1)S(1)}, bf16[512,512]{1,0:T(8,128)(2,1)}, u32[]{:S(2)}) copy-start(bf16[512,512]{1,0:T(8,128)(2,1)} %q_ref) | copy-start | bytes 1572868
  8.0 10.0 %copy-start.1 = (bf16[512,512]{1,0:T(8,128)(2,1)S(1)}, bf16[512,512]{1,0:T(8,128)(2,1)}, u32[]{:S(2)}) copy-start(bf16[512,512]{1,0:T(8,128)(2,1)} %k_ref) | copy-start | bytes 1572868
  8.0 9.9 %copy-start.2 = (bf16[512,512]{1,0:T(8,128)(2,1)S(1)}, bf16[512,512]{1,0:T(8,128)(2,1)}, u32[]{:S(2)}) copy-start(bf16[512,512]{1,0:T(8,128)(2,1)} %v_ref) | copy-start | bytes 1572868
  8.0 9.9 %copy-start.6 = (s32[1,2,16]{2,1,0:T(2,128)S(1)}, s32[1,2,16]{2,1,0:T(2,128)}, u32[]{:S(2)}) copy-start(s32[1,2,16]{2,1,0:T(2,128)} %param.9) | copy-start | bytes 388
  8.0 9.9 %copy-start.7 = (s32[1,256]{1,0:T(1,128)S(1)}, s32[1,256]{1,0:T(1,128)}, u32[]{:S(2)}) copy-start(s32[1,256]{1,0:T(1,128)} %constant.2.clone.slots_ref) | copy-start | bytes 3076
  8.0 22.8 %all-to-all-start = ((bf16[8,192,128]{2,1,0:T(8,128)(2,1)}), bf16[8,192,128]{2,1,0:T(8,128)(2,1)S(1)}, u32[]{:S(2)}, u32[]{:S(2)}) async-start(bf16[8,192,128]{2,1,0:T(8,128)(2,1)} %bitcast.22), calls=%async_computation | async-start | bytes 786432 | tf_op jit(solution)/shard_map/all_to_all | solution.py:283
  14.3 7.7 %collective-permute-start.4 = (bf16[3,4,32,128]{3,2,1,0:T(8,128)(2,1)S(1)}, bf16[3,4,32,128]{3,2,1,0:T(8,128)(2,1)S(1)}, u32[]{:S(2)}, u32[]{:S(2)}) collective-permute-start(bf16[3,4,32,128]{3,2,1,0:T(8,128)(2,1)S(1)} %shard_map.65.refs_1_), channel_id=1, source_target_pairs={{0,4},{4,0},{8,12},{12,8},{16,20},{20,16},{24,28},{28,24},{1,5},{5... | collective-permute-start | bytes 294920 | tf_op jit(solution)/shard_map/ppermute | solution.py:251
  16.3 5.6 %collective-permute-start.3 = (bf16[1,4,32,128]{3,2,1,0:T(8,128)(2,1)S(1)}, bf16[1,4,32,128]{3,2,1,0:T(8,128)(2,1)S(1)}, u32[]{:S(2)}, u32[]{:S(2)}) collective-permute-start(bf16[1,4,32,128]{3,2,1,0:T(8,128)(2,1)S(1)} %bitcast.17), channel_id=1, source_target_pairs={{0,4},{4,0},{8,12},{12,8},{16,20},{20,16},{24,28},{28,24},{1,5},{5... | collective-permute-start | bytes 98312 | tf_op jit(solution)/shard_map/ppermute | solution.py:251
  16.4 12.0 %collective-permute-start.9 = (bf16[128,2048]{1,0:T(8,128)(2,1)S(1)}, bf16[128,2048]{1,0:T(8,128)(2,1)S(1)}, u32[]{:S(2)}, u32[]{:S(2)}) collective-permute-start(bf16[128,2048]{1,0:T(8,128)(2,1)S(1)} %copy-done.3), channel_id=1, source_target_pairs={{0,2},{1,3},{2,0},{3,1},{4,6},{5,7},{6,4},{7,5},{8,10},{9,11},{10,... | collective-permute-start | bytes 1572872 | tf_op jit(solution)/shard_map/ppermute | solution.py:251
  24.4 4.0 %collective-permute-start.6 = (bf16[128,2048]{1,0:T(8,128)(2,1)S(1)}, bf16[128,2048]{1,0:T(8,128)(2,1)S(1)}, u32[]{:S(2)}, u32[]{:S(2)}) collective-permute-start(bf16[128,2048]{1,0:T(8,128)(2,1)S(1)} %get-tuple-element.45), channel_id=1, source_target_pairs={{0,1},{1,0},{2,3},{3,2},{4,5},{5,4},{6,7},{7,6},{8,9},{9,8},{10,11... | collective-permute-start | bytes 1572872 | tf_op jit(solution)/shard_map/ppermute | solution.py:251
  24.5 12.7 %collective-permute-start.8 = (bf16[128,2048]{1,0:T(8,128)(2,1)S(1)}, bf16[128,2048]{1,0:T(8,128)(2,1)S(1)}, u32[]{:S(2)}, u32[]{:S(2)}) collective-permute-start(bf16[128,2048]{1,0:T(8,128)(2,1)S(1)} %copy-done.3), channel_id=1, source_target_pairs={{0,1},{1,0},{2,3},{3,2},{4,5},{5,4},{6,7},{7,6},{8,9},{9,8},{10,11... | collective-permute-start | bytes 1572872 | tf_op jit(solution)/shard_map/ppermute | solution.py:251
  27.4 9.8 %collective-permute-start.5 = (bf16[128,2048]{1,0:T(8,128)(2,1)}, bf16[128,2048]{1,0:T(8,128)(2,1)S(1)}, u32[]{:S(2)}, u32[]{:S(2)}) collective-permute-start(bf16[128,2048]{1,0:T(8,128)(2,1)} %get-tuple-element.43), channel_id=1, source_target_pairs={{0,1},{1,0},{2,3},{3,2},{4,5},{5,4},{6,7},{7,6},{8,9},{9,8},{10,11... | collective-permute-start | bytes 1572872 | tf_op jit(solution)/shard_map/ppermute | solution.py:251
  28.4 17.0 %collective-permute-start.10 = (bf16[128,2048]{1,0:T(8,128)(2,1)S(1)}, bf16[128,2048]{1,0:T(8,128)(2,1)S(1)}, u32[]{:S(2)}, u32[]{:S(2)}) collective-permute-start(bf16[128,2048]{1,0:T(8,128)(2,1)S(1)} %collective-permute-done.9.refs_2_), channel_id=1, source_target_pairs={{0,1},{1,0},{2,3},{3,2},{4,5},{5,4},{6,7},{7,6},{8,9},{9,8},{10,11... | collective-permute-start | bytes 1572872 | tf_op jit(solution)/shard_map/ppermute | solution.py:251
  29.3 16.1 %collective-permute-start.7 = (bf16[128,2048]{1,0:T(8,128)(2,1)}, bf16[128,2048]{1,0:T(8,128)(2,1)}, u32[]{:S(2)}, u32[]{:S(2)}) collective-permute-start(bf16[128,2048]{1,0:T(8,128)(2,1)} %shard_map.69), channel_id=1, source_target_pairs={{0,2},{1,3},{2,0},{3,1},{4,6},{5,7},{6,4},{7,5},{8,10},{9,11},{10,... | collective-permute-start | bytes 1572872 | tf_op jit(solution)/shard_map/ppermute | solution.py:251
  31.8 0.6 %copy-start.5 = (bf16[8,64,128]{2,1,0:T(8,128)(2,1)}, bf16[8,64,128]{2,1,0:T(8,128)(2,1)S(1)}, u32[]{:S(2)}) copy-start(bf16[8,64,128]{2,1,0:T(8,128)(2,1)S(1)} %shard_map.70) | copy-start | bytes 393220
  32.5 13.0 %all-to-all-start.1 = ((bf16[32,16,128]{2,1,0:T(8,128)(2,1)}), bf16[32,16,128]{2,1,0:T(8,128)(2,1)S(1)}, u32[]{:S(2)}, u32[]{:S(2)}) async-start(bf16[32,16,128]{2,1,0:T(8,128)(2,1)} %bitcast.20), calls=%async_computation.1 | async-start | bytes 262144 | tf_op jit(solution)/shard_map/all_to_all | solution.py:330

commit v5 on v4

--- a/solution.py
+++ b/solution.py
@@ -15,6 +15,7 @@
 JOIN_COST = 10**9
 COLUMN_COST = 10**9*3
 OWN_ROOM = 48
+SETTLE_COST = 25*10**8
 BF16 = jnp.bfloat16
 F32 = jnp.float32
 HBM = pl.BlockSpec(memory_space=pltpu.HBM)
@@ -75,7 +76,10 @@
             come.append((ref.at[parts - 1, near, :, pl.ds((2 + f) * HEAD_DIM, HEAD_DIM)], tail.at[2 * i + f]))
     for i, ref in enumerate((q_ref, k_ref, v_ref)):
         come.append((ref.at[:, :, :, pl.ds(HEAD_DIM, HEAD_DIM)], cols.at[i]))
-    come = start(sems, come + [(w_ref.at[pl.ds(HEAD_DIM, HEAD_DIM)], w_col)])
+    quarter = HEAD_DIM // 4
+    for i in range(4):
+        come.append((w_ref.at[pl.ds(HEAD_DIM + i * quarter, quarter)], w_col.at[pl.ds(i * quarter, quarter)]))
+    come = start(sems, come)
     first = len(come)
     wait(come[:4])
     gone = start(sems, [(tail, tail_ref)], first)
@@ -83,8 +87,10 @@
         wait([copy])
         pairs = [(cols.at[i, j], packed_ref.at[:, i, j]) for j in range(parts)]
         gone += start(sems, pairs, first + 1 + i * parts)
-    wait(come[7:])
-    gone += start(sems, [(w_col, w_col_ref)], first + 1 + 3 * parts)
+    for i, copy in enumerate(come[7:]):
+        wait([copy])
+        rows = pl.ds(i * quarter, quarter)
+        gone += start(sems, [(w_col.at[rows], w_col_ref.at[rows])], first + 1 + 3 * parts + i)
     wait(gone)
 
 
@@ -111,7 +117,7 @@
         [(HBM, tail_cut), (HBM, (count, 3, parts, per, HEAD_DIM)), (HBM, w_shape)],
         [(HBM, x.reshape(parts, count, per, width)) for x in (queries, keys, values)] + [(HBM, out_weight)],
         [pltpu.VMEM(tail_cut, BF16), pltpu.VMEM((3, parts, count, per, HEAD_DIM), BF16), pltpu.VMEM(w_shape, BF16)],
-        10 + 3 * parts,
+        16 + 3 * parts,
         room=63,
     )
     return packed, tail.reshape(tail_shape), w_col
@@ -182,31 +188,29 @@
     )
 
 
-def part_kernel(flips, parts, slots, row_ref, sum_ref, stat_ref, q_ref, w_ref, mult_ref, *refs):
-    tails, refs = refs[: len(slots)], refs[len(slots) :]
-    outs, (far, sems) = refs[: len(flips)], refs[len(flips) :]
-    pairs, at = [], 0
-    for tail, many in zip(tails, slots):
-        pairs.append((tail, far.at[pl.ds(at, many)]))
-        at += many
-    wait(start(sems, pairs))
+def part_kernel(flips, parts, row_ref, sum_ref, stat_ref, q_ref, w_ref, mult_ref, *refs):
+    tails, outs = refs[: -len(flips) - 1], refs[-len(flips) - 1 : -1]
     rows = q_ref.shape[0] // parts
     me = lax.axis_index("head")
-    away_kv = [far[:, i].reshape(at * SUMMARY, HEAD_DIM) for i in range(4)]
-    for flip, out_ref in zip(flips, outs):
-        here = pl.ds(pl.multiple_of((me ^ flip) * rows, rows), rows)
-        found = [row_ref[here, :]]
-        for f in range(2):
-            mult = mult_ref[f : f + 1, :]
-            away = jnp.where(mult > 0, dot_t(q_ref[here, head(f)], away_kv[f]), NEG)
-            own_denom, own_peak = stat_ref[f, here, :1], stat_ref[f, here, HEAD_DIM // 2 : HEAD_DIM // 2 + 1]
-            peak = jnp.maximum(own_peak, jnp.max(away, axis=1, keepdims=True))
-            shrink = jnp.exp2((own_peak - peak) * SCALE2)
-            away = jnp.exp2((away - peak) * SCALE2) * mult
-            denom = own_denom * shrink + jnp.sum(away, axis=1, keepdims=True)
-            total = sum_ref[f, here, :] * shrink + dot(away.astype(BF16), away_kv[2 + f])
-            found.append((total / denom).astype(BF16))
-        out_ref[...] = dot(jnp.concatenate(found, axis=1), w_ref[...]).astype(BF16)
+    away_kv = [
+        jnp.concatenate([x[:, i].reshape(x.shape[0] * SUMMARY, HEAD_DIM) for x in tails], axis=0) for i in range(4)
+    ]
+    here = [pl.ds(pl.multiple_of((me ^ flip) * rows, rows), rows) for flip in flips]
+    items = [(at, f) for at in here for f in range(2)]
+    mult = [mult_ref[f : f + 1, :] for f in range(2)]
+    ones = jnp.ones_like(away_kv[0])
+    values = [jnp.concatenate([away_kv[2 + f], ones], axis=1) for f in range(2)]
+    away = [jnp.where(mult[f] > 0, dot_t(q_ref[at, head(f)], away_kv[f]), NEG) for at, f in items]
+    own_peak = [stat_ref[f, at, HEAD_DIM // 2 : HEAD_DIM // 2 + 1] for at, f in items]
+    peak = [jnp.maximum(x, jnp.max(y, axis=1, keepdims=True)) for x, y in zip(own_peak, away)]
+    away = [(jnp.exp2((x - y) * SCALE2) * mult[f]).astype(BF16) for x, y, (_, f) in zip(away, peak, items)]
+    total = [dot(x, values[f]) for x, (_, f) in zip(away, items)]
+    shrink = [jnp.exp2((x - y) * SCALE2) for x, y in zip(own_peak, peak)]
+    denom = [stat_ref[f, at, :1] * z + x[:, HEAD_DIM:] for (at, f), x, z in zip(items, total, shrink)]
+    total = [sum_ref[f, at, :] * z + x[:, :HEAD_DIM] for (at, f), x, z in zip(items, total, shrink)]
+    found = [(x / y).astype(BF16) for x, y in zip(total, denom)]
+    for i, (at, out_ref) in enumerate(zip(here, outs)):
+        out_ref[...] = dot(jnp.concatenate([row_ref[at, :], *found[2 * i : 2 * i + 2]], axis=1), w_ref[...]).astype(BF16)
 
 
 def add_kernel(a_ref, b_ref, out_ref, done, sems):
@@ -228,7 +232,7 @@
 
 
 def last_kernel(own_ref, core_ref, far_ref, moved_ref, *refs):
-    ws, (out_ref, moved, far, done, sems) = refs[:-5], refs[-5:]
+    ws, (out_ref, moved, far, done, sems) = refs[:-6], refs[-5:]
     pieces = (sems.shape[0] - 1) // 2
     cut = done.shape[1] // pieces
     cols = [pl.ds(i * cut, cut) for i in range(pieces)]
@@ -245,6 +249,10 @@
         done[:, c] = (total + far[:, c].astype(F32)).astype(BF16)
         sent += start(sems, [(done.at[:, c], out_ref.at[:, c])], 1 + pieces + i)
     wait(sent)
+
+
+def settle_kernel(w_ref, out_ref, sems):
+    wait(start(sems, [(w_ref.at[pl.ds(0, 16), pl.ds(0, HEAD_DIM)], out_ref)]))
 
 
 def swap(x, axis, flip, count):
@@ -287,10 +295,9 @@
     if columns % 16:
         moved = moved.transpose(1, 0, 2, 3).reshape(1, 3, block, HEAD_DIM)
 
-    held = [queries, keys, values, out_weight, w_col]
+    held = [queries, keys, values, out_weight]
     if len(tails) > 1:
         *held, tails[0] = lax.optimization_barrier((*held, tails[0]))
-    w_col = held[4]
     w_far = swap(w_col, "head", 2, parts)
     w_core = swap(w_col, "head", 1, parts)
     w_both = swap(w_far, "head", 1, parts)
@@ -301,11 +308,9 @@
 
     def partial_sums(flips):
         return call(
-            functools.partial(part_kernel, flips, parts, [x.shape[0] for x in tails]),
+            functools.partial(part_kernel, flips, parts),
             [(VMEM, shape)] * len(flips),
-            [(VMEM, x) for x in (*own, mult)] + [(HBM, x) for x in tails],
-            [pltpu.VMEM((count, 4, SUMMARY, HEAD_DIM), BF16)],
-            len(tails),
+            [(VMEM, x) for x in (*own, mult, *tails)],
         )
 
     both_sum, far_sum = partial_sums((3, 2))
@@ -331,10 +336,11 @@
     back = back.reshape(count, parts, per, HEAD_DIM)
     if per % 16:
         back = back.transpose(1, 0, 2, 3).reshape(1, parts, count * per, HEAD_DIM)
+    (settled,) = call(settle_kernel, [(VMEM, (16, HEAD_DIM))], [(HBM, w_both)], cost=SETTLE_COST)
     (mixed,) = call(
         last_kernel,
         [(HBM, shape)],
-        [(VMEM, own_sum), (VMEM, core_in), (HBM, far_in), (HBM, back)] + [(VMEM, x) for x in (w_col, w_core, w_far, w_both)],
+        [(VMEM, own_sum), (VMEM, core_in), (HBM, far_in), (HBM, back)] + [(VMEM, x) for x in (w_col, w_core, w_far, w_both, settled)],
         [pltpu.VMEM(back.shape, BF16), pltpu.VMEM(shape, BF16), pltpu.VMEM(shape, BF16)],
         1 + 2 * 1,
     )

time: 47.9 us -> 46.5 us (0.971)
  Pallas kernels: 14.8 us -> 13 us
    pallas_call x8 -> x9, Pallas kernels: 14.8 us -> 13 us  [call(): pl.pallas_call(kernel, out_shape=[jax.ShapeDtypeStruct(x[1], x[2] if len(...]
    all_to_all x1, starting transfers between devices: 4.73 us -> 5.4 us  [per_device(): lax.all_to_all(column_out, ('seq', 'head'), split_axis=0, concat_axis=0,...]
  transfers between devices with their start and end apart: 13 -> 13, of which waited for: 3 -> 2; matrix products, arithmetic and copies ran while one was open for 0% -> 0% of each run, Pallas kernels for 22% -> 19%
where the time goes in v5:
time: 46.5 us; the launch traced here: 46.1 us
  starting transfers between devices  22.6 us (49%)
  Pallas kernels  13 us (28%)
  waiting for transfers between devices  9.69 us (21%)
  local copies, waits for them, and re-layouts  0.66 us (1%)
    pallas_call x9, Pallas kernels, call(): pl.pallas_call(kernel, out_shape=[jax.ShapeDtypeStruct(x[1], x[2] if len(...  13 us
    ppermute x11, starting transfers between devices, swap(): return lax.ppermute(x, axis, [(i, i ^ flip) for i in range(count)])  11.3 us
    all_to_all x1, waiting for transfers between devices, per_device(): lax.all_to_all(column_out, ('seq', 'head'), split_axis=0, concat_axis=0,...  8.17 us
    all_to_all x1, starting transfers between devices, per_device(): lax.all_to_all(packed.reshape(count, 3 * columns, HEAD_DIM), 'seq', split...  5.95 us
    all_to_all x1, starting transfers between devices, per_device(): lax.all_to_all(column_out, ('seq', 'head'), split_axis=0, concat_axis=0,...  5.4 us
    ppermute x11, waiting for transfers between devices, swap(): return lax.ppermute(x, axis, [(i, i ^ flip) for i in range(count)])  1.52 us
  transfers between devices with their start and end apart: 13, of which 2 were waited for; matrix products, arithmetic and copies ran while one was open for 0% of the time, Pallas kernels for 19%

profile of v5, /device:TPU:0, one launch (start us, length us, event | category | flops | bytes accessed | tf_op | source)
XLA Modules:
  0.0 46.1 jit_solution(16353327115323464014)
XLA Ops:
  0.0 2.2 %shard_map.64 = (bf16[4,2,16,128]{3,2,1,0:T(8,128)(2,1)}, bf16[8,3,4,16,128]{4,3,2,1,0:T(8,128)(2,1)}, bf16[128,2048]{1,0:T(8,128)(2,1)}) custom-call(bf16[4,8,16,512]{3,2,1,0:T(8,128)(2,1)} %bitcast.9, bf16[4,8,16,512]{3,2,1,0:T(8,128)(2,1)} %bitcast.10, bf16[4,8,16,512]{3,2,1,0:T(8,128)(2,1)} %bitcast.11, bf16[512,2048]{1,0:T(8,128)(2,1)} %w_ref.2), custom_call_target="tpu_custom_call" | custom-call | flops 1 | bytes 1 | tf_op jit(solution)/shard_map/pallas_call | solution.py:28
  2.2 3.1 %collective-permute-start = (bf16[1,4,32,128]{3,2,1,0:T(8,128)(2,1)}, bf16[1,4,32,128]{3,2,1,0:T(8,128)(2,1)S(1)}, u32[]{:S(2)}, u32[]{:S(2)}) collective-permute-start(bf16[1,4,32,128]{3,2,1,0:T(8,128)(2,1)} %bitcast.14), channel_id=1, source_target_pairs={{0,8},{4,12},{8,0},{12,4},{16,24},{20,28},{24,16},{28,20},{1,9},{5... | collective-permute-start | bytes 98312 | tf_op jit(solution)/shard_map/ppermute | solution.py:259
  5.3 2.6 %collective-permute-start.1 = (bf16[1,4,32,128]{3,2,1,0:T(8,128)(2,1)}, bf16[1,4,32,128]{3,2,1,0:T(8,128)(2,1)S(1)}, u32[]{:S(2)}, u32[]{:S(2)}) collective-permute-start(bf16[1,4,32,128]{3,2,1,0:T(8,128)(2,1)} %bitcast.15), channel_id=1, source_target_pairs={{0,16},{4,20},{8,24},{12,28},{16,0},{20,4},{24,8},{28,12},{1,17},{... | collective-permute-start | bytes 98312 | tf_op jit(solution)/shard_map/ppermute | solution.py:259
  7.9 1.7 %collective-permute-start.9 = (bf16[128,2048]{1,0:T(8,128)(2,1)}, bf16[128,2048]{1,0:T(8,128)(2,1)S(1)}, u32[]{:S(2)}, u32[]{:S(2)}) collective-permute-start(bf16[128,2048]{1,0:T(8,128)(2,1)} %get-tuple-element.46.refs_0_), channel_id=1, source_target_pairs={{0,2},{1,3},{2,0},{3,1},{4,6},{5,7},{6,4},{7,5},{8,10},{9,11},{10,... | collective-permute-start | bytes 1572872 | tf_op jit(solution)/shard_map/ppermute | solution.py:259
  9.7 0.0 copy-start.6
  9.7 0.0 copy-start.7
  9.7 5.9 %all-to-all-start = ((bf16[8,192,128]{2,1,0:T(8,128)(2,1)}), bf16[8,192,128]{2,1,0:T(8,128)(2,1)S(1)}, u32[]{:S(2)}, u32[]{:S(2)}) async-start(bf16[8,192,128]{2,1,0:T(8,128)(2,1)} %bitcast.22), calls=%async_computation | async-start | bytes 786432 | tf_op jit(solution)/shard_map/all_to_all | solution.py:291
  15.7 2.1 %collective-permute-start.4 = (bf16[3,4,32,128]{3,2,1,0:T(8,128)(2,1)S(1)}, bf16[3,4,32,128]{3,2,1,0:T(8,128)(2,1)S(1)}, u32[]{:S(2)}, u32[]{:S(2)}) collective-permute-start(bf16[3,4,32,128]{3,2,1,0:T(8,128)(2,1)S(1)} %shard_map.65.refs_1_), channel_id=1, source_target_pairs={{0,4},{4,0},{8,12},{12,8},{16,20},{20,16},{24,28},{28,24},{1,5},{5... | collective-permute-start | bytes 294920 | tf_op jit(solution)/shard_map/ppermute | solution.py:259
  17.8 0.1 collective-permute-start.3
  17.9 3.7 %shard_map.66 = (bf16[512,128]{1,0:T(8,128)(2,1)S(1)}, f32[2,512,128]{2,1,0:T(8,128)S(1)}, f32[2,512,128]{2,1,0:T(8,128)S(1)}, bf16[512,256]{1,0:T(8,128)(2,1)S(...) custom-call(bf16[512,512]{1,0:T(8,128)(2,1)S(1)} %copy-done, bf16[512,512]{1,0:T(8,128)(2,1)S(1)} %copy-done.1, ...), custom_call_target="tpu_custom_call" | custom-call | flops 1 | bytes 1 | tf_op jit(solution)/shard_map/pallas_call | solution.py:28
  21.6 1.5 %collective-permute-done.3.refs_2_ = bf16[1,4,32,128]{3,2,1,0:T(8,128)(2,1)S(1)} collective-permute-done((bf16[1,4,32,128]{3,2,1,0:T(8,128)(2,1)S(1)}, bf16[1,4,32,128]{3,2,1,0:T(8,128)(2,1)S(1)}, u32[]{:S(2)}, u32[]{:S(2)}) %collective-permute-start.3) | collective-permute-done | bytes 32800 | tf_op jit(solution)/shard_map/ppermute | solution.py:259
  23.1 1.3 %shard_map.68 = (bf16[128,2048]{1,0:T(8,128)(2,1)S(1)}, bf16[128,2048]{1,0:T(8,128)(2,1)S(1)}) custom-call(bf16[512,128]{1,0:T(8,128)(2,1)S(1)} %get-tuple-element.32.row_ref, f32[2,512,128]{2,1,0:T(8,128)S(1)} %get-tuple-element.33.sum_ref, f32[2,512,128]{2,1,0:T(8,128)S(1)} %get-tuple-element.34.stat_ref, bf16[512,256]{1,0:T(8,128)(2,1)S(1)} %get-tuple-element.35.q_ref, ...), custom_call_target="tpu_custom_call" | custom-call | flops 1 | bytes 1 | tf_op jit(solution)/shard_map/pallas_call | solution.py:28
  24.4 0.1 collective-permute-start.6
  24.5 0.5 %collective-permute-start.10 = (bf16[128,2048]{1,0:T(8,128)(2,1)S(1)}, bf16[128,2048]{1,0:T(8,128)(2,1)S(1)}, u32[]{:S(2)}, u32[]{:S(2)}) collective-permute-start(bf16[128,2048]{1,0:T(8,128)(2,1)S(1)} %collective-permute-done.9.refs_2_), channel_id=1, source_target_pairs={{0,1},{1,0},{2,3},{3,2},{4,5},{5,4},{6,7},{7,6},{8,9},{9,8},{10,11... | collective-permute-start | bytes 1572872 | tf_op jit(solution)/shard_map/ppermute | solution.py:259
  25.0 0.1 collective-permute-start.8
  25.1 1.8 %shard_map.67 = (bf16[128,2048]{1,0:T(8,128)(2,1)}, bf16[128,2048]{1,0:T(8,128)(2,1)S(1)}) custom-call(bf16[512,128]{1,0:T(8,128)(2,1)S(1)} %get-tuple-element.32.row_ref, f32[2,512,128]{2,1,0:T(8,128)S(1)} %get-tuple-element.33.sum_ref, f32[2,512,128]{2,1,0:T(8,128)S(1)} %get-tuple-element.34.stat_ref, bf16[512,256]{1,0:T(8,128)(2,1)S(1)} %get-tuple-element.35.q_ref, ...), custom_call_target="tpu_custom_call" | custom-call | flops 1 | bytes 1 | tf_op jit(solution)/shard_map/pallas_call | solution.py:28
  26.9 0.5 %collective-permute-start.5 = (bf16[128,2048]{1,0:T(8,128)(2,1)}, bf16[128,2048]{1,0:T(8,128)(2,1)S(1)}, u32[]{:S(2)}, u32[]{:S(2)}) collective-permute-start(bf16[128,2048]{1,0:T(8,128)(2,1)} %get-tuple-element.41), channel_id=1, source_target_pairs={{0,1},{1,0},{2,3},{3,2},{4,5},{5,4},{6,7},{7,6},{8,9},{9,8},{10,11... | collective-permute-start | bytes 1572872 | tf_op jit(solution)/shard_map/ppermute | solution.py:259
  27.4 0.9 %shard_map.69 = bf16[128,2048]{1,0:T(8,128)(2,1)} custom-call(bf16[128,2048]{1,0:T(8,128)(2,1)S(1)} %get-tuple-element.42.a_ref, bf16[128,2048]{1,0:T(8,128)(2,1)S(1)} %collective-permute-done.6.b_ref), custom_call_target="tpu_custom_call" | custom-call | flops 1 | bytes 1 | tf_op jit(solution)/shard_map/pallas_call | solution.py:28
  28.2 0.6 %collective-permute-start.7 = (bf16[128,2048]{1,0:T(8,128)(2,1)}, bf16[128,2048]{1,0:T(8,128)(2,1)}, u32[]{:S(2)}, u32[]{:S(2)}) collective-permute-start(bf16[128,2048]{1,0:T(8,128)(2,1)} %shard_map.69), channel_id=1, source_target_pairs={{0,2},{1,3},{2,0},{3,1},{4,6},{5,7},{6,4},{7,5},{8,10},{9,11},{10,... | collective-permute-start | bytes 1572872 | tf_op jit(solution)/shard_map/ppermute | solution.py:259
  28.8 0.9 %shard_map.70 = bf16[8,64,128]{2,1,0:T(8,128)(2,1)S(1)} custom-call(bf16[8,3,64,128]{3,2,1,0:T(8,128)(2,1)S(1)} %bitcast.13), custom_call_target="tpu_custom_call" | custom-call | flops 3000000000 | bytes 1 | tf_op jit(solution)/shard_map/pallas_call | solution.py:28
  29.8 0.6 %copy-done.5 = bf16[8,64,128]{2,1,0:T(8,128)(2,1)} copy-done((bf16[8,64,128]{2,1,0:T(8,128)(2,1)}, bf16[8,64,128]{2,1,0:T(8,128)(2,1)S(1)}, u32[]{:S(2)}) %copy-start.5) | copy-done | bytes 131096
  30.4 5.4 %all-to-all-start.1 = ((bf16[32,16,128]{2,1,0:T(8,128)(2,1)}), bf16[32,16,128]{2,1,0:T(8,128)(2,1)S(1)}, u32[]{:S(2)}, u32[]{:S(2)}) async-start(bf16[32,16,128]{2,1,0:T(8,128)(2,1)} %bitcast.20), calls=%async_computation.1 | async-start | bytes 262144 | tf_op jit(solution)/shard_map/all_to_all | solution.py:335
  35.9 8.2 %all-to-all-done.1 = bf16[32,16,128]{2,1,0:T(8,128)(2,1)S(1)} async-done(((bf16[32,16,128]{2,1,0:T(8,128)(2,1)}), bf16[32,16,128]{2,1,0:T(8,128)(2,1)S(1)}, u32[]{:S(2)}, u32[]{:S(2)}) %all-to-all-start.1) | async-done | bytes 131104 | tf_op jit(solution)/shard_map/all_to_all | solution.py:335
  44.0 2.1 %shard_map.72 = bf16[128,2048]{1,0:T(8,128)(2,1)} custom-call(bf16[128,2048]{1,0:T(8,128)(2,1)S(1)} %get-tuple-element.40.own_ref, bf16[128,2048]{1,0:T(8,128)(2,1)S(1)} %collective-permute-done.5.core_ref, bf16[128,2048]{1,0:T(8,128)(2,1)} %collective-permute-done.7.far_ref, bf16[8,4,16,128]{3,2,1,0:T(8,128)(2,1)S(1)} %bitcast.12, ...), custom_call_target="tpu_custom_call" | custom-call | flops 1 | bytes 1 | tf_op jit(solution)/shard_map/pallas_call | solution.py:28
  (27 shorter events, 0.1 us)
Async XLA Ops:
  2.2 13.4 %collective-permute-start = (bf16[1,4,32,128]{3,2,1,0:T(8,128)(2,1)}, bf16[1,4,32,128]{3,2,1,0:T(8,128)(2,1)S(1)}, u32[]{:S(2)}, u32[]{:S(2)}) collective-permute-start(bf16[1,4,32,128]{3,2,1,0:T(8,128)(2,1)} %bitcast.14), channel_id=1, source_target_pairs={{0,8},{4,12},{8,0},{12,4},{16,24},{20,28},{24,16},{28,20},{1,9},{5... | collective-permute-start | bytes 98312 | tf_op jit(solution)/shard_map/ppermute | solution.py:259
  5.3 10.3 %collective-permute-start.1 = (bf16[1,4,32,128]{3,2,1,0:T(8,128)(2,1)}, bf16[1,4,32,128]{3,2,1,0:T(8,128)(2,1)S(1)}, u32[]{:S(2)}, u32[]{:S(2)}) collective-permute-start(bf16[1,4,32,128]{3,2,1,0:T(8,128)(2,1)} %bitcast.15), channel_id=1, source_target_pairs={{0,16},{4,20},{8,24},{12,28},{16,0},{20,4},{24,8},{28,12},{1,17},{... | collective-permute-start | bytes 98312 | tf_op jit(solution)/shard_map/ppermute | solution.py:259
  7.9 7.7 %collective-permute-start.2 = (bf16[1,4,32,128]{3,2,1,0:T(8,128)(2,1)}, bf16[1,4,32,128]{3,2,1,0:T(8,128)(2,1)S(1)}, u32[]{:S(2)}, u32[]{:S(2)}) collective-permute-start(bf16[1,4,32,128]{3,2,1,0:T(8,128)(2,1)} %bitcast.16), channel_id=1, source_target_pairs={{0,24},{4,28},{8,16},{12,20},{16,8},{20,12},{24,0},{28,4},{1,25},{... | collective-permute-start | bytes 98312 | tf_op jit(solution)/shard_map/ppermute | solution.py:259
  7.9 16.6 %collective-permute-start.9 = (bf16[128,2048]{1,0:T(8,128)(2,1)}, bf16[128,2048]{1,0:T(8,128)(2,1)S(1)}, u32[]{:S(2)}, u32[]{:S(2)}) collective-permute-start(bf16[128,2048]{1,0:T(8,128)(2,1)} %get-tuple-element.46.refs_0_), channel_id=1, source_target_pairs={{0,2},{1,3},{2,0},{3,1},{4,6},{5,7},{6,4},{7,5},{8,10},{9,11},{10,... | collective-permute-start | bytes 1572872 | tf_op jit(solution)/shard_map/ppermute | solution.py:259
  9.6 8.1 %copy-start.4 = (bf16[4,2,16,128]{3,2,1,0:T(8,128)(2,1)S(1)}, bf16[4,2,16,128]{3,2,1,0:T(8,128)(2,1)}, u32[]{:S(2)}) copy-start(bf16[4,2,16,128]{3,2,1,0:T(8,128)(2,1)} %get-tuple-element.26) | copy-start | bytes 98308
  9.7 8.2 %copy-start = (bf16[512,512]{1,0:T(8,128)(2,1)S(1)}, bf16[512,512]{1,0:T(8,128)(2,1)}, u32[]{:S(2)}) copy-start(bf16[512,512]{1,0:T(8,128)(2,1)} %q_ref) | copy-start | bytes 1572868
  9.7 8.2 %copy-start.1 = (bf16[512,512]{1,0:T(8,128)(2,1)S(1)}, bf16[512,512]{1,0:T(8,128)(2,1)}, u32[]{:S(2)}) copy-start(bf16[512,512]{1,0:T(8,128)(2,1)} %k_ref) | copy-start | bytes 1572868
  9.7 8.2 %copy-start.2 = (bf16[512,512]{1,0:T(8,128)(2,1)S(1)}, bf16[512,512]{1,0:T(8,128)(2,1)}, u32[]{:S(2)}) copy-start(bf16[512,512]{1,0:T(8,128)(2,1)} %v_ref) | copy-start | bytes 1572868
  9.7 8.2 %copy-start.6 = (s32[1,2,16]{2,1,0:T(2,128)S(1)}, s32[1,2,16]{2,1,0:T(2,128)}, u32[]{:S(2)}) copy-start(s32[1,2,16]{2,1,0:T(2,128)} %param.9) | copy-start | bytes 388
  9.7 8.2 %copy-start.7 = (s32[1,256]{1,0:T(1,128)S(1)}, s32[1,256]{1,0:T(1,128)}, u32[]{:S(2)}) copy-start(s32[1,256]{1,0:T(1,128)} %constant.2.clone.slots_ref) | copy-start | bytes 3076
  9.7 19.1 %all-to-all-start = ((bf16[8,192,128]{2,1,0:T(8,128)(2,1)}), bf16[8,192,128]{2,1,0:T(8,128)(2,1)S(1)}, u32[]{:S(2)}, u32[]{:S(2)}) async-start(bf16[8,192,128]{2,1,0:T(8,128)(2,1)} %bitcast.22), calls=%async_computation | async-start | bytes 786432 | tf_op jit(solution)/shard_map/all_to_all | solution.py:291
  15.7 7.4 %collective-permute-start.4 = (bf16[3,4,32,128]{3,2,1,0:T(8,128)(2,1)S(1)}, bf16[3,4,32,128]{3,2,1,0:T(8,128)(2,1)S(1)}, u32[]{:S(2)}, u32[]{:S(2)}) collective-permute-start(bf16[3,4,32,128]{3,2,1,0:T(8,128)(2,1)S(1)} %shard_map.65.refs_1_), channel_id=1, source_target_pairs={{0,4},{4,0},{8,12},{12,8},{16,20},{20,16},{24,28},{28,24},{1,5},{5... | collective-permute-start | bytes 294920 | tf_op jit(solution)/shard_map/ppermute | solution.py:259
  17.8 5.3 %collective-permute-start.3 = (bf16[1,4,32,128]{3,2,1,0:T(8,128)(2,1)S(1)}, bf16[1,4,32,128]{3,2,1,0:T(8,128)(2,1)S(1)}, u32[]{:S(2)}, u32[]{:S(2)}) collective-permute-start(bf16[1,4,32,128]{3,2,1,0:T(8,128)(2,1)S(1)} %bitcast.17), channel_id=1, source_target_pairs={{0,4},{4,0},{8,12},{12,8},{16,20},{20,16},{24,28},{28,24},{1,5},{5... | collective-permute-start | bytes 98312 | tf_op jit(solution)/shard_map/ppermute | solution.py:259
  21.6 3.4 %copy-start.3 = (bf16[128,2048]{1,0:T(8,128)(2,1)S(1)}, bf16[128,2048]{1,0:T(8,128)(2,1)}, u32[]{:S(2)}) copy-start(bf16[128,2048]{1,0:T(8,128)(2,1)} %get-tuple-element.46.refs_0_) | copy-start | bytes 1572868
  24.4 3.0 %collective-permute-start.6 = (bf16[128,2048]{1,0:T(8,128)(2,1)S(1)}, bf16[128,2048]{1,0:T(8,128)(2,1)S(1)}, u32[]{:S(2)}, u32[]{:S(2)}) collective-permute-start(bf16[128,2048]{1,0:T(8,128)(2,1)S(1)} %get-tuple-element.43), channel_id=1, source_target_pairs={{0,1},{1,0},{2,3},{3,2},{4,5},{5,4},{6,7},{7,6},{8,9},{9,8},{10,11... | collective-permute-start | bytes 1572872 | tf_op jit(solution)/shard_map/ppermute | solution.py:259
  24.5 11.3 %collective-permute-start.10 = (bf16[128,2048]{1,0:T(8,128)(2,1)S(1)}, bf16[128,2048]{1,0:T(8,128)(2,1)S(1)}, u32[]{:S(2)}, u32[]{:S(2)}) collective-permute-start(bf16[128,2048]{1,0:T(8,128)(2,1)S(1)} %collective-permute-done.9.refs_2_), channel_id=1, source_target_pairs={{0,1},{1,0},{2,3},{3,2},{4,5},{5,4},{6,7},{7,6},{8,9},{9,8},{10,11... | collective-permute-start | bytes 1572872 | tf_op jit(solution)/shard_map/ppermute | solution.py:259
  25.0 10.9 %collective-permute-start.8 = (bf16[128,2048]{1,0:T(8,128)(2,1)S(1)}, bf16[128,2048]{1,0:T(8,128)(2,1)S(1)}, u32[]{:S(2)}, u32[]{:S(2)}) collective-permute-start(bf16[128,2048]{1,0:T(8,128)(2,1)S(1)} %copy-done.3), channel_id=1, source_target_pairs={{0,1},{1,0},{2,3},{3,2},{4,5},{5,4},{6,7},{7,6},{8,9},{9,8},{10,11... | collective-permute-start | bytes 1572872 | tf_op jit(solution)/shard_map/ppermute | solution.py:259
  26.9 9.0 %collective-permute-start.5 = (bf16[128,2048]{1,0:T(8,128)(2,1)}, bf16[128,2048]{1,0:T(8,128)(2,1)S(1)}, u32[]{:S(2)}, u32[]{:S(2)}) collective-permute-start(bf16[128,2048]{1,0:T(8,128)(2,1)} %get-tuple-element.41), channel_id=1, source_target_pairs={{0,1},{1,0},{2,3},{3,2},{4,5},{5,4},{6,7},{7,6},{8,9},{9,8},{10,11... | collective-permute-start | bytes 1572872 | tf_op jit(solution)/shard_map/ppermute | solution.py:259
  28.2 15.8 %collective-permute-start.7 = (bf16[128,2048]{1,0:T(8,128)(2,1)}, bf16[128,2048]{1,0:T(8,128)(2,1)}, u32[]{:S(2)}, u32[]{:S(2)}) collective-permute-start(bf16[128,2048]{1,0:T(8,128)(2,1)} %shard_map.69), channel_id=1, source_target_pairs={{0,2},{1,3},{2,0},{3,1},{4,6},{5,7},{6,4},{7,5},{8,10},{9,11},{10,... | collective-permute-start | bytes 1572872 | tf_op jit(solution)/shard_map/ppermute | solution.py:259
  29.8 0.6 %copy-start.5 = (bf16[8,64,128]{2,1,0:T(8,128)(2,1)}, bf16[8,64,128]{2,1,0:T(8,128)(2,1)S(1)}, u32[]{:S(2)}) copy-start(bf16[8,64,128]{2,1,0:T(8,128)(2,1)S(1)} %shard_map.70) | copy-start | bytes 393220
  30.4 13.6 %all-to-all-start.1 = ((bf16[32,16,128]{2,1,0:T(8,128)(2,1)}), bf16[32,16,128]{2,1,0:T(8,128)(2,1)S(1)}, u32[]{:S(2)}, u32[]{:S(2)}) async-start(bf16[32,16,128]{2,1,0:T(8,128)(2,1)} %bitcast.20), calls=%async_computation.1 | async-start | bytes 262144 | tf_op jit(solution)/shard_map/all_to_all | solution.py:335

commit v6 on v5

--- a/solution.py
+++ b/solution.py
@@ -123,25 +123,28 @@
     return packed, tail.reshape(tail_shape), w_col
 
 
-def column_kernel(columns, moved_ref, out_ref, held, done, sems):
+def column_kernel(columns, moved_ref, out_ref, held, sems):
     outer, _, inner, depth = moved_ref.shape
     rows = outer * inner
     copies = start(sems, [(moved_ref.at[:, i], held.at[i]) for i in range(3)])
     wait(copies[:2])
     q, k, v = (held.at[i] for i in range(3))
     step = HEAD_DIM
-    results = []
-    for first in range(0, rows, step):
+    starts = range(0, rows, step)
+    at_k = lax.rem(lax.broadcasted_iota(jnp.int32, (1, rows), 1), columns)
+    scores = []
+    for first in starts:
         upto = first + step
         at_q = first + lax.broadcasted_iota(jnp.int32, (step, 1), 0)
-        at_k = lax.broadcasted_iota(jnp.int32, (1, upto), 1)
-        valid = (lax.rem(at_q, columns) == lax.rem(at_k, columns)) & (at_k <= at_q)
-        q_rows = q[...].reshape(rows, depth)[first:upto]
-        results.append((upto, *weigh(dot_t(q_rows, k[...].reshape(rows, depth)[:upto]), valid)))
+        valid = (lax.rem(at_q, columns) == at_k[:, :upto]) & (lax.broadcasted_iota(jnp.int32, (1, upto), 1) <= at_q)
+        scores.append(jnp.where(valid, dot_t(q[...].reshape(rows, depth)[first:upto], k[...].reshape(rows, depth)[:upto]), NEG))
+    peaks = [jnp.max(x, axis=1, keepdims=True) for x in scores]
+    weights = [jnp.exp2((x - y) * SCALE2).astype(BF16) for x, y in zip(scores, peaks)]
     wait(copies[2:])
-    out = [dot(weights, v[...].reshape(rows, depth)[:upto]) / denom for upto, weights, denom, _ in results]
-    done[...] = jnp.concatenate(out, axis=0).astype(BF16).reshape(outer, inner, depth)
-    wait(start(sems, [(done, out_ref)]))
+    values = jnp.concatenate([v[...].reshape(rows, depth), jnp.ones((rows, depth), BF16)], axis=1)
+    totals = [dot(x, values[: first + step]) for x, first in zip(weights, starts)]
+    out = [x[:, :depth] / x[:, depth:] for x in totals]
+    out_ref[...] = jnp.concatenate(out, axis=0).astype(BF16).reshape(outer, inner, depth)
 
 
 def own_kernel(relative, q_ref, k_ref, v_ref, w_ref, lists_ref, slots_ref, row_ref, sum_ref, stat_ref, q_fixed, w_all, mult_ref, q_all, k_all, v_all, sems):
@@ -320,9 +323,9 @@
     column_shape = (moved.shape[0], moved.shape[2], HEAD_DIM)
     (column_out,) = call(
         functools.partial(column_kernel, columns),
-        [(HBM, column_shape)],
+        [(VMEM, column_shape)],
         [(HBM, moved)],
-        [pltpu.VMEM((3, *column_shape), BF16), pltpu.VMEM(column_shape, BF16)],
+        [pltpu.VMEM((3, *column_shape), BF16)],
         3,
         COLUMN_COST,
     )

time: 46.5 us -> 46.2 us (level)
  transfers between devices with their start and end apart: 13 -> 13, of which waited for: 2 -> 2; matrix products, arithmetic and copies ran while one was open for 0% -> 0% of each run, Pallas kernels for 19% -> 18%
where the time goes in v6:
time: 46.2 us; the launch traced here: 45.9 us
  starting transfers between devices  22.6 us (49%)
  Pallas kernels  12.7 us (27%)
  waiting for transfers between devices  9.69 us (21%)
  local copies, waits for them, and re-layouts  0.66 us (1%)
    pallas_call x9, Pallas kernels, call(): pl.pallas_call(kernel, out_shape=[jax.ShapeDtypeStruct(x[1], x[2] if len(...  12.7 us
    ppermute x11, starting transfers between devices, swap(): return lax.ppermute(x, axis, [(i, i ^ flip) for i in range(count)])  11.3 us
    all_to_all x1, waiting for transfers between devices, per_device(): lax.all_to_all(column_out, ('seq', 'head'), split_axis=0, concat_axis=0,...  8.17 us
    all_to_all x1, starting transfers between devices, per_device(): lax.all_to_all(packed.reshape(count, 3 * columns, HEAD_DIM), 'seq', split...  5.95 us
    all_to_all x1, starting transfers between devices, per_device(): lax.all_to_all(column_out, ('seq', 'head'), split_axis=0, concat_axis=0,...  5.4 us
    ppermute x11, waiting for transfers between devices, swap(): return lax.ppermute(x, axis, [(i, i ^ flip) for i in range(count)])  1.52 us
  transfers between devices with their start and end apart: 13, of which 2 were waited for; matrix products, arithmetic and copies ran while one was open for 0% of the time, Pallas kernels for 18%

profile of v6, /device:TPU:0, one launch (start us, length us, event | category | flops | bytes accessed | tf_op | source)
XLA Modules:
  0.0 45.9 jit_solution(16010839903201450564)
XLA Ops:
  0.0 2.2 %shard_map.64 = (bf16[4,2,16,128]{3,2,1,0:T(8,128)(2,1)}, bf16[8,3,4,16,128]{4,3,2,1,0:T(8,128)(2,1)}, bf16[128,2048]{1,0:T(8,128)(2,1)}) custom-call(bf16[4,8,16,512]{3,2,1,0:T(8,128)(2,1)} %bitcast.9, bf16[4,8,16,512]{3,2,1,0:T(8,128)(2,1)} %bitcast.10, bf16[4,8,16,512]{3,2,1,0:T(8,128)(2,1)} %bitcast.11, bf16[512,2048]{1,0:T(8,128)(2,1)} %w_ref.2), custom_call_target="tpu_custom_call" | custom-call | flops 1 | bytes 1 | tf_op jit(solution)/shard_map/pallas_call | solution.py:28
  2.2 3.1 %collective-permute-start = (bf16[1,4,32,128]{3,2,1,0:T(8,128)(2,1)}, bf16[1,4,32,128]{3,2,1,0:T(8,128)(2,1)S(1)}, u32[]{:S(2)}, u32[]{:S(2)}) collective-permute-start(bf16[1,4,32,128]{3,2,1,0:T(8,128)(2,1)} %bitcast.14), channel_id=1, source_target_pairs={{0,8},{4,12},{8,0},{12,4},{16,24},{20,28},{24,16},{28,20},{1,9},{5... | collective-permute-start | bytes 98312 | tf_op jit(solution)/shard_map/ppermute | solution.py:262
  5.3 2.6 %collective-permute-start.1 = (bf16[1,4,32,128]{3,2,1,0:T(8,128)(2,1)}, bf16[1,4,32,128]{3,2,1,0:T(8,128)(2,1)S(1)}, u32[]{:S(2)}, u32[]{:S(2)}) collective-permute-start(bf16[1,4,32,128]{3,2,1,0:T(8,128)(2,1)} %bitcast.15), channel_id=1, source_target_pairs={{0,16},{4,20},{8,24},{12,28},{16,0},{20,4},{24,8},{28,12},{1,17},{... | collective-permute-start | bytes 98312 | tf_op jit(solution)/shard_map/ppermute | solution.py:262
  7.9 1.7 %collective-permute-start.9 = (bf16[128,2048]{1,0:T(8,128)(2,1)}, bf16[128,2048]{1,0:T(8,128)(2,1)S(1)}, u32[]{:S(2)}, u32[]{:S(2)}) collective-permute-start(bf16[128,2048]{1,0:T(8,128)(2,1)} %get-tuple-element.46.refs_0_), channel_id=1, source_target_pairs={{0,2},{1,3},{2,0},{3,1},{4,6},{5,7},{6,4},{7,5},{8,10},{9,11},{10,... | collective-permute-start | bytes 1572872 | tf_op jit(solution)/shard_map/ppermute | solution.py:262
  9.7 0.0 copy-start.6
  9.7 0.0 copy-start.7
  9.7 5.9 %all-to-all-start = ((bf16[8,192,128]{2,1,0:T(8,128)(2,1)}), bf16[8,192,128]{2,1,0:T(8,128)(2,1)S(1)}, u32[]{:S(2)}, u32[]{:S(2)}) async-start(bf16[8,192,128]{2,1,0:T(8,128)(2,1)} %bitcast.22), calls=%async_computation | async-start | bytes 786432 | tf_op jit(solution)/shard_map/all_to_all | solution.py:294
  15.7 2.1 %collective-permute-start.4 = (bf16[3,4,32,128]{3,2,1,0:T(8,128)(2,1)S(1)}, bf16[3,4,32,128]{3,2,1,0:T(8,128)(2,1)S(1)}, u32[]{:S(2)}, u32[]{:S(2)}) collective-permute-start(bf16[3,4,32,128]{3,2,1,0:T(8,128)(2,1)S(1)} %shard_map.65.refs_1_), channel_id=1, source_target_pairs={{0,4},{4,0},{8,12},{12,8},{16,20},{20,16},{24,28},{28,24},{1,5},{5... | collective-permute-start | bytes 294920 | tf_op jit(solution)/shard_map/ppermute | solution.py:262
  17.8 0.1 collective-permute-start.3
  17.9 3.7 %shard_map.66 = (bf16[512,128]{1,0:T(8,128)(2,1)S(1)}, f32[2,512,128]{2,1,0:T(8,128)S(1)}, f32[2,512,128]{2,1,0:T(8,128)S(1)}, bf16[512,256]{1,0:T(8,128)(2,1)S(...) custom-call(bf16[512,512]{1,0:T(8,128)(2,1)S(1)} %copy-done, bf16[512,512]{1,0:T(8,128)(2,1)S(1)} %copy-done.1, ...), custom_call_target="tpu_custom_call" | custom-call | flops 1 | bytes 1 | tf_op jit(solution)/shard_map/pallas_call | solution.py:28
  21.6 1.5 %collective-permute-done.3.refs_2_ = bf16[1,4,32,128]{3,2,1,0:T(8,128)(2,1)S(1)} collective-permute-done((bf16[1,4,32,128]{3,2,1,0:T(8,128)(2,1)S(1)}, bf16[1,4,32,128]{3,2,1,0:T(8,128)(2,1)S(1)}, u32[]{:S(2)}, u32[]{:S(2)}) %collective-permute-start.3) | collective-permute-done | bytes 32800 | tf_op jit(solution)/shard_map/ppermute | solution.py:262
  23.1 1.3 %shard_map.68 = (bf16[128,2048]{1,0:T(8,128)(2,1)S(1)}, bf16[128,2048]{1,0:T(8,128)(2,1)S(1)}) custom-call(bf16[512,128]{1,0:T(8,128)(2,1)S(1)} %get-tuple-element.32.row_ref, f32[2,512,128]{2,1,0:T(8,128)S(1)} %get-tuple-element.33.sum_ref, f32[2,512,128]{2,1,0:T(8,128)S(1)} %get-tuple-element.34.stat_ref, bf16[512,256]{1,0:T(8,128)(2,1)S(1)} %get-tuple-element.35.q_ref, ...), custom_call_target="tpu_custom_call" | custom-call | flops 1 | bytes 1 | tf_op jit(solution)/shard_map/pallas_call | solution.py:28
  24.4 0.1 collective-permute-start.6
  24.5 0.5 %collective-permute-start.10 = (bf16[128,2048]{1,0:T(8,128)(2,1)S(1)}, bf16[128,2048]{1,0:T(8,128)(2,1)S(1)}, u32[]{:S(2)}, u32[]{:S(2)}) collective-permute-start(bf16[128,2048]{1,0:T(8,128)(2,1)S(1)} %collective-permute-done.9.refs_2_), channel_id=1, source_target_pairs={{0,1},{1,0},{2,3},{3,2},{4,5},{5,4},{6,7},{7,6},{8,9},{9,8},{10,11... | collective-permute-start | bytes 1572872 | tf_op jit(solution)/shard_map/ppermute | solution.py:262
  25.0 0.1 collective-permute-start.8
  25.1 1.8 %shard_map.67 = (bf16[128,2048]{1,0:T(8,128)(2,1)}, bf16[128,2048]{1,0:T(8,128)(2,1)S(1)}) custom-call(bf16[512,128]{1,0:T(8,128)(2,1)S(1)} %get-tuple-element.32.row_ref, f32[2,512,128]{2,1,0:T(8,128)S(1)} %get-tuple-element.33.sum_ref, f32[2,512,128]{2,1,0:T(8,128)S(1)} %get-tuple-element.34.stat_ref, bf16[512,256]{1,0:T(8,128)(2,1)S(1)} %get-tuple-element.35.q_ref, ...), custom_call_target="tpu_custom_call" | custom-call | flops 1 | bytes 1 | tf_op jit(solution)/shard_map/pallas_call | solution.py:28
  26.9 0.5 %collective-permute-start.5 = (bf16[128,2048]{1,0:T(8,128)(2,1)}, bf16[128,2048]{1,0:T(8,128)(2,1)S(1)}, u32[]{:S(2)}, u32[]{:S(2)}) collective-permute-start(bf16[128,2048]{1,0:T(8,128)(2,1)} %get-tuple-element.41), channel_id=1, source_target_pairs={{0,1},{1,0},{2,3},{3,2},{4,5},{5,4},{6,7},{7,6},{8,9},{9,8},{10,11... | collective-permute-start | bytes 1572872 | tf_op jit(solution)/shard_map/ppermute | solution.py:262
  27.4 0.9 %shard_map.69 = bf16[128,2048]{1,0:T(8,128)(2,1)} custom-call(bf16[128,2048]{1,0:T(8,128)(2,1)S(1)} %get-tuple-element.42.a_ref, bf16[128,2048]{1,0:T(8,128)(2,1)S(1)} %collective-permute-done.6.b_ref), custom_call_target="tpu_custom_call" | custom-call | flops 1 | bytes 1 | tf_op jit(solution)/shard_map/pallas_call | solution.py:28
  28.2 0.6 %collective-permute-start.7 = (bf16[128,2048]{1,0:T(8,128)(2,1)}, bf16[128,2048]{1,0:T(8,128)(2,1)}, u32[]{:S(2)}, u32[]{:S(2)}) collective-permute-start(bf16[128,2048]{1,0:T(8,128)(2,1)} %shard_map.69), channel_id=1, source_target_pairs={{0,2},{1,3},{2,0},{3,1},{4,6},{5,7},{6,4},{7,5},{8,10},{9,11},{10,... | collective-permute-start | bytes 1572872 | tf_op jit(solution)/shard_map/ppermute | solution.py:262
  28.8 0.7 %shard_map.70 = bf16[8,64,128]{2,1,0:T(8,128)(2,1)S(1)} custom-call(bf16[8,3,64,128]{3,2,1,0:T(8,128)(2,1)S(1)} %bitcast.13), custom_call_target="tpu_custom_call" | custom-call | flops 3000000000 | bytes 1 | tf_op jit(solution)/shard_map/pallas_call | solution.py:28
  29.6 0.6 %copy-done.5 = bf16[8,64,128]{2,1,0:T(8,128)(2,1)} copy-done((bf16[8,64,128]{2,1,0:T(8,128)(2,1)}, bf16[8,64,128]{2,1,0:T(8,128)(2,1)S(1)}, u32[]{:S(2)}) %copy-start.5) | copy-done | bytes 131096
  30.2 5.4 %all-to-all-start.1 = ((bf16[32,16,128]{2,1,0:T(8,128)(2,1)}), bf16[32,16,128]{2,1,0:T(8,128)(2,1)S(1)}, u32[]{:S(2)}, u32[]{:S(2)}) async-start(bf16[32,16,128]{2,1,0:T(8,128)(2,1)} %bitcast.20), calls=%async_computation.1 | async-start | bytes 262144 | tf_op jit(solution)/shard_map/all_to_all | solution.py:338
  35.6 8.2 %all-to-all-done.1 = bf16[32,16,128]{2,1,0:T(8,128)(2,1)S(1)} async-done(((bf16[32,16,128]{2,1,0:T(8,128)(2,1)}), bf16[32,16,128]{2,1,0:T(8,128)(2,1)S(1)}, u32[]{:S(2)}, u32[]{:S(2)}) %all-to-all-start.1) | async-done | bytes 131104 | tf_op jit(solution)/shard_map/all_to_all | solution.py:338
  43.8 2.1 %shard_map.72 = bf16[128,2048]{1,0:T(8,128)(2,1)} custom-call(bf16[128,2048]{1,0:T(8,128)(2,1)S(1)} %get-tuple-element.40.own_ref, bf16[128,2048]{1,0:T(8,128)(2,1)S(1)} %collective-permute-done.5.core_ref, bf16[128,2048]{1,0:T(8,128)(2,1)} %collective-permute-done.7.far_ref, bf16[8,4,16,128]{3,2,1,0:T(8,128)(2,1)S(1)} %bitcast.12, ...), custom_call_target="tpu_custom_call" | custom-call | flops 1 | bytes 1 | tf_op jit(solution)/shard_map/pallas_call | solution.py:28
  (27 shorter events, 0.1 us)
Async XLA Ops:
  2.2 13.4 %collective-permute-start = (bf16[1,4,32,128]{3,2,1,0:T(8,128)(2,1)}, bf16[1,4,32,128]{3,2,1,0:T(8,128)(2,1)S(1)}, u32[]{:S(2)}, u32[]{:S(2)}) collective-permute-start(bf16[1,4,32,128]{3,2,1,0:T(8,128)(2,1)} %bitcast.14), channel_id=1, source_target_pairs={{0,8},{4,12},{8,0},{12,4},{16,24},{20,28},{24,16},{28,20},{1,9},{5... | collective-permute-start | bytes 98312 | tf_op jit(solution)/shard_map/ppermute | solution.py:262
  5.3 10.3 %collective-permute-start.1 = (bf16[1,4,32,128]{3,2,1,0:T(8,128)(2,1)}, bf16[1,4,32,128]{3,2,1,0:T(8,128)(2,1)S(1)}, u32[]{:S(2)}, u32[]{:S(2)}) collective-permute-start(bf16[1,4,32,128]{3,2,1,0:T(8,128)(2,1)} %bitcast.15), channel_id=1, source_target_pairs={{0,16},{4,20},{8,24},{12,28},{16,0},{20,4},{24,8},{28,12},{1,17},{... | collective-permute-start | bytes 98312 | tf_op jit(solution)/shard_map/ppermute | solution.py:262
  7.9 7.7 %collective-permute-start.2 = (bf16[1,4,32,128]{3,2,1,0:T(8,128)(2,1)}, bf16[1,4,32,128]{3,2,1,0:T(8,128)(2,1)S(1)}, u32[]{:S(2)}, u32[]{:S(2)}) collective-permute-start(bf16[1,4,32,128]{3,2,1,0:T(8,128)(2,1)} %bitcast.16), channel_id=1, source_target_pairs={{0,24},{4,28},{8,16},{12,20},{16,8},{20,12},{24,0},{28,4},{1,25},{... | collective-permute-start | bytes 98312 | tf_op jit(solution)/shard_map/ppermute | solution.py:262
  7.9 16.6 %collective-permute-start.9 = (bf16[128,2048]{1,0:T(8,128)(2,1)}, bf16[128,2048]{1,0:T(8,128)(2,1)S(1)}, u32[]{:S(2)}, u32[]{:S(2)}) collective-permute-start(bf16[128,2048]{1,0:T(8,128)(2,1)} %get-tuple-element.46.refs_0_), channel_id=1, source_target_pairs={{0,2},{1,3},{2,0},{3,1},{4,6},{5,7},{6,4},{7,5},{8,10},{9,11},{10,... | collective-permute-start | bytes 1572872 | tf_op jit(solution)/shard_map/ppermute | solution.py:262
  9.6 8.1 %copy-start.4 = (bf16[4,2,16,128]{3,2,1,0:T(8,128)(2,1)S(1)}, bf16[4,2,16,128]{3,2,1,0:T(8,128)(2,1)}, u32[]{:S(2)}) copy-start(bf16[4,2,16,128]{3,2,1,0:T(8,128)(2,1)} %get-tuple-element.26) | copy-start | bytes 98308
  9.7 8.2 %copy-start = (bf16[512,512]{1,0:T(8,128)(2,1)S(1)}, bf16[512,512]{1,0:T(8,128)(2,1)}, u32[]{:S(2)}) copy-start(bf16[512,512]{1,0:T(8,128)(2,1)} %q_ref) | copy-start | bytes 1572868
  9.7 8.2 %copy-start.1 = (bf16[512,512]{1,0:T(8,128)(2,1)S(1)}, bf16[512,512]{1,0:T(8,128)(2,1)}, u32[]{:S(2)}) copy-start(bf16[512,512]{1,0:T(8,128)(2,1)} %k_ref) | copy-start | bytes 1572868
  9.7 8.2 %copy-start.2 = (bf16[512,512]{1,0:T(8,128)(2,1)S(1)}, bf16[512,512]{1,0:T(8,128)(2,1)}, u32[]{:S(2)}) copy-start(bf16[512,512]{1,0:T(8,128)(2,1)} %v_ref) | copy-start | bytes 1572868
  9.7 8.2 %copy-start.6 = (s32[1,2,16]{2,1,0:T(2,128)S(1)}, s32[1,2,16]{2,1,0:T(2,128)}, u32[]{:S(2)}) copy-start(s32[1,2,16]{2,1,0:T(2,128)} %param.9) | copy-start | bytes 388
  9.7 8.2 %copy-start.7 = (s32[1,256]{1,0:T(1,128)S(1)}, s32[1,256]{1,0:T(1,128)}, u32[]{:S(2)}) copy-start(s32[1,256]{1,0:T(1,128)} %constant.2.clone.slots_ref) | copy-start | bytes 3076
  9.7 19.1 %all-to-all-start = ((bf16[8,192,128]{2,1,0:T(8,128)(2,1)}), bf16[8,192,128]{2,1,0:T(8,128)(2,1)S(1)}, u32[]{:S(2)}, u32[]{:S(2)}) async-start(bf16[8,192,128]{2,1,0:T(8,128)(2,1)} %bitcast.22), calls=%async_computation | async-start | bytes 786432 | tf_op jit(solution)/shard_map/all_to_all | solution.py:294
  15.7 7.4 %collective-permute-start.4 = (bf16[3,4,32,128]{3,2,1,0:T(8,128)(2,1)S(1)}, bf16[3,4,32,128]{3,2,1,0:T(8,128)(2,1)S(1)}, u32[]{:S(2)}, u32[]{:S(2)}) collective-permute-start(bf16[3,4,32,128]{3,2,1,0:T(8,128)(2,1)S(1)} %shard_map.65.refs_1_), channel_id=1, source_target_pairs={{0,4},{4,0},{8,12},{12,8},{16,20},{20,16},{24,28},{28,24},{1,5},{5... | collective-permute-start | bytes 294920 | tf_op jit(solution)/shard_map/ppermute | solution.py:262
  17.8 5.3 %collective-permute-start.3 = (bf16[1,4,32,128]{3,2,1,0:T(8,128)(2,1)S(1)}, bf16[1,4,32,128]{3,2,1,0:T(8,128)(2,1)S(1)}, u32[]{:S(2)}, u32[]{:S(2)}) collective-permute-start(bf16[1,4,32,128]{3,2,1,0:T(8,128)(2,1)S(1)} %bitcast.17), channel_id=1, source_target_pairs={{0,4},{4,0},{8,12},{12,8},{16,20},{20,16},{24,28},{28,24},{1,5},{5... | collective-permute-start | bytes 98312 | tf_op jit(solution)/shard_map/ppermute | solution.py:262
  21.6 3.4 %copy-start.3 = (bf16[128,2048]{1,0:T(8,128)(2,1)S(1)}, bf16[128,2048]{1,0:T(8,128)(2,1)}, u32[]{:S(2)}) copy-start(bf16[128,2048]{1,0:T(8,128)(2,1)} %get-tuple-element.46.refs_0_) | copy-start | bytes 1572868
  24.4 3.0 %collective-permute-start.6 = (bf16[128,2048]{1,0:T(8,128)(2,1)S(1)}, bf16[128,2048]{1,0:T(8,128)(2,1)S(1)}, u32[]{:S(2)}, u32[]{:S(2)}) collective-permute-start(bf16[128,2048]{1,0:T(8,128)(2,1)S(1)} %get-tuple-element.43), channel_id=1, source_target_pairs={{0,1},{1,0},{2,3},{3,2},{4,5},{5,4},{6,7},{7,6},{8,9},{9,8},{10,11... | collective-permute-start | bytes 1572872 | tf_op jit(solution)/shard_map/ppermute | solution.py:262
  24.5 11.1 %collective-permute-start.10 = (bf16[128,2048]{1,0:T(8,128)(2,1)S(1)}, bf16[128,2048]{1,0:T(8,128)(2,1)S(1)}, u32[]{:S(2)}, u32[]{:S(2)}) collective-permute-start(bf16[128,2048]{1,0:T(8,128)(2,1)S(1)} %collective-permute-done.9.refs_2_), channel_id=1, source_target_pairs={{0,1},{1,0},{2,3},{3,2},{4,5},{5,4},{6,7},{7,6},{8,9},{9,8},{10,11... | collective-permute-start | bytes 1572872 | tf_op jit(solution)/shard_map/ppermute | solution.py:262
  25.0 10.7 %collective-permute-start.8 = (bf16[128,2048]{1,0:T(8,128)(2,1)S(1)}, bf16[128,2048]{1,0:T(8,128)(2,1)S(1)}, u32[]{:S(2)}, u32[]{:S(2)}) collective-permute-start(bf16[128,2048]{1,0:T(8,128)(2,1)S(1)} %copy-done.3), channel_id=1, source_target_pairs={{0,1},{1,0},{2,3},{3,2},{4,5},{5,4},{6,7},{7,6},{8,9},{9,8},{10,11... | collective-permute-start | bytes 1572872 | tf_op jit(solution)/shard_map/ppermute | solution.py:262
  26.9 8.8 %collective-permute-start.5 = (bf16[128,2048]{1,0:T(8,128)(2,1)}, bf16[128,2048]{1,0:T(8,128)(2,1)S(1)}, u32[]{:S(2)}, u32[]{:S(2)}) collective-permute-start(bf16[128,2048]{1,0:T(8,128)(2,1)} %get-tuple-element.41), channel_id=1, source_target_pairs={{0,1},{1,0},{2,3},{3,2},{4,5},{5,4},{6,7},{7,6},{8,9},{9,8},{10,11... | collective-permute-start | bytes 1572872 | tf_op jit(solution)/shard_map/ppermute | solution.py:262
  28.2 15.6 %collective-permute-start.7 = (bf16[128,2048]{1,0:T(8,128)(2,1)}, bf16[128,2048]{1,0:T(8,128)(2,1)}, u32[]{:S(2)}, u32[]{:S(2)}) collective-permute-start(bf16[128,2048]{1,0:T(8,128)(2,1)} %shard_map.69), channel_id=1, source_target_pairs={{0,2},{1,3},{2,0},{3,1},{4,6},{5,7},{6,4},{7,5},{8,10},{9,11},{10,... | collective-permute-start | bytes 1572872 | tf_op jit(solution)/shard_map/ppermute | solution.py:262
  29.5 0.6 %copy-start.5 = (bf16[8,64,128]{2,1,0:T(8,128)(2,1)}, bf16[8,64,128]{2,1,0:T(8,128)(2,1)S(1)}, u32[]{:S(2)}) copy-start(bf16[8,64,128]{2,1,0:T(8,128)(2,1)S(1)} %shard_map.70) | copy-start | bytes 393220
  30.2 13.6 %all-to-all-start.1 = ((bf16[32,16,128]{2,1,0:T(8,128)(2,1)}), bf16[32,16,128]{2,1,0:T(8,128)(2,1)S(1)}, u32[]{:S(2)}, u32[]{:S(2)}) async-start(bf16[32,16,128]{2,1,0:T(8,128)(2,1)} %bitcast.20), calls=%async_computation.1 | async-start | bytes 262144 | tf_op jit(solution)/shard_map/all_to_all | solution.py:338

commit v7 on v6

--- a/solution.py
+++ b/solution.py
@@ -239,7 +239,7 @@
     pieces = (sems.shape[0] - 1) // 2
     cut = done.shape[1] // pieces
     cols = [pl.ds(i * cut, cut) for i in range(pieces)]
-    first, *copies = start(sems, [(moved_ref, moved)] + [(far_ref.at[:, c], far.at[:, c]) for c in cols])
+    *copies, first = start(sems, [(far_ref.at[:, c], far.at[:, c]) for c in cols] + [(moved_ref, moved)])
     outer, heads, inner, depth = moved.shape
     me = lax.axis_index("head")
     wait([first])

time: 46.2 us -> 46.1 us (level)
  no operation moved by 1% of the time
where the time goes in v7:
time: 46.1 us; the launch traced here: 45.8 us
  starting transfers between devices  22.6 us (49%)
  Pallas kernels  12.6 us (27%)
  waiting for transfers between devices  9.69 us (21%)
  local copies, waits for them, and re-layouts  0.66 us (1%)
    pallas_call x9, Pallas kernels, call(): pl.pallas_call(kernel, out_shape=[jax.ShapeDtypeStruct(x[1], x[2] if len(...  12.6 us
    ppermute x11, starting transfers between devices, swap(): return lax.ppermute(x, axis, [(i, i ^ flip) for i in range(count)])  11.3 us
    all_to_all x1, waiting for transfers between devices, per_device(): lax.all_to_all(column_out, ('seq', 'head'), split_axis=0, concat_axis=0,...  8.17 us
    all_to_all x1, starting transfers between devices, per_device(): lax.all_to_all(packed.reshape(count, 3 * columns, HEAD_DIM), 'seq', split...  5.95 us
    all_to_all x1, starting transfers between devices, per_device(): lax.all_to_all(column_out, ('seq', 'head'), split_axis=0, concat_axis=0,...  5.4 us
    ppermute x11, waiting for transfers between devices, swap(): return lax.ppermute(x, axis, [(i, i ^ flip) for i in range(count)])  1.52 us
  transfers between devices with their start and end apart: 13, of which 2 were waited for; matrix products, arithmetic and copies ran while one was open for 0% of the time, Pallas kernels for 18%

profile of v7, /device:TPU:0, one launch (start us, length us, event | category | flops | bytes accessed | tf_op | source)
XLA Modules:
  0.0 45.8 jit_solution(15570799276663826584)
XLA Ops:
  0.0 2.2 %shard_map.64 = (bf16[4,2,16,128]{3,2,1,0:T(8,128)(2,1)}, bf16[8,3,4,16,128]{4,3,2,1,0:T(8,128)(2,1)}, bf16[128,2048]{1,0:T(8,128)(2,1)}) custom-call(bf16[4,8,16,512]{3,2,1,0:T(8,128)(2,1)} %bitcast.9, bf16[4,8,16,512]{3,2,1,0:T(8,128)(2,1)} %bitcast.10, bf16[4,8,16,512]{3,2,1,0:T(8,128)(2,1)} %bitcast.11, bf16[512,2048]{1,0:T(8,128)(2,1)} %w_ref.2), custom_call_target="tpu_custom_call" | custom-call | flops 1 | bytes 1 | tf_op jit(solution)/shard_map/pallas_call | solution.py:28
  2.2 3.1 %collective-permute-start = (bf16[1,4,32,128]{3,2,1,0:T(8,128)(2,1)}, bf16[1,4,32,128]{3,2,1,0:T(8,128)(2,1)S(1)}, u32[]{:S(2)}, u32[]{:S(2)}) collective-permute-start(bf16[1,4,32,128]{3,2,1,0:T(8,128)(2,1)} %bitcast.14), channel_id=1, source_target_pairs={{0,8},{4,12},{8,0},{12,4},{16,24},{20,28},{24,16},{28,20},{1,9},{5... | collective-permute-start | bytes 98312 | tf_op jit(solution)/shard_map/ppermute | solution.py:262
  5.3 2.6 %collective-permute-start.1 = (bf16[1,4,32,128]{3,2,1,0:T(8,128)(2,1)}, bf16[1,4,32,128]{3,2,1,0:T(8,128)(2,1)S(1)}, u32[]{:S(2)}, u32[]{:S(2)}) collective-permute-start(bf16[1,4,32,128]{3,2,1,0:T(8,128)(2,1)} %bitcast.15), channel_id=1, source_target_pairs={{0,16},{4,20},{8,24},{12,28},{16,0},{20,4},{24,8},{28,12},{1,17},{... | collective-permute-start | bytes 98312 | tf_op jit(solution)/shard_map/ppermute | solution.py:262
  7.9 1.7 %collective-permute-start.9 = (bf16[128,2048]{1,0:T(8,128)(2,1)}, bf16[128,2048]{1,0:T(8,128)(2,1)S(1)}, u32[]{:S(2)}, u32[]{:S(2)}) collective-permute-start(bf16[128,2048]{1,0:T(8,128)(2,1)} %get-tuple-element.46.refs_0_), channel_id=1, source_target_pairs={{0,2},{1,3},{2,0},{3,1},{4,6},{5,7},{6,4},{7,5},{8,10},{9,11},{10,... | collective-permute-start | bytes 1572872 | tf_op jit(solution)/shard_map/ppermute | solution.py:262
  9.7 0.0 copy-start.6
  9.7 0.0 copy-start.7
  9.7 5.9 %all-to-all-start = ((bf16[8,192,128]{2,1,0:T(8,128)(2,1)}), bf16[8,192,128]{2,1,0:T(8,128)(2,1)S(1)}, u32[]{:S(2)}, u32[]{:S(2)}) async-start(bf16[8,192,128]{2,1,0:T(8,128)(2,1)} %bitcast.22), calls=%async_computation | async-start | bytes 786432 | tf_op jit(solution)/shard_map/all_to_all | solution.py:294
  15.7 2.1 %collective-permute-start.4 = (bf16[3,4,32,128]{3,2,1,0:T(8,128)(2,1)S(1)}, bf16[3,4,32,128]{3,2,1,0:T(8,128)(2,1)S(1)}, u32[]{:S(2)}, u32[]{:S(2)}) collective-permute-start(bf16[3,4,32,128]{3,2,1,0:T(8,128)(2,1)S(1)} %shard_map.65.refs_1_), channel_id=1, source_target_pairs={{0,4},{4,0},{8,12},{12,8},{16,20},{20,16},{24,28},{28,24},{1,5},{5... | collective-permute-start | bytes 294920 | tf_op jit(solution)/shard_map/ppermute | solution.py:262
  17.8 0.1 collective-permute-start.3
  17.9 3.7 %shard_map.66 = (bf16[512,128]{1,0:T(8,128)(2,1)S(1)}, f32[2,512,128]{2,1,0:T(8,128)S(1)}, f32[2,512,128]{2,1,0:T(8,128)S(1)}, bf16[512,256]{1,0:T(8,128)(2,1)S(...) custom-call(bf16[512,512]{1,0:T(8,128)(2,1)S(1)} %copy-done, bf16[512,512]{1,0:T(8,128)(2,1)S(1)} %copy-done.1, ...), custom_call_target="tpu_custom_call" | custom-call | flops 1 | bytes 1 | tf_op jit(solution)/shard_map/pallas_call | solution.py:28
  21.6 1.5 %collective-permute-done.3.refs_2_ = bf16[1,4,32,128]{3,2,1,0:T(8,128)(2,1)S(1)} collective-permute-done((bf16[1,4,32,128]{3,2,1,0:T(8,128)(2,1)S(1)}, bf16[1,4,32,128]{3,2,1,0:T(8,128)(2,1)S(1)}, u32[]{:S(2)}, u32[]{:S(2)}) %collective-permute-start.3) | collective-permute-done | bytes 32800 | tf_op jit(solution)/shard_map/ppermute | solution.py:262
  23.1 1.3 %shard_map.68 = (bf16[128,2048]{1,0:T(8,128)(2,1)S(1)}, bf16[128,2048]{1,0:T(8,128)(2,1)S(1)}) custom-call(bf16[512,128]{1,0:T(8,128)(2,1)S(1)} %get-tuple-element.32.row_ref, f32[2,512,128]{2,1,0:T(8,128)S(1)} %get-tuple-element.33.sum_ref, f32[2,512,128]{2,1,0:T(8,128)S(1)} %get-tuple-element.34.stat_ref, bf16[512,256]{1,0:T(8,128)(2,1)S(1)} %get-tuple-element.35.q_ref, ...), custom_call_target="tpu_custom_call" | custom-call | flops 1 | bytes 1 | tf_op jit(solution)/shard_map/pallas_call | solution.py:28
  24.4 0.1 collective-permute-start.6
  24.5 0.5 %collective-permute-start.10 = (bf16[128,2048]{1,0:T(8,128)(2,1)S(1)}, bf16[128,2048]{1,0:T(8,128)(2,1)S(1)}, u32[]{:S(2)}, u32[]{:S(2)}) collective-permute-start(bf16[128,2048]{1,0:T(8,128)(2,1)S(1)} %collective-permute-done.9.refs_2_), channel_id=1, source_target_pairs={{0,1},{1,0},{2,3},{3,2},{4,5},{5,4},{6,7},{7,6},{8,9},{9,8},{10,11... | collective-permute-start | bytes 1572872 | tf_op jit(solution)/shard_map/ppermute | solution.py:262
  25.0 0.1 collective-permute-start.8
  25.1 1.8 %shard_map.67 = (bf16[128,2048]{1,0:T(8,128)(2,1)}, bf16[128,2048]{1,0:T(8,128)(2,1)S(1)}) custom-call(bf16[512,128]{1,0:T(8,128)(2,1)S(1)} %get-tuple-element.32.row_ref, f32[2,512,128]{2,1,0:T(8,128)S(1)} %get-tuple-element.33.sum_ref, f32[2,512,128]{2,1,0:T(8,128)S(1)} %get-tuple-element.34.stat_ref, bf16[512,256]{1,0:T(8,128)(2,1)S(1)} %get-tuple-element.35.q_ref, ...), custom_call_target="tpu_custom_call" | custom-call | flops 1 | bytes 1 | tf_op jit(solution)/shard_map/pallas_call | solution.py:28
  26.9 0.5 %collective-permute-start.5 = (bf16[128,2048]{1,0:T(8,128)(2,1)}, bf16[128,2048]{1,0:T(8,128)(2,1)S(1)}, u32[]{:S(2)}, u32[]{:S(2)}) collective-permute-start(bf16[128,2048]{1,0:T(8,128)(2,1)} %get-tuple-element.41), channel_id=1, source_target_pairs={{0,1},{1,0},{2,3},{3,2},{4,5},{5,4},{6,7},{7,6},{8,9},{9,8},{10,11... | collective-permute-start | bytes 1572872 | tf_op jit(solution)/shard_map/ppermute | solution.py:262
  27.4 0.9 %shard_map.69 = bf16[128,2048]{1,0:T(8,128)(2,1)} custom-call(bf16[128,2048]{1,0:T(8,128)(2,1)S(1)} %get-tuple-element.42.a_ref, bf16[128,2048]{1,0:T(8,128)(2,1)S(1)} %collective-permute-done.6.b_ref), custom_call_target="tpu_custom_call" | custom-call | flops 1 | bytes 1 | tf_op jit(solution)/shard_map/pallas_call | solution.py:28
  28.2 0.6 %collective-permute-start.7 = (bf16[128,2048]{1,0:T(8,128)(2,1)}, bf16[128,2048]{1,0:T(8,128)(2,1)}, u32[]{:S(2)}, u32[]{:S(2)}) collective-permute-start(bf16[128,2048]{1,0:T(8,128)(2,1)} %shard_map.69), channel_id=1, source_target_pairs={{0,2},{1,3},{2,0},{3,1},{4,6},{5,7},{6,4},{7,5},{8,10},{9,11},{10,... | collective-permute-start | bytes 1572872 | tf_op jit(solution)/shard_map/ppermute | solution.py:262
  28.8 0.7 %shard_map.70 = bf16[8,64,128]{2,1,0:T(8,128)(2,1)S(1)} custom-call(bf16[8,3,64,128]{3,2,1,0:T(8,128)(2,1)S(1)} %bitcast.13), custom_call_target="tpu_custom_call" | custom-call | flops 3000000000 | bytes 1 | tf_op jit(solution)/shard_map/pallas_call | solution.py:28
  29.6 0.6 %copy-done.5 = bf16[8,64,128]{2,1,0:T(8,128)(2,1)} copy-done((bf16[8,64,128]{2,1,0:T(8,128)(2,1)}, bf16[8,64,128]{2,1,0:T(8,128)(2,1)S(1)}, u32[]{:S(2)}) %copy-start.5) | copy-done | bytes 131096
  30.2 5.4 %all-to-all-start.1 = ((bf16[32,16,128]{2,1,0:T(8,128)(2,1)}), bf16[32,16,128]{2,1,0:T(8,128)(2,1)S(1)}, u32[]{:S(2)}, u32[]{:S(2)}) async-start(bf16[32,16,128]{2,1,0:T(8,128)(2,1)} %bitcast.20), calls=%async_computation.1 | async-start | bytes 262144 | tf_op jit(solution)/shard_map/all_to_all | solution.py:338
  35.6 8.2 %all-to-all-done.1 = bf16[32,16,128]{2,1,0:T(8,128)(2,1)S(1)} async-done(((bf16[32,16,128]{2,1,0:T(8,128)(2,1)}), bf16[32,16,128]{2,1,0:T(8,128)(2,1)S(1)}, u32[]{:S(2)}, u32[]{:S(2)}) %all-to-all-start.1) | async-done | bytes 131104 | tf_op jit(solution)/shard_map/all_to_all | solution.py:338
  43.8 1.9 %shard_map.72 = bf16[128,2048]{1,0:T(8,128)(2,1)} custom-call(bf16[128,2048]{1,0:T(8,128)(2,1)S(1)} %get-tuple-element.40.own_ref, bf16[128,2048]{1,0:T(8,128)(2,1)S(1)} %collective-permute-done.5.core_ref, bf16[128,2048]{1,0:T(8,128)(2,1)} %collective-permute-done.7.far_ref, bf16[8,4,16,128]{3,2,1,0:T(8,128)(2,1)S(1)} %bitcast.12, ...), custom_call_target="tpu_custom_call" | custom-call | flops 1 | bytes 1 | tf_op jit(solution)/shard_map/pallas_call | solution.py:28
  (27 shorter events, 0.1 us)
Async XLA Ops:
  2.2 13.4 %collective-permute-start = (bf16[1,4,32,128]{3,2,1,0:T(8,128)(2,1)}, bf16[1,4,32,128]{3,2,1,0:T(8,128)(2,1)S(1)}, u32[]{:S(2)}, u32[]{:S(2)}) collective-permute-start(bf16[1,4,32,128]{3,2,1,0:T(8,128)(2,1)} %bitcast.14), channel_id=1, source_target_pairs={{0,8},{4,12},{8,0},{12,4},{16,24},{20,28},{24,16},{28,20},{1,9},{5... | collective-permute-start | bytes 98312 | tf_op jit(solution)/shard_map/ppermute | solution.py:262
  5.3 10.3 %collective-permute-start.1 = (bf16[1,4,32,128]{3,2,1,0:T(8,128)(2,1)}, bf16[1,4,32,128]{3,2,1,0:T(8,128)(2,1)S(1)}, u32[]{:S(2)}, u32[]{:S(2)}) collective-permute-start(bf16[1,4,32,128]{3,2,1,0:T(8,128)(2,1)} %bitcast.15), channel_id=1, source_target_pairs={{0,16},{4,20},{8,24},{12,28},{16,0},{20,4},{24,8},{28,12},{1,17},{... | collective-permute-start | bytes 98312 | tf_op jit(solution)/shard_map/ppermute | solution.py:262
  7.9 7.7 %collective-permute-start.2 = (bf16[1,4,32,128]{3,2,1,0:T(8,128)(2,1)}, bf16[1,4,32,128]{3,2,1,0:T(8,128)(2,1)S(1)}, u32[]{:S(2)}, u32[]{:S(2)}) collective-permute-start(bf16[1,4,32,128]{3,2,1,0:T(8,128)(2,1)} %bitcast.16), channel_id=1, source_target_pairs={{0,24},{4,28},{8,16},{12,20},{16,8},{20,12},{24,0},{28,4},{1,25},{... | collective-permute-start | bytes 98312 | tf_op jit(solution)/shard_map/ppermute | solution.py:262
  7.9 16.6 %collective-permute-start.9 = (bf16[128,2048]{1,0:T(8,128)(2,1)}, bf16[128,2048]{1,0:T(8,128)(2,1)S(1)}, u32[]{:S(2)}, u32[]{:S(2)}) collective-permute-start(bf16[128,2048]{1,0:T(8,128)(2,1)} %get-tuple-element.46.refs_0_), channel_id=1, source_target_pairs={{0,2},{1,3},{2,0},{3,1},{4,6},{5,7},{6,4},{7,5},{8,10},{9,11},{10,... | collective-permute-start | bytes 1572872 | tf_op jit(solution)/shard_map/ppermute | solution.py:262
  9.6 8.1 %copy-start.4 = (bf16[4,2,16,128]{3,2,1,0:T(8,128)(2,1)S(1)}, bf16[4,2,16,128]{3,2,1,0:T(8,128)(2,1)}, u32[]{:S(2)}) copy-start(bf16[4,2,16,128]{3,2,1,0:T(8,128)(2,1)} %get-tuple-element.26) | copy-start | bytes 98308
  9.7 8.2 %copy-start = (bf16[512,512]{1,0:T(8,128)(2,1)S(1)}, bf16[512,512]{1,0:T(8,128)(2,1)}, u32[]{:S(2)}) copy-start(bf16[512,512]{1,0:T(8,128)(2,1)} %q_ref) | copy-start | bytes 1572868
  9.7 8.2 %copy-start.1 = (bf16[512,512]{1,0:T(8,128)(2,1)S(1)}, bf16[512,512]{1,0:T(8,128)(2,1)}, u32[]{:S(2)}) copy-start(bf16[512,512]{1,0:T(8,128)(2,1)} %k_ref) | copy-start | bytes 1572868
  9.7 8.2 %copy-start.2 = (bf16[512,512]{1,0:T(8,128)(2,1)S(1)}, bf16[512,512]{1,0:T(8,128)(2,1)}, u32[]{:S(2)}) copy-start(bf16[512,512]{1,0:T(8,128)(2,1)} %v_ref) | copy-start | bytes 1572868
  9.7 8.2 %copy-start.6 = (s32[1,2,16]{2,1,0:T(2,128)S(1)}, s32[1,2,16]{2,1,0:T(2,128)}, u32[]{:S(2)}) copy-start(s32[1,2,16]{2,1,0:T(2,128)} %param.9) | copy-start | bytes 388
  9.7 8.2 %copy-start.7 = (s32[1,256]{1,0:T(1,128)S(1)}, s32[1,256]{1,0:T(1,128)}, u32[]{:S(2)}) copy-start(s32[1,256]{1,0:T(1,128)} %constant.2.clone.slots_ref) | copy-start | bytes 3076
  9.7 19.1 %all-to-all-start = ((bf16[8,192,128]{2,1,0:T(8,128)(2,1)}), bf16[8,192,128]{2,1,0:T(8,128)(2,1)S(1)}, u32[]{:S(2)}, u32[]{:S(2)}) async-start(bf16[8,192,128]{2,1,0:T(8,128)(2,1)} %bitcast.22), calls=%async_computation | async-start | bytes 786432 | tf_op jit(solution)/shard_map/all_to_all | solution.py:294
  15.7 7.4 %collective-permute-start.4 = (bf16[3,4,32,128]{3,2,1,0:T(8,128)(2,1)S(1)}, bf16[3,4,32,128]{3,2,1,0:T(8,128)(2,1)S(1)}, u32[]{:S(2)}, u32[]{:S(2)}) collective-permute-start(bf16[3,4,32,128]{3,2,1,0:T(8,128)(2,1)S(1)} %shard_map.65.refs_1_), channel_id=1, source_target_pairs={{0,4},{4,0},{8,12},{12,8},{16,20},{20,16},{24,28},{28,24},{1,5},{5... | collective-permute-start | bytes 294920 | tf_op jit(solution)/shard_map/ppermute | solution.py:262
  17.8 5.3 %collective-permute-start.3 = (bf16[1,4,32,128]{3,2,1,0:T(8,128)(2,1)S(1)}, bf16[1,4,32,128]{3,2,1,0:T(8,128)(2,1)S(1)}, u32[]{:S(2)}, u32[]{:S(2)}) collective-permute-start(bf16[1,4,32,128]{3,2,1,0:T(8,128)(2,1)S(1)} %bitcast.17), channel_id=1, source_target_pairs={{0,4},{4,0},{8,12},{12,8},{16,20},{20,16},{24,28},{28,24},{1,5},{5... | collective-permute-start | bytes 98312 | tf_op jit(solution)/shard_map/ppermute | solution.py:262
  21.6 3.4 %copy-start.3 = (bf16[128,2048]{1,0:T(8,128)(2,1)S(1)}, bf16[128,2048]{1,0:T(8,128)(2,1)}, u32[]{:S(2)}) copy-start(bf16[128,2048]{1,0:T(8,128)(2,1)} %get-tuple-element.46.refs_0_) | copy-start | bytes 1572868
  24.4 3.0 %collective-permute-start.6 = (bf16[128,2048]{1,0:T(8,128)(2,1)S(1)}, bf16[128,2048]{1,0:T(8,128)(2,1)S(1)}, u32[]{:S(2)}, u32[]{:S(2)}) collective-permute-start(bf16[128,2048]{1,0:T(8,128)(2,1)S(1)} %get-tuple-element.43), channel_id=1, source_target_pairs={{0,1},{1,0},{2,3},{3,2},{4,5},{5,4},{6,7},{7,6},{8,9},{9,8},{10,11... | collective-permute-start | bytes 1572872 | tf_op jit(solution)/shard_map/ppermute | solution.py:262
  24.5 11.1 %collective-permute-start.10 = (bf16[128,2048]{1,0:T(8,128)(2,1)S(1)}, bf16[128,2048]{1,0:T(8,128)(2,1)S(1)}, u32[]{:S(2)}, u32[]{:S(2)}) collective-permute-start(bf16[128,2048]{1,0:T(8,128)(2,1)S(1)} %collective-permute-done.9.refs_2_), channel_id=1, source_target_pairs={{0,1},{1,0},{2,3},{3,2},{4,5},{5,4},{6,7},{7,6},{8,9},{9,8},{10,11... | collective-permute-start | bytes 1572872 | tf_op jit(solution)/shard_map/ppermute | solution.py:262
  25.0 10.7 %collective-permute-start.8 = (bf16[128,2048]{1,0:T(8,128)(2,1)S(1)}, bf16[128,2048]{1,0:T(8,128)(2,1)S(1)}, u32[]{:S(2)}, u32[]{:S(2)}) collective-permute-start(bf16[128,2048]{1,0:T(8,128)(2,1)S(1)} %copy-done.3), channel_id=1, source_target_pairs={{0,1},{1,0},{2,3},{3,2},{4,5},{5,4},{6,7},{7,6},{8,9},{9,8},{10,11... | collective-permute-start | bytes 1572872 | tf_op jit(solution)/shard_map/ppermute | solution.py:262
  26.9 8.8 %collective-permute-start.5 = (bf16[128,2048]{1,0:T(8,128)(2,1)}, bf16[128,2048]{1,0:T(8,128)(2,1)S(1)}, u32[]{:S(2)}, u32[]{:S(2)}) collective-permute-start(bf16[128,2048]{1,0:T(8,128)(2,1)} %get-tuple-element.41), channel_id=1, source_target_pairs={{0,1},{1,0},{2,3},{3,2},{4,5},{5,4},{6,7},{7,6},{8,9},{9,8},{10,11... | collective-permute-start | bytes 1572872 | tf_op jit(solution)/shard_map/ppermute | solution.py:262
  28.2 15.6 %collective-permute-start.7 = (bf16[128,2048]{1,0:T(8,128)(2,1)}, bf16[128,2048]{1,0:T(8,128)(2,1)}, u32[]{:S(2)}, u32[]{:S(2)}) collective-permute-start(bf16[128,2048]{1,0:T(8,128)(2,1)} %shard_map.69), channel_id=1, source_target_pairs={{0,2},{1,3},{2,0},{3,1},{4,6},{5,7},{6,4},{7,5},{8,10},{9,11},{10,... | collective-permute-start | bytes 1572872 | tf_op jit(solution)/shard_map/ppermute | solution.py:262
  29.5 0.6 %copy-start.5 = (bf16[8,64,128]{2,1,0:T(8,128)(2,1)}, bf16[8,64,128]{2,1,0:T(8,128)(2,1)S(1)}, u32[]{:S(2)}) copy-start(bf16[8,64,128]{2,1,0:T(8,128)(2,1)S(1)} %shard_map.70) | copy-start | bytes 393220
  30.2 13.6 %all-to-all-start.1 = ((bf16[32,16,128]{2,1,0:T(8,128)(2,1)}), bf16[32,16,128]{2,1,0:T(8,128)(2,1)S(1)}, u32[]{:S(2)}, u32[]{:S(2)}) async-start(bf16[32,16,128]{2,1,0:T(8,128)(2,1)} %bitcast.20), calls=%async_computation.1 | async-start | bytes 262144 | tf_op jit(solution)/shard_map/all_to_all | solution.py:338
